TPU v7x, 32 devices: a whole 2x2x4 slice. The times are simulated.
32 devices in a mesh: tm: 4 (over y, core), asset: 8 (over z, x).
Axes of the slice: x: 2, y: 2, z: 4, core: 2. Of those that a mesh axis runs over, the one named last changes fastest.
Arguments:
- features: bfloat16 [8, 10240, 512], P('tm', 'asset'), may hold values from -6 to 6
- w_value: bfloat16 [512, 512], replicated, may hold values from -0.25 to 0.25
- w_gate: bfloat16 [512, 512], replicated, may hold values from -0.25 to 0.25
- cotangent: bfloat16 [8, 10240, 512], P('tm', 'asset'), may hold values from -6 to 6
- local_rows: int32 [160], P('asset'), may hold values from 0 to 9
- local_cols: int32 [160], P('asset'), may hold values from 0 to 9
- local_count: int32 [8], P('asset'), may hold values from 10 to 20, as said below
- local_tiles: bfloat16 [160, 128, 128], P('asset'), may hold values from -0.3125 to 0.3125
- remote_rows: int32 [64], P('asset'), may hold values from 0 to 9
- remote_cols: int32 [64], P('asset'), may hold values from 0 to 9
- remote_live: int32 [64], P('asset'), may hold values from 0 to 1, as said below
- remote_tiles: bfloat16 [64, 128, 128], P('asset'), may hold values from -0.3125 to 0.3125
Outputs:
- output: bfloat16 [8, 10240, 512], P('tm', 'asset')
- grad_features: bfloat16 [8, 10240, 512], P('tm', 'asset')
- grad_value: float32 [512, 512], replicated
- grad_gate: float32 [512, 512], replicated
Inputs may be any that keep to these rules, and one draw needn't show every extreme that they name: `local_count`: used local slots of each index of asset; some index uses all 20 in every draw. `remote_live`: at most one remote tile for each pair of indices of asset, never from an index to itself; in every draw some index holds a tile for every other index, and some index receives a tile from every other index.
All inputs are finite; a program needn't handle non-finite values.
Results may differ from a plain program's by a relative error of at most 0.0057.
Values may be sent and summed in bfloat16 or wider, within the bound.
No kernel may reach another device: no remote copies, remote signals or barrier semaphores. Data moves between devices by JAX's collectives and lax.ppermute only.
A program may use at most 128 MiB of HBM per device.

v0:
```python
import jax
import jax.numpy as jnp
from jax import lax
from jax.sharding import PartitionSpec as P


def one_hot_rows(indices, blocks):
    return (indices[None, :] == jnp.arange(blocks, dtype=jnp.int32)[:, None]).astype(jnp.bfloat16)


def per_device(
    features,
    w_value,
    w_gate,
    cotangent,
    local_rows,
    local_cols,
    local_count,
    local_tiles,
    remote_rows,
    remote_cols,
    remote_live,
    remote_tiles,
):
    steps, assets, width = features.shape
    tile = local_tiles.shape[1]
    blocks = assets // tile
    slots = local_tiles.shape[0]
    flat = features.reshape(-1, width)
    value = jnp.dot(flat, w_value, preferred_element_type=jnp.float32).astype(jnp.bfloat16)
    gate = jax.nn.sigmoid(jnp.dot(flat, w_gate, preferred_element_type=jnp.float32))
    value_blocks = value.reshape(steps, blocks, tile, width)
    live_local = (jnp.arange(slots, dtype=jnp.int32) < local_count[0]).astype(jnp.bfloat16)
    masked_remote = remote_tiles * remote_live.astype(jnp.bfloat16)[:, None, None]
    row_select = one_hot_rows(local_rows, blocks) * live_local[None, :]
    col_select = one_hot_rows(local_cols, blocks) * live_local[None, :]
    in_select = one_hot_rows(remote_rows, blocks)
    out_select = one_hot_rows(remote_cols, blocks)
    sent_blocks = jnp.take(value_blocks, remote_cols, axis=1)
    terms = jnp.einsum(
        "sij,tsjd->tsid", masked_remote, sent_blocks, preferred_element_type=jnp.float32
    ).astype(jnp.bfloat16)
    arrived = lax.all_to_all(terms, "asset", split_axis=1, concat_axis=1, tiled=True)
    picked = jnp.take(value_blocks, local_cols, axis=1)
    local_terms = jnp.einsum(
        "lij,tljd->tlid", local_tiles, picked, preferred_element_type=jnp.float32
    ).astype(jnp.bfloat16)
    agg_blocks = jnp.einsum(
        "bl,tlid->tbid", row_select, local_terms, preferred_element_type=jnp.float32
    )
    agg_blocks = agg_blocks + jnp.einsum(
        "bs,tsid->tbid", in_select, arrived, preferred_element_type=jnp.float32
    )
    agg = agg_blocks.reshape(-1, width)
    output = (flat.astype(jnp.float32) + gate * agg).astype(jnp.bfloat16)
    grad_out = cotangent.reshape(-1, width).astype(jnp.float32)
    dagg = (grad_out * gate).astype(jnp.bfloat16)
    dgate = (grad_out * agg * gate * (1.0 - gate)).astype(jnp.bfloat16)
    dagg_blocks = dagg.reshape(steps, blocks, tile, width)
    rows_needed = jnp.take(dagg_blocks, remote_rows, axis=1)
    returned = lax.all_to_all(rows_needed, "asset", split_axis=1, concat_axis=1, tiled=True)
    back = jnp.einsum(
        "sji,tsjd->tsid", masked_remote, returned, preferred_element_type=jnp.float32
    ).astype(jnp.bfloat16)
    taken = jnp.take(dagg_blocks, local_rows, axis=1)
    local_back = jnp.einsum(
        "lji,tljd->tlid", local_tiles, taken, preferred_element_type=jnp.float32
    ).astype(jnp.bfloat16)
    grad_blocks = jnp.einsum(
        "bl,tlid->tbid", col_select, local_back, preferred_element_type=jnp.float32
    )
    grad_blocks = grad_blocks + jnp.einsum(
        "bs,tsid->tbid", out_select, back, preferred_element_type=jnp.float32
    )
    dvalue = grad_blocks.reshape(-1, width).astype(jnp.bfloat16)
    grad_features = grad_out + jnp.dot(dvalue, w_value.T, preferred_element_type=jnp.float32)
    grad_features = grad_features + jnp.dot(dgate, w_gate.T, preferred_element_type=jnp.float32)
    partial_value = jnp.dot(flat.T, dvalue, preferred_element_type=jnp.float32)
    partial_gate = jnp.dot(flat.T, dgate, preferred_element_type=jnp.float32)
    total_value, total_gate = lax.psum((partial_value, partial_gate), ("tm", "asset"))
    scale = float(steps * assets * lax.axis_size("tm") * lax.axis_size("asset")) ** (-0.5)
    return (
        output.reshape(steps, assets, width),
        grad_features.astype(jnp.bfloat16).reshape(steps, assets, width),
        total_value * scale,
        total_gate * scale,
    )


def solution(mesh):
    return jax.shard_map(
        per_device,
        mesh=mesh,
        in_specs=(
            P("tm", "asset", None),
            P(),
            P(),
            P("tm", "asset", None),
            P("asset"),
            P("asset"),
            P("asset"),
            P("asset", None, None),
            P("asset"),
            P("asset"),
            P("asset"),
            P("asset", None, None),
        ),
        out_specs=(P("tm", "asset", None), P("tm", "asset", None), P(), P()),
        check_vma=False,
    )
```

profile of v0, /device:TPU:0, one launch (start us, length us, event | category | flops | bytes accessed | tf_op | source)
XLA Modules:
  0.0 313.7 jit_solution(16852440097444203016)
XLA Ops:
  9.2 3.4 %convolution_convert_fusion = bf16[2560,512]{1,0:T(8,128)(2,1)S(1)} fusion(bf16[2560,512]{1,0:T(8,128)(2,1)} %bitcast.111, bf16[512,512]{1,0:T(8,128)(2,1)} %param.17), kind=kOutput, calls=%fused_computation.29 | convolution fusion | flops 1343488000 | bytes 5767168 | tf_op jit(solution)/shard_map/dot_general | solution.py:30
  14.6 3.8 %convert_bitcast_fusion.3 = bf16[2,8,128,512]{2,3,0,1:T(8,128)(2,1)} fusion(bf16[8,2,128,512]{3,2,1,0:T(8,128)(2,1)} %gather_fusion.1, pred[8]{0:T(512)(128)(4,1)S(1)} %compare_and_fusion.2, bf16[8,128,128]{2,1,0:T(8,128)(2,1)S(1)} %copy-done.8, bf16[8]{0:T(256)(128)(2,1)S(1)} %convert_element_type.78), kind=kOutput, calls=%fused_computation.39 | convolution fusion | flops 270663680 | bytes 4456472 | tf_op jit(solution)/shard_map/sij,tsjd->tsid/dot_general | solution.py:40
  18.4 3.9 %copy.35 = bf16[2,8,128,512]{3,2,0,1:T(8,128)(2,1)} copy(bf16[2,8,128,512]{2,3,0,1:T(8,128)(2,1)} %convert_bitcast_fusion.3) | data formatting | bytes 4194304 | tf_op jit(solution)/shard_map/convert_element_type | solution.py:42
  22.3 7.4 %all-to-all-start = ((bf16[2,8,128,512]{3,2,0,1:T(8,128)(2,1)}), bf16[2,8,128,512]{3,2,0,1:T(8,128)(2,1)}, u32[]{:S(2)}, u32[]{:S(2)}) async-start(bf16[2,8,128,512]{3,2,0,1:T(8,128)(2,1)} %copy.35), calls=%async_computation | async-start | bytes 4194304 | tf_op jit(solution)/shard_map/all_to_all | solution.py:43
  29.7 4.1 %gather_fusion = bf16[20,2,128,512]{3,2,1,0:T(8,128)(2,1)} fusion(bf16[2,10,128,512]{3,2,1,0:T(8,128)(2,1)S(1)} %bitcast.106, s32[1024]{0:T(1024)S(1)} %pad_clamp_fusion.3), kind=kCustom, calls=%fused_computation.clone | custom fusion | bytes 10485840 | tf_op jit(solution)/shard_map/jit(_take)/gather | solution.py:44
  33.8 6.6 %convert_bitcast_fusion.1 = bf16[2,20,128,512]{2,3,0,1:T(8,128)(2,1)} fusion(bf16[20,2,128,512]{3,2,1,0:T(8,128)(2,1)} %gather_fusion, pred[20]{0:T(512)(128)(4,1)S(1)} %compare_and_fusion.3, bf16[20,128,128]{2,1,0:T(8,128)(2,1)S(1)} %copy-done), kind=kOutput, calls=%fused_computation.25 | convolution fusion | flops 676331520 | bytes 11141140 | tf_op jit(solution)/shard_map/lij,tljd->tlid/dot_general | solution.py:45
  40.4 8.6 %copy.33 = bf16[2,20,128,512]{3,1,2,0:T(8,128)(2,1)} copy(bf16[2,20,128,512]{2,3,0,1:T(8,128)(2,1)} %convert_bitcast_fusion.1) | data formatting | bytes 10485760 | tf_op jit(solution)/shard_map/convert_element_type | solution.py:47
  50.3 7.5 %fusion.45 = f32[2,128,512,10]{2,3,1,0:T(8,128)} fusion(bf16[2,20,128,512]{3,1,2,0:T(8,128)(2,1)} %copy.33, s32[20]{0:T(128)S(1)} %copy-done.10, bf16[20]{0:T(256)(128)(2,1)S(1)} %compare_convert_fusion), kind=kOutput, calls=%fused_computation.61 | convolution fusion | flops 52429200 | bytes 10485880 | tf_op jit(solution)/shard_map/bl,tlid->tbid/dot_general | solution.py:48
  57.8 20.3 %all-to-all-done = bf16[2,8,128,512]{3,2,0,1:T(8,128)(2,1)} async-done(((bf16[2,8,128,512]{3,2,0,1:T(8,128)(2,1)}), bf16[2,8,128,512]{3,2,0,1:T(8,128)(2,1)}, u32[]{:S(2)}, u32[]{:S(2)}) %all-to-all-start) | async-done | bytes 2097184 | tf_op jit(solution)/shard_map/all_to_all | solution.py:43
  78.0 5.9 %add_bitcast_fusion = f32[2,10,128,512]{3,1,2,0:T(8,128)S(1)} fusion(f32[2,128,512,10]{2,3,1,0:T(8,128)} %fusion.45, bf16[2,8,128,512]{3,2,0,1:T(8,128)(2,1)} %all-to-all-done, s32[8]{0:T(128)S(1)} %copy-done.9), kind=kOutput, calls=%fused_computation.5 | convolution fusion | flops 22282320 | bytes 12582944 | tf_op jit(solution)/shard_map/bs,tsid->tbid/dot_general | solution.py:51
  84.0 3.0 copy.37
  87.1 5.5 %fusion.5 = (bf16[2560,512]{1,0:T(8,128)(2,1)}, bf16[2560,512]{1,0:T(8,128)(2,1)}, bf16[2560,512]{1,0:T(8,128)(2,1)S(1)}) fusion(f32[2,10,128,512]{3,2,1,0:T(8,128)S(1)} %copy.37, bf16[2,1280,512]{2,1,0:T(8,128)(2,1)S(1)} %copy-done.2, bf16[2,1280,512]{2,1,0:T(8,128)(2,1)S(1)} %copy-done.16, bf16[2560,512]{1,0:T(8,128)(2,1)S(1)} %bitcast.113, ...), kind=kOutput, calls=%fused_computation.14 | convolution fusion | flops 1361838080 | bytes 21495808 | tf_op jit(solution)/shard_map/dot_general | solution.py:31
  94.6 3.9 %copy.40 = bf16[8,2,128,512]{2,3,1,0:T(8,128)(2,1)} copy(bf16[8,2,128,512]{3,2,1,0:T(8,128)(2,1)} %gather_fusion.3) | data formatting | bytes 4194304 | tf_op jit(solution)/shard_map/jit(_take)/gather | solution.py:60
  98.6 3.2 %select_bitcast_fusion = bf16[2,8,128,512]{2,3,0,1:T(8,128)(2,1)} fusion(bf16[8,2,128,512]{2,3,1,0:T(8,128)(2,1)} %copy.40, pred[8]{0:T(512)(128)(4,1)S(1)} %copy-done.15), kind=kLoop, calls=%fused_computation.36 | loop fusion | flops 1048576 | bytes 4194312 | tf_op jit(solution)/shard_map/jit(_take)/select_n | solution.py:60
  101.8 4.3 %all-to-all-start.1 = ((bf16[2,8,128,512]{2,3,0,1:T(8,128)(2,1)}), bf16[2,8,128,512]{2,3,0,1:T(8,128)(2,1)}, u32[]{:S(2)}, u32[]{:S(2)}) async-start(bf16[2,8,128,512]{2,3,0,1:T(8,128)(2,1)} %select_bitcast_fusion), calls=%async_computation.1 | async-start | bytes 4194304 | tf_op jit(solution)/shard_map/all_to_all | solution.py:61
  106.7 4.1 %gather_fusion.2 = bf16[20,2,128,512]{3,2,1,0:T(8,128)(2,1)} fusion(bf16[2,10,128,512]{3,2,1,0:T(8,128)(2,1)S(1)} %bitcast.104, s32[1024]{0:T(1024)S(1)} %pad_clamp_fusion.1), kind=kCustom, calls=%fused_computation.2.clone | custom fusion | bytes 10485840 | tf_op jit(solution)/shard_map/jit(_take)/gather | solution.py:65
  110.8 6.6 %convert_bitcast_fusion = bf16[2,20,128,512]{2,3,0,1:T(8,128)(2,1)} fusion(bf16[20,2,128,512]{3,2,1,0:T(8,128)(2,1)} %gather_fusion.2, pred[20]{0:T(512)(128)(4,1)S(1)} %copy-done.18, bf16[20,128,128]{2,1,0:T(8,128)(2,1)S(1)} %copy-done), kind=kOutput, calls=%fused_computation.24 | convolution fusion | flops 676331520 | bytes 11141140 | tf_op jit(solution)/shard_map/lji,tljd->tlid/dot_general | solution.py:66
  117.4 8.8 %copy.39 = bf16[2,20,128,512]{3,1,2,0:T(8,128)(2,1)} copy(bf16[2,20,128,512]{2,3,0,1:T(8,128)(2,1)} %convert_bitcast_fusion) | data formatting | bytes 10485760 | tf_op jit(solution)/shard_map/convert_element_type | solution.py:68
  126.3 4.4 %convolution_bitcast_fusion = f32[512,512]{0,1:T(8,128)} fusion(bf16[2560,512]{1,0:T(8,128)(2,1)S(1)} %copy-done.4, bf16[2560,512]{1,0:T(8,128)(2,1)} %bitcast.112), kind=kOutput, calls=%fused_computation.41 | convolution fusion | flops 1342177280 | bytes 6291456 | tf_op jit(solution)/shard_map/dot_general | solution.py:79
  130.7 4.7 %fusion.42 = f32[2,128,512,10]{2,3,1,0:T(8,128)} fusion(bf16[2,20,128,512]{3,1,2,0:T(8,128)(2,1)S(1)} %copy-done.1, s32[20]{0:T(128)S(1)} %copy-done.11, bf16[20]{0:T(256)(128)(2,1)S(1)} %compare_convert_fusion), kind=kOutput, calls=%fused_computation.59 | convolution fusion | flops 52429200 | bytes 10485880 | tf_op jit(solution)/shard_map/bl,tlid->tbid/dot_general | solution.py:69
  135.4 18.5 %all-to-all-done.1 = bf16[2,8,128,512]{2,3,0,1:T(8,128)(2,1)} async-done(((bf16[2,8,128,512]{2,3,0,1:T(8,128)(2,1)}), bf16[2,8,128,512]{2,3,0,1:T(8,128)(2,1)}, u32[]{:S(2)}, u32[]{:S(2)}) %all-to-all-start.1) | async-done | bytes 2097184 | tf_op jit(solution)/shard_map/all_to_all | solution.py:61
  159.3 5.6 %fusion.16 = bf16[2,10,128,512]{3,1,2,0:T(8,128)(2,1)S(1)} fusion(f32[2,128,512,10]{2,3,1,0:T(8,128)} %fusion.42, bf16[2,8,128,512]{3,1,2,0:T(8,128)(2,1)} %copy.41, s32[8]{0:T(128)S(1)} %copy-done.12), kind=kOutput, calls=%fused_computation.30 | convolution fusion | flops 23593040 | bytes 9961504 | tf_op jit(solution)/shard_map/bs,tsid->tbid/dot_general | solution.py:72
  172.1 3.3 %fusion.2 = bf16[2560,512]{1,0:T(8,128)(2,1)} fusion(f32[2560,512]{1,0:T(8,128)S(1)} %fusion.64, bf16[2560,512]{1,0:T(8,128)(2,1)S(1)} %bitcast.109, bf16[2560,512]{1,0:T(8,128)(2,1)S(1)} %copy-done.5, bf16[512,512]{1,0:T(8,128)(2,1)S(1)} %copy-done.7), kind=kOutput, calls=%fused_computation.11 | convolution fusion | flops 1347420160 | bytes 13631488 | tf_op jit(solution)/shard_map/dot_general | solution.py:77
  175.5 127.0 %all-reduce.3.cloned.1.call-done = (f32[512,512]{0,1:T(8,128)}, f32[512,512]{0,1:T(8,128)}) async-done(((f32[512,512]{0,1:T(8,128)}, f32[512,512]{0,1:T(8,128)}), (f32[512,512]{0,1:T(8,128)}, f32[512,512]{0,1:T(8,128)})) %all-reduce.3.cloned.1.call-update) | async-done | bytes 2097168 | tf_op jit(solution)/shard_map/psum | solution.py:80
  (64 shorter events, 24.1 us)
Async XLA Ops:
  7.2 26.7 %copy-start = (bf16[20,128,128]{2,1,0:T(8,128)(2,1)S(1)}, bf16[20,128,128]{2,1,0:T(8,128)(2,1)}, u32[]{:S(2)}) copy-start(bf16[20,128,128]{2,1,0:T(8,128)(2,1)} %param.23) | copy-start | bytes 1966084
  9.2 5.4 %copy-start.13 = (bf16[8]{0:T(256)(128)(2,1)}, bf16[8]{0:T(256)(128)(2,1)S(1)}, u32[]{:S(2)}) copy-start(bf16[8]{0:T(256)(128)(2,1)S(1)} %convert_element_type.78) | copy-start | bytes 52
  12.6 2.0 copy-start.8
  22.3 7.4 %copy-start.11 = (s32[20]{0:T(128)S(1)}, s32[20]{0:T(128)}, u32[]{:S(2)}) copy-start(s32[20]{0:T(128)} %param.21) | copy-start | bytes 244
  22.3 55.7 %all-to-all-start = ((bf16[2,8,128,512]{3,2,0,1:T(8,128)(2,1)}), bf16[2,8,128,512]{3,2,0,1:T(8,128)(2,1)}, u32[]{:S(2)}, u32[]{:S(2)}) async-start(bf16[2,8,128,512]{3,2,0,1:T(8,128)(2,1)} %copy.35), calls=%async_computation | async-start | bytes 4194304 | tf_op jit(solution)/shard_map/all_to_all | solution.py:43
  40.4 9.3 %copy-start.9 = (s32[8]{0:T(128)S(1)}, s32[8]{0:T(128)}, u32[]{:S(2)}) copy-start(s32[8]{0:T(128)} %param.24) | copy-start | bytes 100
  40.4 9.8 %copy-start.10 = (s32[20]{0:T(128)S(1)}, s32[20]{0:T(128)}, u32[]{:S(2)}) copy-start(s32[20]{0:T(128)} %param.20) | copy-start | bytes 244
  84.0 3.1 copy-start.2
  84.0 3.1 copy-start.6
  84.0 3.1 copy-start.16
  94.6 3.9 %copy-start.15 = (pred[8]{0:T(512)(128)(4,1)S(1)}, pred[8]{0:T(512)(128)(4,1)}, u32[]{:S(2)}) copy-start(pred[8]{0:T(512)(128)(4,1)} %compare_and_fusion) | copy-start | bytes 28
  101.8 52.2 %all-to-all-start.1 = ((bf16[2,8,128,512]{2,3,0,1:T(8,128)(2,1)}), bf16[2,8,128,512]{2,3,0,1:T(8,128)(2,1)}, u32[]{:S(2)}, u32[]{:S(2)}) async-start(bf16[2,8,128,512]{2,3,0,1:T(8,128)(2,1)} %select_bitcast_fusion), calls=%async_computation.1 | async-start | bytes 4194304 | tf_op jit(solution)/shard_map/all_to_all | solution.py:61
  106.1 196.4 %all-reduce.3.cloned.1.call-start = ((), (), s32[]{:S(2)}) async-start(), calls=%async_computation.2 | async-start | bytes 4194304 | tf_op jit(solution)/shard_map/psum | solution.py:80
  106.7 4.1 %copy-start.18 = (pred[20]{0:T(512)(128)(4,1)S(1)}, pred[20]{0:T(512)(128)(4,1)}, u32[]{:S(2)}) copy-start(pred[20]{0:T(512)(128)(4,1)} %compare_and_fusion.1) | copy-start | bytes 64
  117.4 8.9 %copy-start.4 = (bf16[2560,512]{1,0:T(8,128)(2,1)S(1)}, bf16[2560,512]{1,0:T(8,128)(2,1)}, u32[]{:S(2)}) copy-start(bf16[2560,512]{1,0:T(8,128)(2,1)} %get-tuple-element.24) | copy-start | bytes 7864324
  126.3 4.4 %copy-start.1 = (bf16[2,20,128,512]{3,1,2,0:T(8,128)(2,1)S(1)}, bf16[2,20,128,512]{3,1,2,0:T(8,128)(2,1)}, u32[]{:S(2)}) copy-start(bf16[2,20,128,512]{3,1,2,0:T(8,128)(2,1)} %copy.39) | copy-start | bytes 15728644
  130.7 23.2 %copy-start.14 = (bf16[8]{0:T(256)(128)(2,1)S(1)}, bf16[8]{0:T(256)(128)(2,1)}, u32[]{:S(2)}) copy-start(bf16[8]{0:T(256)(128)(2,1)} %copy-done.13) | copy-start | bytes 52
  156.3 3.0 copy-start.12
  165.0 1.7 copy-start.17
  169.2 2.9 copy-start.3
  169.2 2.9 copy-start.5
  169.3 2.9 copy-start.7
Sparse Core Ops, SparseCore 0:
  169.3 133.0 all-reduce.2
where the time goes:
time: 315 us; the launch traced here: 314 us
  waiting for transfers between devices  166 us (53%)
  matrix products  65.1 us (21%)
  local copies, waits for them, and re-layouts  48 us (15%)
  between operations  14.9 us (5%)
  starting transfers between devices  11.8 us (4%)
  other arithmetic  8.1 us (3%)
    psum x1, waiting for transfers between devices, per_device(): lax.psum((partial_value, partial_gate), ('tm', 'asset'))  127 us
    all_to_all x1, waiting for transfers between devices, per_device(): lax.all_to_all(terms, 'asset', split_axis=1, concat_axis=1, tiled=True)  20.3 us
    all_to_all x1, waiting for transfers between devices, per_device(): lax.all_to_all(rows_needed, 'asset', split_axis=1, concat_axis=1, tiled=T...  18.5 us
    convert_element_type x1, local copies, waits for them, and re-layouts, per_device(): local_back = jnp.einsum('lji,tljd->tlid', local_tiles, taken, preferred_e...  8.85 us
    convert_element_type x1, local copies, waits for them, and re-layouts, per_device(): local_terms = jnp.einsum('lij,tljd->tlid', local_tiles, picked, preferred...  8.62 us
    dot_general x1, matrix products, per_device(): jnp.einsum('bl,tlid->tbid', row_select, local_terms, preferred_element_ty...  7.47 us
    all_to_all x1, starting transfers between devices, per_device(): lax.all_to_all(terms, 'asset', split_axis=1, concat_axis=1, tiled=True)  7.38 us
    dot_general x1, matrix products, per_device(): jnp.einsum('lji,tljd->tlid', local_tiles, taken, preferred_element_type=j...  6.62 us
  transfers between devices with their start and end apart: 3, of which 3 were waited for; matrix products, arithmetic and copies ran while one was open for 20% of the time, Pallas kernels for 0%

commit v1 on v0

v1 whole, which is shorter than its diff:
```python
import math

import jax
import jax.numpy as jnp
from jax import lax
from jax.experimental import pallas as pl
from jax.experimental.pallas import tpu as pltpu
from jax.sharding import PartitionSpec as P

F32 = jnp.float32
BF16 = jnp.bfloat16
ANY = pl.BlockSpec(memory_space=pl.ANY)
VMEM = pl.BlockSpec(memory_space=pltpu.VMEM)
SMEM = pl.BlockSpec(memory_space=pltpu.SMEM)
MIB = 1 << 20


def params(mib):
    return pltpu.CompilerParams(vmem_limit_bytes=mib * MIB)


def cost(flops, moved):
    return pl.CostEstimate(flops=int(flops), bytes_accessed=int(moved), transcendentals=0)


def mm(a, b):
    return lax.dot_general(a, b, (((1,), (0,)), ((), ())), preferred_element_type=F32)


def mm_tn(a, b):
    return lax.dot_general(a, b, (((0,), (0,)), ((), ())), preferred_element_type=F32)


def mm_nt(a, b):
    return lax.dot_general(a, b, (((1,), (1,)), ((), ())), preferred_element_type=F32)


def after(x, *others):
    return lax.optimization_barrier((x,) + others)[0]


def row_chunk(rows, most):
    return max(c for c in range(8, most + 1, 8) if rows % c == 0)


def target_of(index, shift, n):
    return index ^ shift if n & (n - 1) == 0 else (index + shift) % n


def source_of(index, shift, n):
    return index ^ shift if n & (n - 1) == 0 else (index + n - shift) % n


def exchange(block, shift, n):
    return lax.ppermute(block, "asset", [(i, target_of(i, shift, n)) for i in range(n)])


def send_forward(me, features, tiles, cols, live, shifts, n):
    steps, _, width = features.shape
    tile = tiles.shape[1]
    count = len(shifts)

    def body(me_ref, cols_ref, live_ref, tiles_ref, f_ref, *rest):
        outs, (buf, sem) = rest[:count], rest[count:]
        copies = []
        for j, shift in enumerate(shifts):
            col = cols_ref[target_of(me_ref[0], shift, n)]
            start = pl.multiple_of(col * tile, tile)
            copy = pltpu.make_async_copy(f_ref.at[:, pl.ds(start, tile), :], buf.at[j], sem.at[j])
            copy.start()
            copies.append(copy)
        for j, shift in enumerate(shifts):
            to = target_of(me_ref[0], shift, n)
            weights = tiles_ref[to] * live_ref[to].astype(F32).astype(BF16)
            copies[j].wait()
            for t in range(steps):
                outs[j][t] = mm(weights, buf[j, t]).astype(BF16)

    block = jax.ShapeDtypeStruct((steps, tile, width), BF16)
    size = steps * tile * width
    return pl.pallas_call(
        body,
        out_shape=[block] * count,
        in_specs=[SMEM, SMEM, SMEM, VMEM, ANY],
        out_specs=[VMEM] * count,
        scratch_shapes=[pltpu.VMEM((count, steps, tile, width), BF16), pltpu.SemaphoreType.DMA((count,))],
        compiler_params=params(32),
        cost_estimate=cost(2 * count * size * tile, 4 * count * size),
        name="send_forward",
    )(me, cols, live, tiles, features)


def send_backward(me, back, rows, shifts, n, tile):
    steps, _, width = back.shape
    count = len(shifts)

    def body(me_ref, rows_ref, r_ref, *rest):
        outs, sem = rest[:count], rest[count]
        copies = []
        for j, shift in enumerate(shifts):
            row = rows_ref[target_of(me_ref[0], shift, n)]
            start = pl.multiple_of(row * tile, tile)
            copy = pltpu.make_async_copy(r_ref.at[:, pl.ds(start, tile), :], outs[j], sem.at[j])
            copy.start()
            copies.append(copy)
        for copy in copies:
            copy.wait()

    block = jax.ShapeDtypeStruct((steps, tile, width), BF16)
    return pl.pallas_call(
        body,
        out_shape=[block] * count,
        in_specs=[SMEM, SMEM, ANY],
        out_specs=[ANY] * count,
        scratch_shapes=[pltpu.SemaphoreType.DMA((count,))],
        compiler_params=params(32),
        cost_estimate=cost(0, 4 * count * steps * tile * width),
        name="send_backward",
    )(me, rows, back)


def project(flat, grad, w_value, w_gate):
    rows, width = flat.shape
    chunk = row_chunk(rows, 640)

    def body(f_ref, c_ref, wv_ref, wg_ref, gate_ref, dagg_ref, back_ref):
        gate = jax.nn.sigmoid(mm(f_ref[...], wg_ref[...]))
        gate_ref[...] = gate
        dagg = (c_ref[...].astype(F32) * gate).astype(BF16)
        dagg_ref[...] = dagg
        back_ref[...] = mm_nt(dagg, wv_ref[...]).astype(BF16)

    line = pl.BlockSpec((chunk, width), lambda i: (i, 0))
    whole = pl.BlockSpec((width, width), lambda i: (0, 0))
    half = jax.ShapeDtypeStruct((rows, width), BF16)
    return pl.pallas_call(
        body,
        grid=(rows // chunk,),
        out_shape=[jax.ShapeDtypeStruct((rows, width), F32), half, half],
        in_specs=[line, line, whole, whole],
        out_specs=[line] * 3,
        compiler_params=params(32),
        cost_estimate=cost(4 * rows * width * width, 12 * rows * width),
        name="project",
    )(flat, grad, w_value, w_gate)


def local_sum(tiles, count, place, pick, source, base):
    steps, assets, width = source.shape
    slots, tile, _ = tiles.shape
    transposed = base is not None

    def body(count_ref, place_ref, pick_ref, tiles_ref, s_ref, *rest):
        out = rest[-1]
        out[...] = rest[0][...].astype(F32) if transposed else jnp.zeros(out.shape, F32)

        @pl.loop(0, count_ref[0])
        def _(l):
            to = pl.ds(pl.multiple_of(place_ref[l] * tile, tile), tile)
            at = pl.ds(pl.multiple_of(pick_ref[l] * tile, tile), tile)
            weights = tiles_ref[l]
            for t in range(steps):
                block = s_ref[t, at, :]
                out[t, to, :] += mm_tn(weights, block) if transposed else mm(weights, block)

    extra = [base] if transposed else []
    return pl.pallas_call(
        body,
        out_shape=jax.ShapeDtypeStruct(source.shape, F32),
        in_specs=[SMEM, SMEM, SMEM, VMEM, VMEM] + [VMEM] * len(extra),
        out_specs=VMEM,
        compiler_params=params(40),
        cost_estimate=cost(2 * slots * tile * steps * tile * width, 8 * steps * assets * width),
        name="local_back" if transposed else "local_forward",
    )(count, place, pick, tiles, source, *extra)


def gather_sum(me, local, arrived, rows, dagg, shifts, n, tile):
    steps, assets, width = local.shape
    blocks = assets // tile
    count = len(shifts)
    per = max(p for p in range(1, 6) if blocks % p == 0)

    def body(me_ref, rows_ref, l_ref, d_ref, *rest):
        parts, (g_ref, w_ref) = rest[:count], rest[count:]
        t, b = pl.program_id(0), pl.program_id(1)
        g_ref[...] = l_ref[...]

        for j, shift in enumerate(shifts):
            place = rows_ref[source_of(me_ref[0], shift, n)] - b * per

            @pl.when((place >= 0) & (place < per))
            def _():
                to = pl.ds(pl.multiple_of(place * tile, tile), tile)
                g_ref[0, to, :] += parts[j][t].astype(F32)

        part = mm_tn(g_ref[0].astype(BF16), d_ref[0])

        @pl.when((t == 0) & (b == 0))
        def _():
            w_ref[...] = part

        @pl.when((t > 0) | (b > 0))
        def _():
            w_ref[...] += part

    line = pl.BlockSpec((1, per * tile, width), lambda t, b: (t, b, 0))
    piece = pl.BlockSpec((steps, tile, width), lambda t, b: (0, 0, 0))
    whole = pl.BlockSpec((width, width), lambda t, b: (0, 0))
    return pl.pallas_call(
        body,
        grid=(steps, blocks // per),
        out_shape=[jax.ShapeDtypeStruct(local.shape, F32), jax.ShapeDtypeStruct((width, width), F32)],
        in_specs=[SMEM, SMEM, line, line] + [piece] * count,
        out_specs=[line, whole],
        compiler_params=params(40),
        cost_estimate=cost(2 * steps * assets * width * width, 12 * steps * assets * width),
        name="gather_sum",
    )(me, rows, local, dagg, *arrived)


def mix(total, w_value, gate, flat, grad):
    rows, width = flat.shape
    chunk = row_chunk(rows, 640)

    def body(g_ref, wv_ref, gate_ref, f_ref, c_ref, out_ref, dgate_ref, w_ref):
        i = pl.program_id(0)
        agg = mm(g_ref[...].astype(BF16), wv_ref[...])
        gate = gate_ref[...]
        kept = gate * agg
        out_ref[...] = (f_ref[...].astype(F32) + kept).astype(BF16)
        dgate = (c_ref[...].astype(F32) * kept * (1.0 - gate)).astype(BF16)
        dgate_ref[...] = dgate
        part = mm_tn(f_ref[...], dgate)

        @pl.when(i == 0)
        def _():
            w_ref[...] = part

        @pl.when(i > 0)
        def _():
            w_ref[...] += part

    line = pl.BlockSpec((chunk, width), lambda i: (i, 0))
    whole = pl.BlockSpec((width, width), lambda i: (0, 0))
    half = jax.ShapeDtypeStruct((rows, width), BF16)
    return pl.pallas_call(
        body,
        grid=(rows // chunk,),
        out_shape=[half, half, jax.ShapeDtypeStruct((width, width), F32)],
        in_specs=[line, whole, line, line, line],
        out_specs=[line, line, whole],
        compiler_params=params(40),
        cost_estimate=cost(4 * rows * width * width, 16 * rows * width),
        name="mix",
    )(total, w_value, gate, flat, grad)


def add_gate(base, dgate, w_gate):
    rows, width = base.shape
    chunk = row_chunk(rows, 640)

    def body(b_ref, d_ref, w_ref, out_ref):
        out_ref[...] = b_ref[...] + mm_nt(d_ref[...], w_ref[...])

    line = pl.BlockSpec((chunk, width), lambda i: (i, 0))
    whole = pl.BlockSpec((width, width), lambda i: (0, 0))
    return pl.pallas_call(
        body,
        grid=(rows // chunk,),
        out_shape=jax.ShapeDtypeStruct((rows, width), F32),
        in_specs=[line, line, whole],
        out_specs=line,
        compiler_params=params(32),
        cost_estimate=cost(2 * rows * width * width, 10 * rows * width),
        name="add_gate",
    )(base, dgate, w_gate)


def finish(me, base, returned, cols, live, tiles, shifts, n):
    steps, assets, width = base.shape
    tile = tiles.shape[1]
    blocks = assets // tile
    count = len(shifts)

    def body(me_ref, cols_ref, live_ref, tiles_ref, b_ref, *rest):
        parts, (out_ref, acc) = rest[:count], rest[count:]
        b = pl.program_id(0)
        acc[...] = b_ref[...]
        for j, shift in enumerate(shifts):
            of = source_of(me_ref[0], shift, n)

            @pl.when((cols_ref[of] == b) & (live_ref[of] != 0))
            def _():
                weights = tiles_ref[of]
                for t in range(steps):
                    acc[t] += mm_tn(weights, parts[j][t])

        out_ref[...] = acc[...].astype(BF16)

    line = pl.BlockSpec((steps, tile, width), lambda b: (0, b, 0))
    piece = pl.BlockSpec((steps, tile, width), lambda b: (0, 0, 0))
    every = pl.BlockSpec(tiles.shape, lambda b: (0, 0, 0))
    size = steps * assets * width
    return pl.pallas_call(
        body,
        grid=(blocks,),
        out_shape=jax.ShapeDtypeStruct(base.shape, BF16),
        in_specs=[SMEM, SMEM, SMEM, every, line] + [piece] * count,
        out_specs=line,
        scratch_shapes=[pltpu.VMEM((steps, tile, width), F32)],
        compiler_params=params(32),
        cost_estimate=cost(2 * size * tile, 10 * size),
        name="finish",
    )(me, cols, live, tiles, base, *returned)


def levels(tm, asset):
    low = max(d for d in range(1, math.isqrt(asset) + 1) if asset % d == 0)
    pair = 2 if tm % 2 == 0 else 1
    return [("tm", 1, pair, tm), ("tm", pair, tm // pair, tm), ("asset", 1, low, asset), ("asset", low, asset // low, asset)]


def member(level):
    axis, stride, size, _ = level
    return (lax.axis_index(axis) // stride) % size


def pairs_of(level, shift):
    _, stride, size, n = level
    return [(i, i + ((i // stride + shift) % size - (i // stride) % size) * stride) for i in range(n)]


def scatter_sum(x, level):
    axis, _, size, _ = level
    me = member(level)
    total = lax.dynamic_index_in_dim(x, me, 0, keepdims=False)
    arrived = [
        lax.ppermute(lax.dynamic_index_in_dim(x, (me + s) % size, 0, keepdims=False), axis, pairs_of(level, s))
        for s in range(1, size)
    ]
    for part in arrived:
        total = total + part
    return total


def spread(x, level):
    axis, _, size, _ = level
    return jnp.stack([x] + [lax.ppermute(x, axis, pairs_of(level, s)) for s in range(1, size)])


def unshuffle(x, order, shape):
    sizes = [level[2] for level in order]
    place = jnp.arange(math.prod(sizes), dtype=jnp.int32)
    index, stride = 0, 1
    for level in reversed(order):
        size = level[2]
        index = index + ((member(level) - place // stride) % size) * stride
        stride *= size
    flat = x.reshape(math.prod(sizes), -1, shape[1])
    return jnp.take(flat, index, axis=0, mode="clip").reshape(shape).astype(F32)


def per_device(
    features,
    w_value,
    w_gate,
    cotangent,
    local_rows,
    local_cols,
    local_count,
    local_tiles,
    remote_rows,
    remote_cols,
    remote_live,
    remote_tiles,
):
    steps, assets, width = features.shape
    tile = local_tiles.shape[1]
    n = lax.axis_size("asset")
    tm = lax.axis_size("tm")
    me = lax.axis_index("asset").astype(jnp.int32).reshape(1)
    flat = features.reshape(-1, width)
    grad = cotangent.reshape(-1, width)

    far = list(range(n // 2, n))
    near = list(range(1, n // 2))
    shifts = far + near

    sent = dict(zip(shifts, send_forward(me, features, remote_tiles, remote_cols, remote_live, shifts, n)))
    came = {}
    for j, s in enumerate(far):
        came[s] = exchange(sent[s] if j < 2 else after(sent[s], came[far[j - 2]]), s, n)
    for j, s in enumerate(near):
        came[s] = exchange(sent[s] if j < 3 else after(sent[s], came[near[j - 3]]), s, n)

    gate, dagg, back = project(flat, grad, w_value, w_gate)
    back_steps = back.reshape(features.shape)
    owed = dict(zip(shifts, send_backward(me, back_steps, remote_rows, shifts, n, tile)))
    local = local_sum(local_tiles, local_count, local_rows, local_cols, features, None)
    base = local_sum(local_tiles, local_count, local_cols, local_rows, back_steps, cotangent)

    half = len(far) // 2
    got = {}
    for j, s in enumerate(far[:half]):
        got[s] = exchange(after(owed[s], came[far[half + j]]), s, n)

    total, part_value = gather_sum(
        me, local, [came[s] for s in shifts], remote_rows, dagg.reshape(features.shape), shifts, n, tile
    )
    output, dgate, part_gate = mix(total.reshape(-1, width), w_value, gate, flat, grad)
    base = add_gate(base.reshape(-1, width), dgate, w_gate).reshape(features.shape)

    order = levels(tm, n)
    sizes = [level[2] for level in order]
    rows = width // math.prod(sizes)
    sums = [part.reshape(sizes + [rows, width]) for part in (part_value, part_gate)]
    for level in order[:-1]:
        sums = [scatter_sum(x, level) for x in sums]
    both = jnp.concatenate(sums, axis=1)
    both = scatter_sum(both, order[-1]).astype(BF16)
    both = spread(both, order[-1])
    for j, s in enumerate(far[half:]):
        got[s] = exchange(after(owed[s], both), s, n)
    for j, s in enumerate(near):
        got[s] = exchange(after(owed[s], both), s, n)
    for level in reversed(order[:-1]):
        both = spread(both, level)
    both = both.reshape(math.prod(sizes), 2, rows, width)
    scale = float(steps * assets * tm * n) ** (-0.5)
    grad_value, grad_gate = [unshuffle(both[:, i], order, (width, width)) * scale for i in range(2)]

    grad_features = finish(
        me, base, [got[s] for s in shifts], remote_cols, remote_live, remote_tiles, shifts, n
    )
    return output.reshape(features.shape), grad_features, grad_value, grad_gate


def solution(mesh):
    return jax.shard_map(
        per_device,
        mesh=mesh,
        in_specs=(
            P("tm", "asset", None),
            P(),
            P(),
            P("tm", "asset", None),
            P("asset"),
            P("asset"),
            P("asset"),
            P("asset", None, None),
            P("asset"),
            P("asset"),
            P("asset"),
            P("asset", None, None),
        ),
        out_specs=(P("tm", "asset", None), P("tm", "asset", None), P(), P()),
        check_vma=False,
    )
```

time: 315 us -> 181 us (0.57)
  waiting for transfers between devices: 166 us -> 70 us
  matrix products: 65.1 us -> 0 us
  Pallas kernels: 0 us -> 40 us
  starting transfers between devices: 11.8 us -> 42.5 us
  local copies, waits for them, and re-layouts: 48 us -> 21.9 us
  between operations: 14.9 us -> 1.71 us
  other arithmetic: 8.1 us -> 4.01 us
    psum x1 -> x0, waiting for transfers between devices: 127 us -> none  [per_device(): lax.psum((partial_value, partial_gate), ('tm', 'asset'))]
    ppermute x0 -> x29, waiting for transfers between devices: none -> 70 us  [the longest x14 42.3 us: exchange(): lax.ppermute(block, 'asset', [(i, target_of(i, shift, n)) for i in range(...]
    dot_general x14 -> x0, matrix products: 65.1 us -> none  [the longest x1 7.47 us: per_device(): jnp.einsum('bl,tlid->tbid', row_select, local_terms, preferred_element_ty...]
    ppermute x0 -> x29, starting transfers between devices: none -> 42.5 us  [the longest x14 28.4 us: exchange(): lax.ppermute(block, 'asset', [(i, target_of(i, shift, n)) for i in range(...]
    pallas_call x0 -> x9, Pallas kernels: none -> 40 us  [the longest x2 9.7 us: local_sum(): pl.pallas_call(body, out_shape=jax.ShapeDtypeStruct(source.shape, F32), i...]
    all_to_all x2 -> x0, waiting for transfers between devices: 38.8 us -> none  [the longest x1 20.3 us: per_device(): lax.all_to_all(terms, 'asset', split_axis=1, concat_axis=1, tiled=True)]
    convert_element_type x5 -> x0, local copies, waits for them, and re-layouts: 25.9 us -> none  [the longest x1 8.85 us: per_device(): local_back = jnp.einsum('lji,tljd->tlid', local_tiles, taken, preferred_e...]
    unnamed x40 -> x62, local copies, waits for them, and re-layouts: 2.97 us -> 19.7 us
  transfers between devices with their start and end apart: 3 -> 29, of which waited for: 3 -> 15; matrix products, arithmetic and copies ran while one was open for 20% -> 1% of each run, Pallas kernels for 0% -> 17%
where the time goes in v1:
time: 181 us; the launch traced here: 180 us
  waiting for transfers between devices  70 us (39%)
  starting transfers between devices  42.5 us (23%)
  Pallas kernels  40 us (22%)
  local copies, waits for them, and re-layouts  21.9 us (12%)
  other arithmetic  4.01 us (2%)
    ppermute x14, waiting for transfers between devices, exchange(): lax.ppermute(block, 'asset', [(i, target_of(i, shift, n)) for i in range(...  42.3 us
    ppermute x14, starting transfers between devices, exchange(): lax.ppermute(block, 'asset', [(i, target_of(i, shift, n)) for i in range(...  28.4 us
    unnamed x62, local copies, waits for them, and re-layouts  19.7 us
    ppermute x9, waiting for transfers between devices, scatter_sum(): lax.ppermute(lax.dynamic_index_in_dim(x, (me + s) % size, 0, keepdims=Fal...  19.6 us
    pallas_call x2, Pallas kernels, local_sum(): pl.pallas_call(body, out_shape=jax.ShapeDtypeStruct(source.shape, F32), i...  9.7 us
    ppermute x9, starting transfers between devices, scatter_sum(): lax.ppermute(lax.dynamic_index_in_dim(x, (me + s) % size, 0, keepdims=Fal...  8.32 us
    pallas_call x1, Pallas kernels, mix(): pl.pallas_call(body, grid=(rows // chunk,), out_shape=[half, half, jax.Sh...  8.28 us
    ppermute x6, waiting for transfers between devices, spread(): lax.ppermute(x, axis, pairs_of(level, s))  8.08 us
  transfers between devices with their start and end apart: 29, of which 15 were waited for; matrix products, arithmetic and copies ran while one was open for 1% of the time, Pallas kernels for 17%

profile of v1, /device:TPU:0, one launch (start us, length us, event | category | flops | bytes accessed | tf_op | source)
XLA Modules:
  0.0 180.2 jit_solution(639280389817071996)
XLA Ops:
  4.7 3.2 %send_forward.1 = (bf16[2,128,512]{2,1,0:T(8,128)(2,1)S(1)}, bf16[2,128,512]{2,1,0:T(8,128)(2,1)S(1)}, bf16[2,128,512]{2,1,0:T(8,128)(2,1)}, bf16[2,128,512]{2,1...) custom-call(s32[1]{0:T(128)} %bitcast.me_ref, ...), custom_call_target="tpu_custom_call" | custom-call | flops 234881024 | bytes 3670016 | tf_op jit(solution)/shard_map/send_forward/pallas_call | solution.py:81
  7.9 4.1 %collective-permute-start = (bf16[2,128,512]{2,1,0:T(8,128)(2,1)S(1)}, bf16[2,128,512]{2,1,0:T(8,128)(2,1)S(1)}, u32[]{:S(2)}, u32[]{:S(2)}) collective-permute-start(bf16[2,128,512]{2,1,0:T(8,128)(2,1)S(1)} %get-tuple-element.36), channel_id=1, source_target_pairs={{0,4},{1,5},{2,6},{3,7},{4,0},{5,1},{6,2},{7,3},{8,12},{9,13},{10,... | collective-permute-start | bytes 786440 | tf_op jit(solution)/shard_map/ppermute | solution.py:55
  17.4 13.1 %collective-permute-done.rest_0_ = bf16[2,128,512]{2,1,0:T(8,128)(2,1)S(1)} collective-permute-done((bf16[2,128,512]{2,1,0:T(8,128)(2,1)S(1)}, bf16[2,128,512]{2,1,0:T(8,128)(2,1)S(1)}, u32[]{:S(2)}, u32[]{:S(2)}) %collective-permute-start) | collective-permute-done | bytes 262176 | tf_op jit(solution)/shard_map/ppermute | solution.py:55
  30.5 2.8 %collective-permute-start.2 = (bf16[2,128,512]{2,1,0:T(8,128)(2,1)}, bf16[2,128,512]{2,1,0:T(8,128)(2,1)}, u32[]{:S(2)}, u32[]{:S(2)}) collective-permute-start(bf16[2,128,512]{2,1,0:T(8,128)(2,1)} %get-tuple-element.39), channel_id=1, source_target_pairs={{0,6},{1,7},{2,4},{3,5},{4,2},{5,3},{6,0},{7,1},{8,14},{9,15},{10,... | collective-permute-start | bytes 786440 | tf_op jit(solution)/shard_map/ppermute | solution.py:55
  33.3 5.2 %collective-permute-done.1.rest_1_ = bf16[2,128,512]{2,1,0:T(8,128)(2,1)S(1)} collective-permute-done((bf16[2,128,512]{2,1,0:T(8,128)(2,1)S(1)}, bf16[2,128,512]{2,1,0:T(8,128)(2,1)S(1)}, u32[]{:S(2)}, u32[]{:S(2)}) %collective-permute-start.1) | collective-permute-done | bytes 262176 | tf_op jit(solution)/shard_map/ppermute | solution.py:55
  42.4 4.5 %local_forward.1.l_ref = f32[2,1280,512]{2,1,0:T(8,128)S(1)} custom-call(s32[1]{0:T(128)S(6)} %copy.16.count_ref, s32[20]{0:T(128)S(1)} %copy-done.25, s32[20]{0:T(128)S(1)} %copy-done.26, bf16[20,128,128]{2,1,0:T(8,128)(2,1)S(1)} %copy-done.10, bf16[2,1280,512]{2,1,0:T(8,128)(2,1)S(1)} %copy-done.1), custom_call_target="tpu_custom_call" | custom-call | flops 671088640 | bytes 10485760 | tf_op jit(solution)/shard_map/local_forward/pallas_call | solution.py:167
  47.0 2.4 %copy-done.2 = f32[2,1280,512]{2,1,0:T(8,128)} copy-done((f32[2,1280,512]{2,1,0:T(8,128)}, f32[2,1280,512]{2,1,0:T(8,128)S(1)}, u32[]{:S(2)}) %copy-start.2) | copy-done | bytes 5242904
  52.1 3.6 %project.1 = (f32[2560,512]{1,0:T(8,128)S(1)}, bf16[2560,512]{1,0:T(8,128)(2,1)S(1)}, bf16[2560,512]{1,0:T(8,128)(2,1)S(1)}) custom-call(bf16[2560,512]{1,0:T(8,128)(2,1)S(1)} %bitcast.73, bf16[2560,512]{1,0:T(8,128)(2,1)S(1)} %bitcast.77, bf16[512,512]{1,0:T(8,128)(2,1)S(1)} %copy-done.19, bf16[512,512]{1,0:T(8,128)(2,1)S(1)} %copy-done.20), custom_call_target="tpu_custom_call" | custom-call | flops 2684354560 | bytes 15728640 | tf_op jit(solution)/shard_map/project/pallas_call | solution.py:136
  59.6 6.1 %gather_sum.1 = (f32[2,1280,512]{2,1,0:T(8,128)S(1)}, f32[512,512]{1,0:T(8,128)S(1)}) custom-call(s32[1]{0:T(128)} %bitcast.me_ref, s32[8]{0:T(128)S(1)} %copy-done.24, f32[2,1280,512]{2,1,0:T(8,128)} %copy-done.2, bf16[2,1280,512]{2,1,0:T(8,128)(2,1)S(1)} %bitcast.82, bf16[2,128,512]{2,1,0:T(8,128)(2,1)S(1)} %collective-permute-done.rest_0_, ...), custom_call_target="tpu_custom_call" | custom-call | flops 1342177280 | bytes 15728640 | tf_op jit(solution)/shard_map/gather_sum/pallas_call | solution.py:210
  65.8 2.4 %copy-done.9 = f32[2,1280,512]{2,1,0:T(8,128)} copy-done((f32[2,1280,512]{2,1,0:T(8,128)}, f32[2,1280,512]{2,1,0:T(8,128)S(1)}, u32[]{:S(2)}) %copy-start.9) | copy-done | bytes 5242904
  69.0 8.3 %mix.1 = (bf16[2560,512]{1,0:T(8,128)(2,1)}, bf16[2560,512]{1,0:T(8,128)(2,1)S(1)}, f32[512,512]{1,0:T(8,128)S(1)}) custom-call(f32[2560,512]{1,0:T(8,128)} %bitcast.81, bf16[512,512]{1,0:T(8,128)(2,1)S(1)} %copy-done.19, f32[2560,512]{1,0:T(8,128)} %copy-done.8, bf16[2560,512]{1,0:T(8,128)(2,1)S(1)} %bitcast.74, bf16[2560,512]{1,0:T(8,128)(2,1)S(1)} %bitcast.78), custom_call_target="tpu_custom_call" | custom-call | flops 2684354560 | bytes 20971520 | tf_op jit(solution)/shard_map/mix/pallas_call | solution.py:247
  84.0 6.9 %collective-permute-done.10 = f32[2,4,16,512]{3,2,1,0:T(8,128)S(1)} collective-permute-done((f32[2,4,16,512]{3,2,1,0:T(8,128)S(1)}, f32[2,4,16,512]{3,2,1,0:T(8,128)S(1)}, u32[]{:S(2)}, u32[]{:S(2)}) %collective-permute-start.10) | collective-permute-done | bytes 262176 | tf_op jit(solution)/shard_map/ppermute | solution.py:339
  91.9 4.0 %collective-permute-done.13 = f32[2,4,16,512]{3,2,1,0:T(8,128)S(1)} collective-permute-done((f32[2,4,16,512]{3,2,1,0:T(8,128)S(1)}, f32[2,4,16,512]{3,2,1,0:T(8,128)S(1)}, u32[]{:S(2)}, u32[]{:S(2)}) %collective-permute-start.13) | collective-permute-done | bytes 262176 | tf_op jit(solution)/shard_map/ppermute | solution.py:339
  96.8 4.1 %collective-permute-done.14 = f32[4,16,512]{2,1,0:T(8,128)S(1)} collective-permute-done((f32[4,16,512]{2,1,0:T(8,128)S(1)}, f32[4,16,512]{2,1,0:T(8,128)S(1)}, u32[]{:S(2)}, u32[]{:S(2)}) %collective-permute-start.14) | collective-permute-done | bytes 131104 | tf_op jit(solution)/shard_map/ppermute | solution.py:339
  101.0 2.3 %collective-permute-start.17 = (f32[32,512]{1,0:T(8,128)S(1)}, f32[32,512]{1,0:T(8,128)S(1)}, u32[]{:S(2)}, u32[]{:S(2)}) collective-permute-start(f32[32,512]{1,0:T(8,128)S(1)} %get-tuple-element.74), channel_id=1, source_target_pairs={{0,6},{1,7},{2,0},{3,1},{4,2},{5,3},{6,4},{7,5},{8,14},{9,15},{10,... | collective-permute-start | bytes 196616 | tf_op jit(solution)/shard_map/ppermute | solution.py:339
  105.3 3.3 %collective-permute-done.16 = f32[32,512]{1,0:T(8,128)S(1)} collective-permute-done((f32[32,512]{1,0:T(8,128)S(1)}, f32[32,512]{1,0:T(8,128)S(1)}, u32[]{:S(2)}, u32[]{:S(2)}) %collective-permute-start.16) | collective-permute-done | bytes 65568 | tf_op jit(solution)/shard_map/ppermute | solution.py:339
  113.4 2.7 %collective-permute-done.19 = bf16[32,512]{1,0:T(8,128)(2,1)S(1)} collective-permute-done((bf16[32,512]{1,0:T(8,128)(2,1)S(1)}, bf16[32,512]{1,0:T(8,128)(2,1)S(1)}, u32[]{:S(2)}, u32[]{:S(2)}) %collective-permute-start.19) | collective-permute-done | bytes 32800 | tf_op jit(solution)/shard_map/ppermute | solution.py:349
  117.5 4.2 %collective-permute-done.26 = bf16[4,32,512]{2,1,0:T(8,128)(2,1)S(1)} collective-permute-done((bf16[4,32,512]{2,1,0:T(8,128)(2,1)S(1)}, bf16[4,32,512]{2,1,0:T(8,128)(2,1)S(1)}, u32[]{:S(2)}, u32[]{:S(2)}) %collective-permute-start.26) | collective-permute-done | bytes 131104 | tf_op jit(solution)/shard_map/ppermute | solution.py:349
  129.2 2.9 %collective-permute-start.22 = (bf16[2,128,512]{2,1,0:T(8,128)(2,1)S(1)}, bf16[2,128,512]{2,1,0:T(8,128)(2,1)S(1)}, u32[]{:S(2)}, u32[]{:S(2)}) collective-permute-start(bf16[2,128,512]{2,1,0:T(8,128)(2,1)S(1)} %get-tuple-element.59), channel_id=1, source_target_pairs={{0,7},{1,6},{2,5},{3,4},{4,3},{5,2},{6,1},{7,0},{8,15},{9,14},{10,... | collective-permute-start | bytes 786440 | tf_op jit(solution)/shard_map/ppermute | solution.py:55
  132.1 17.9 %collective-permute-done.7.rest_0_ = bf16[2,128,512]{2,1,0:T(8,128)(2,1)S(1)} collective-permute-done((bf16[2,128,512]{2,1,0:T(8,128)(2,1)S(1)}, bf16[2,128,512]{2,1,0:T(8,128)(2,1)S(1)}, u32[]{:S(2)}, u32[]{:S(2)}) %collective-permute-start.7) | collective-permute-done | bytes 262176 | tf_op jit(solution)/shard_map/ppermute | solution.py:55
  150.6 5.1 %collective-permute-done.8.rest_1_ = bf16[2,128,512]{2,1,0:T(8,128)(2,1)S(1)} collective-permute-done((bf16[2,128,512]{2,1,0:T(8,128)(2,1)S(1)}, bf16[2,128,512]{2,1,0:T(8,128)(2,1)S(1)}, u32[]{:S(2)}, u32[]{:S(2)}) %collective-permute-start.8) | collective-permute-done | bytes 262176 | tf_op jit(solution)/shard_map/ppermute | solution.py:55
  155.7 6.2 %collective-permute-start.25 = (bf16[2,128,512]{2,1,0:T(8,128)(2,1)S(1)}, bf16[2,128,512]{2,1,0:T(8,128)(2,1)S(1)}, u32[]{:S(2)}, u32[]{:S(2)}) collective-permute-start(bf16[2,128,512]{2,1,0:T(8,128)(2,1)S(1)} %get-tuple-element.65), channel_id=1, source_target_pairs={{0,3},{1,2},{2,1},{3,0},{4,7},{5,6},{6,5},{7,4},{8,11},{9,10},{10,... | collective-permute-start | bytes 786440 | tf_op jit(solution)/shard_map/ppermute | solution.py:55
  161.8 5.2 %local_back.1 = f32[2,1280,512]{2,1,0:T(8,128)S(1)} custom-call(s32[1]{0:T(128)S(6)} %copy.16.count_ref, s32[20]{0:T(128)S(1)} %copy-done.26, s32[20]{0:T(128)S(1)} %copy-done.25, bf16[20,128,128]{2,1,0:T(8,128)(2,1)S(1)} %copy-done.11, bf16[2,1280,512]{2,1,0:T(8,128)(2,1)S(1)} %bitcast.80, bf16[2,1280,512]{2,1,0:T(8,128)(2,1)S(1)} %copy-done.5), custom_call_target="tpu_custom_call" | custom-call | flops 671088640 | bytes 10485760 | tf_op jit(solution)/shard_map/local_back/pallas_call | solution.py:167
  170.4 6.2 %finish.1 = bf16[2,1280,512]{2,1,0:T(8,128)(2,1)} custom-call(s32[1]{0:T(128)} %bitcast.me_ref, s32[8]{0:T(128)S(1)} %copy-done.28, s32[8]{0:T(128)S(1)} %copy-done.30, bf16[8,128,128]{2,1,0:T(8,128)(2,1)S(1)} %copy-done.18, f32[2,1280,512]{2,1,0:T(8,128)S(1)} %bitcast.75, bf16[2,128,512]{2,1,0:T(8,128)(2,1)S(1)} %collective-permute-done.7.rest_0_, ...), custom_call_target="tpu_custom_call" | custom-call | flops 335544320 | bytes 13107200 | tf_op jit(solution)/shard_map/finish/pallas_call | solution.py:305
  (130 shorter events, 52.0 us)
Async XLA Ops:
  7.9 22.6 %collective-permute-start = (bf16[2,128,512]{2,1,0:T(8,128)(2,1)S(1)}, bf16[2,128,512]{2,1,0:T(8,128)(2,1)S(1)}, u32[]{:S(2)}, u32[]{:S(2)}) collective-permute-start(bf16[2,128,512]{2,1,0:T(8,128)(2,1)S(1)} %get-tuple-element.36), channel_id=1, source_target_pairs={{0,4},{1,5},{2,6},{3,7},{4,0},{5,1},{6,2},{7,3},{8,12},{9,13},{10,... | collective-permute-start | bytes 786440 | tf_op jit(solution)/shard_map/ppermute | solution.py:55
  12.0 26.4 %collective-permute-start.1 = (bf16[2,128,512]{2,1,0:T(8,128)(2,1)S(1)}, bf16[2,128,512]{2,1,0:T(8,128)(2,1)S(1)}, u32[]{:S(2)}, u32[]{:S(2)}) collective-permute-start(bf16[2,128,512]{2,1,0:T(8,128)(2,1)S(1)} %get-tuple-element.37), channel_id=1, source_target_pairs={{0,5},{1,4},{2,7},{3,6},{4,1},{5,0},{6,3},{7,2},{8,13},{9,12},{10,... | collective-permute-start | bytes 786440 | tf_op jit(solution)/shard_map/ppermute | solution.py:55
  13.2 46.3 %collective-permute-start.4 = (bf16[2,128,512]{2,1,0:T(8,128)(2,1)}, bf16[2,128,512]{2,1,0:T(8,128)(2,1)}, u32[]{:S(2)}, u32[]{:S(2)}) collective-permute-start(bf16[2,128,512]{2,1,0:T(8,128)(2,1)} %get-tuple-element.42), channel_id=1, source_target_pairs={{0,1},{1,0},{2,3},{3,2},{4,5},{5,4},{6,7},{7,6},{8,9},{9,8},{10,11... | collective-permute-start | bytes 786440 | tf_op jit(solution)/shard_map/ppermute | solution.py:55
  13.5 46.0 %collective-permute-start.5 = (bf16[2,128,512]{2,1,0:T(8,128)(2,1)}, bf16[2,128,512]{2,1,0:T(8,128)(2,1)}, u32[]{:S(2)}, u32[]{:S(2)}) collective-permute-start(bf16[2,128,512]{2,1,0:T(8,128)(2,1)} %get-tuple-element.43), channel_id=1, source_target_pairs={{0,2},{1,3},{2,0},{3,1},{4,6},{5,7},{6,4},{7,5},{8,10},{9,11},{10,... | collective-permute-start | bytes 786440 | tf_op jit(solution)/shard_map/ppermute | solution.py:55
  15.4 44.2 %collective-permute-start.6 = (bf16[2,128,512]{2,1,0:T(8,128)(2,1)}, bf16[2,128,512]{2,1,0:T(8,128)(2,1)}, u32[]{:S(2)}, u32[]{:S(2)}) collective-permute-start(bf16[2,128,512]{2,1,0:T(8,128)(2,1)} %get-tuple-element.44), channel_id=1, source_target_pairs={{0,3},{1,2},{2,1},{3,0},{4,7},{5,6},{6,5},{7,4},{8,11},{9,10},{10,... | collective-permute-start | bytes 786440 | tf_op jit(solution)/shard_map/ppermute | solution.py:55
  30.5 29.1 %collective-permute-start.2 = (bf16[2,128,512]{2,1,0:T(8,128)(2,1)}, bf16[2,128,512]{2,1,0:T(8,128)(2,1)}, u32[]{:S(2)}, u32[]{:S(2)}) collective-permute-start(bf16[2,128,512]{2,1,0:T(8,128)(2,1)} %get-tuple-element.39), channel_id=1, source_target_pairs={{0,6},{1,7},{2,4},{3,5},{4,2},{5,3},{6,0},{7,1},{8,14},{9,15},{10,... | collective-permute-start | bytes 786440 | tf_op jit(solution)/shard_map/ppermute | solution.py:55
  39.1 20.5 %collective-permute-start.3 = (bf16[2,128,512]{2,1,0:T(8,128)(2,1)}, bf16[2,128,512]{2,1,0:T(8,128)(2,1)}, u32[]{:S(2)}, u32[]{:S(2)}) collective-permute-start(bf16[2,128,512]{2,1,0:T(8,128)(2,1)} %get-tuple-element.41), channel_id=1, source_target_pairs={{0,7},{1,6},{2,5},{3,4},{4,3},{5,2},{6,1},{7,0},{8,15},{9,14},{10,... | collective-permute-start | bytes 786440 | tf_op jit(solution)/shard_map/ppermute | solution.py:55
  69.0 11.3 %collective-permute-start.9 = (f32[2,2,4,16,512]{4,3,2,1,0:T(8,128)}, f32[2,2,4,16,512]{4,3,2,1,0:T(8,128)}, u32[]{:S(2)}, u32[]{:S(2)}) collective-permute-start(f32[2,2,4,16,512]{4,3,2,1,0:T(8,128)} %dynamic-slice_bitcast_fusion.1), channel_id=1, source_target_pairs={{0,8},{8,0},{16,24},{24,16},{1,9},{9,1},{17,25},{25,17},{2,10},{10... | collective-permute-start | bytes 1572872 | tf_op jit(solution)/shard_map/ppermute | solution.py:339
  81.7 9.2 %collective-permute-start.10 = (f32[2,4,16,512]{3,2,1,0:T(8,128)S(1)}, f32[2,4,16,512]{3,2,1,0:T(8,128)S(1)}, u32[]{:S(2)}, u32[]{:S(2)}) collective-permute-start(f32[2,4,16,512]{3,2,1,0:T(8,128)S(1)} %dynamic-slice_bitcast_fusion.3), channel_id=1, source_target_pairs={{0,16},{8,24},{16,0},{24,8},{1,17},{9,25},{17,1},{25,9},{2,18},{10... | collective-permute-start | bytes 786440 | tf_op jit(solution)/shard_map/ppermute | solution.py:339
  83.4 12.4 %collective-permute-start.13 = (f32[2,4,16,512]{3,2,1,0:T(8,128)S(1)}, f32[2,4,16,512]{3,2,1,0:T(8,128)S(1)}, u32[]{:S(2)}, u32[]{:S(2)}) collective-permute-start(f32[2,4,16,512]{3,2,1,0:T(8,128)S(1)} %dynamic-slice_bitcast_fusion.2), channel_id=1, source_target_pairs={{0,16},{8,24},{16,0},{24,8},{1,17},{9,25},{17,1},{25,9},{2,18},{10... | collective-permute-start | bytes 786440 | tf_op jit(solution)/shard_map/ppermute | solution.py:339
  91.0 5.8 %collective-permute-start.11 = (f32[4,16,512]{2,1,0:T(8,128)S(1)}, f32[4,16,512]{2,1,0:T(8,128)S(1)}, u32[]{:S(2)}, u32[]{:S(2)}) collective-permute-start(f32[4,16,512]{2,1,0:T(8,128)S(1)} %dynamic-slice_bitcast_fusion.5), channel_id=1, source_target_pairs={{0,1},{1,0},{2,3},{3,2},{4,5},{5,4},{6,7},{7,6},{8,9},{9,8},{10,11... | collective-permute-start | bytes 393224 | tf_op jit(solution)/shard_map/ppermute | solution.py:339
  103.3 5.3 %collective-permute-start.16 = (f32[32,512]{1,0:T(8,128)S(1)}, f32[32,512]{1,0:T(8,128)S(1)}, u32[]{:S(2)}, u32[]{:S(2)}) collective-permute-start(f32[32,512]{1,0:T(8,128)S(1)} %get-tuple-element.73), channel_id=1, source_target_pairs={{0,4},{1,5},{2,6},{3,7},{4,0},{5,1},{6,2},{7,3},{8,12},{9,13},{10,... | collective-permute-start | bytes 196616 | tf_op jit(solution)/shard_map/ppermute | solution.py:339
  103.3 6.1 %collective-permute-start.15 = (f32[32,512]{1,0:T(8,128)S(1)}, f32[32,512]{1,0:T(8,128)S(1)}, u32[]{:S(2)}, u32[]{:S(2)}) collective-permute-start(f32[32,512]{1,0:T(8,128)S(1)} %get-tuple-element.72), channel_id=1, source_target_pairs={{0,2},{1,3},{2,4},{3,5},{4,6},{5,7},{6,0},{7,1},{8,10},{9,11},{10,... | collective-permute-start | bytes 196616 | tf_op jit(solution)/shard_map/ppermute | solution.py:339
  110.9 5.2 %collective-permute-start.19 = (bf16[32,512]{1,0:T(8,128)(2,1)S(1)}, bf16[32,512]{1,0:T(8,128)(2,1)S(1)}, u32[]{:S(2)}, u32[]{:S(2)}) collective-permute-start(bf16[32,512]{1,0:T(8,128)(2,1)S(1)} %fusion.7), channel_id=1, source_target_pairs={{0,4},{1,5},{2,6},{3,7},{4,0},{5,1},{6,2},{7,3},{8,12},{9,13},{10,... | collective-permute-start | bytes 98312 | tf_op jit(solution)/shard_map/ppermute | solution.py:349
  110.9 5.7 %collective-permute-start.18 = (bf16[32,512]{1,0:T(8,128)(2,1)S(1)}, bf16[32,512]{1,0:T(8,128)(2,1)S(1)}, u32[]{:S(2)}, u32[]{:S(2)}) collective-permute-start(bf16[32,512]{1,0:T(8,128)(2,1)S(1)} %fusion.7), channel_id=1, source_target_pairs={{0,2},{1,3},{2,4},{3,5},{4,6},{5,7},{6,0},{7,1},{8,10},{9,11},{10,... | collective-permute-start | bytes 98312 | tf_op jit(solution)/shard_map/ppermute | solution.py:349
  121.7 7.3 %collective-permute-start.27 = (bf16[2,4,32,512]{3,2,1,0:T(8,128)(2,1)S(1)}, bf16[2,4,32,512]{3,2,1,0:T(8,128)(2,1)S(1)}, u32[]{:S(2)}, u32[]{:S(2)}) collective-permute-start(bf16[2,4,32,512]{3,2,1,0:T(8,128)(2,1)S(1)} %get-tuple-element.71), channel_id=1, source_target_pairs={{0,16},{8,24},{16,0},{24,8},{1,17},{9,25},{17,1},{25,9},{2,18},{10... | collective-permute-start | bytes 786440 | tf_op jit(solution)/shard_map/ppermute | solution.py:349
  124.1 25.9 %collective-permute-start.7 = (bf16[2,128,512]{2,1,0:T(8,128)(2,1)S(1)}, bf16[2,128,512]{2,1,0:T(8,128)(2,1)S(1)}, u32[]{:S(2)}, u32[]{:S(2)}) collective-permute-start(bf16[2,128,512]{2,1,0:T(8,128)(2,1)S(1)} %get-tuple-element.51), channel_id=1, source_target_pairs={{0,4},{1,5},{2,6},{3,7},{4,0},{5,1},{6,2},{7,3},{8,12},{9,13},{10,... | collective-permute-start | bytes 786440 | tf_op jit(solution)/shard_map/ppermute | solution.py:55
  125.3 30.4 %collective-permute-start.8 = (bf16[2,128,512]{2,1,0:T(8,128)(2,1)S(1)}, bf16[2,128,512]{2,1,0:T(8,128)(2,1)S(1)}, u32[]{:S(2)}, u32[]{:S(2)}) collective-permute-start(bf16[2,128,512]{2,1,0:T(8,128)(2,1)S(1)} %get-tuple-element.53), channel_id=1, source_target_pairs={{0,5},{1,4},{2,7},{3,6},{4,1},{5,0},{6,3},{7,2},{8,13},{9,12},{10,... | collective-permute-start | bytes 786440 | tf_op jit(solution)/shard_map/ppermute | solution.py:55
  127.3 28.3 %collective-permute-start.21 = (bf16[2,128,512]{2,1,0:T(8,128)(2,1)S(1)}, bf16[2,128,512]{2,1,0:T(8,128)(2,1)S(1)}, u32[]{:S(2)}, u32[]{:S(2)}) collective-permute-start(bf16[2,128,512]{2,1,0:T(8,128)(2,1)S(1)} %get-tuple-element.57), channel_id=1, source_target_pairs={{0,6},{1,7},{2,4},{3,5},{4,2},{5,3},{6,0},{7,1},{8,14},{9,15},{10,... | collective-permute-start | bytes 786440 | tf_op jit(solution)/shard_map/ppermute | solution.py:55
  129.1 47.5 %collective-permute-start.28 = (bf16[2,2,4,32,512]{4,3,2,1,0:T(8,128)(2,1)S(1)}, bf16[2,2,4,32,512]{4,3,2,1,0:T(8,128)(2,1)S(1)}, u32[]{:S(2)}, u32[]{:S(2)}) collective-permute-start(bf16[2,2,4,32,512]{4,3,2,1,0:T(8,128)(2,1)S(1)} %get-tuple-element.69), channel_id=1, source_target_pairs={{0,8},{8,0},{16,24},{24,16},{1,9},{9,1},{17,25},{25,17},{2,10},{10... | collective-permute-start | bytes 1572872 | tf_op jit(solution)/shard_map/ppermute | solution.py:349
  129.2 40.1 %collective-permute-start.22 = (bf16[2,128,512]{2,1,0:T(8,128)(2,1)S(1)}, bf16[2,128,512]{2,1,0:T(8,128)(2,1)S(1)}, u32[]{:S(2)}, u32[]{:S(2)}) collective-permute-start(bf16[2,128,512]{2,1,0:T(8,128)(2,1)S(1)} %get-tuple-element.59), channel_id=1, source_target_pairs={{0,7},{1,6},{2,5},{3,4},{4,3},{5,2},{6,1},{7,0},{8,15},{9,14},{10,... | collective-permute-start | bytes 786440 | tf_op jit(solution)/shard_map/ppermute | solution.py:55
  150.0 19.3 %collective-permute-start.23 = (bf16[2,128,512]{2,1,0:T(8,128)(2,1)S(1)}, bf16[2,128,512]{2,1,0:T(8,128)(2,1)S(1)}, u32[]{:S(2)}, u32[]{:S(2)}) collective-permute-start(bf16[2,128,512]{2,1,0:T(8,128)(2,1)S(1)} %get-tuple-element.61), channel_id=1, source_target_pairs={{0,1},{1,0},{2,3},{3,2},{4,5},{5,4},{6,7},{7,6},{8,9},{9,8},{10,11... | collective-permute-start | bytes 786440 | tf_op jit(solution)/shard_map/ppermute | solution.py:55
  155.7 13.6 %collective-permute-start.24 = (bf16[2,128,512]{2,1,0:T(8,128)(2,1)S(1)}, bf16[2,128,512]{2,1,0:T(8,128)(2,1)S(1)}, u32[]{:S(2)}, u32[]{:S(2)}) collective-permute-start(bf16[2,128,512]{2,1,0:T(8,128)(2,1)S(1)} %get-tuple-element.63), channel_id=1, source_target_pairs={{0,2},{1,3},{2,0},{3,1},{4,6},{5,7},{6,4},{7,5},{8,10},{9,11},{10,... | collective-permute-start | bytes 786440 | tf_op jit(solution)/shard_map/ppermute | solution.py:55
  155.7 14.7 %collective-permute-start.25 = (bf16[2,128,512]{2,1,0:T(8,128)(2,1)S(1)}, bf16[2,128,512]{2,1,0:T(8,128)(2,1)S(1)}, u32[]{:S(2)}, u32[]{:S(2)}) collective-permute-start(bf16[2,128,512]{2,1,0:T(8,128)(2,1)S(1)} %get-tuple-element.65), channel_id=1, source_target_pairs={{0,3},{1,2},{2,1},{3,0},{4,7},{5,6},{6,5},{7,4},{8,11},{9,10},{10,... | collective-permute-start | bytes 786440 | tf_op jit(solution)/shard_map/ppermute | solution.py:55
  (36 other events, 413.7 us)

commit v2 on v0

v2 whole, which is shorter than its diff:
```python
import math

import jax
import jax.numpy as jnp
from jax import lax
from jax.experimental import pallas as pl
from jax.experimental.pallas import tpu as pltpu
from jax.sharding import PartitionSpec as P

F32 = jnp.float32
BF16 = jnp.bfloat16
ANY = pl.BlockSpec(memory_space=pl.ANY)
VMEM = pl.BlockSpec(memory_space=pltpu.VMEM)
SMEM = pl.BlockSpec(memory_space=pltpu.SMEM)
MIB = 1 << 20


def params(mib=16):
    return pltpu.CompilerParams(vmem_limit_bytes=mib * MIB)


def cost(flops, moved):
    return pl.CostEstimate(flops=int(flops), bytes_accessed=int(moved), transcendentals=0)


def mm(a, b):
    return lax.dot_general(a, b, (((1,), (0,)), ((), ())), preferred_element_type=F32)


def mm_tn(a, b):
    return lax.dot_general(a, b, (((0,), (0,)), ((), ())), preferred_element_type=F32)


def mm_nt(a, b):
    return lax.dot_general(a, b, (((1,), (1,)), ((), ())), preferred_element_type=F32)


def far_memory(*arrays):
    return [x if x.dtype == jnp.int32 else pltpu.with_memory_space_constraint(x, pltpu.HBM) for x in arrays]


def flat_rows(x):
    return x.reshape(-1, x.shape[-1])


def after(x, *others):
    return lax.optimization_barrier((x,) + others)[0]


def row_chunk(rows, most):
    return max(c for c in range(8, most + 1, 8) if rows % c == 0)


def target_of(index, shift, n):
    return index ^ shift if n & (n - 1) == 0 else (index + shift) % n


def source_of(index, shift, n):
    return index ^ shift if n & (n - 1) == 0 else (index + n - shift) % n


def exchange(block, shift, n):
    return lax.ppermute(block, "asset", [(i, target_of(i, shift, n)) for i in range(n)])


def send_forward(me, features, tiles, cols, live, shifts, n):
    steps, _, width = features.shape
    tile = tiles.shape[1]
    count = len(shifts)

    def body(me_ref, cols_ref, live_ref, tiles_ref, f_ref, *rest):
        outs, (weights, blocks, made, tile_sem, block_sem, made_sem) = rest[:count], rest[count:]
        loads = []
        for j, shift in enumerate(shifts):
            to = target_of(me_ref[0], shift, n)
            start = pl.multiple_of(cols_ref[to] * tile, tile)
            load = (
                pltpu.make_async_copy(tiles_ref.at[to], weights.at[j], tile_sem.at[j]),
                pltpu.make_async_copy(f_ref.at[:, pl.ds(start, tile), :], blocks.at[j], block_sem.at[j]),
            )
            for copy in load:
                copy.start()
            loads.append(load)
        stores = []
        for j, shift in enumerate(shifts):
            to = target_of(me_ref[0], shift, n)
            for copy in loads[j]:
                copy.wait()
            used = weights[j] * live_ref[to].astype(F32).astype(BF16)
            for t in range(steps):
                made[j, t] = mm(used, blocks[j, t]).astype(BF16)
            store = pltpu.make_async_copy(made.at[j], outs[j], made_sem.at[j])
            store.start()
            stores.append(store)
        for store in stores:
            store.wait()

    block = pltpu.HBM((steps, tile, width), BF16)
    size = steps * tile * width
    many = pltpu.VMEM((count, steps, tile, width), BF16)
    sems = pltpu.SemaphoreType.DMA((count,))
    return pl.pallas_call(
        body,
        out_shape=[block] * count,
        in_specs=[SMEM, SMEM, SMEM, ANY, ANY],
        out_specs=[ANY] * count,
        scratch_shapes=[pltpu.VMEM((count, tile, tile), BF16), many, many, sems, sems, sems],
        compiler_params=params(),
        cost_estimate=cost(2 * count * size * tile, 4 * count * size),
        name="send_forward",
    )(*far_memory(me, cols, live, tiles, features))


def send_backward(back, rows, tile):
    steps, _, width = back.shape
    n = rows.shape[0]

    def body(rows_ref, r_ref, *rest):
        outs, (held, load_sem, store_sem) = rest[:steps], rest[steps:]
        loads = []
        for s in range(n):
            at = pl.ds(pl.multiple_of(rows_ref[s] * tile, tile), tile)
            load = pltpu.make_async_copy(r_ref.at[:, at, :], held.at[:, s], load_sem.at[s])
            load.start()
            loads.append(load)
        for load in loads:
            load.wait()
        stores = [pltpu.make_async_copy(held.at[t], outs[t], store_sem.at[t]) for t in range(steps)]
        for store in stores:
            store.start()
        for store in stores:
            store.wait()

    return pl.pallas_call(
        body,
        out_shape=[pltpu.HBM((n, tile, width), BF16)] * steps,
        in_specs=[SMEM, ANY],
        out_specs=[ANY] * steps,
        scratch_shapes=[
            pltpu.VMEM((steps, n, tile, width), BF16),
            pltpu.SemaphoreType.DMA((n,)),
            pltpu.SemaphoreType.DMA((steps,)),
        ],
        compiler_params=params(),
        cost_estimate=cost(0, 0),
        name="send_backward",
    )(*far_memory(rows, back))


def project(flat, grad, w_value, w_gate):
    rows, width = flat.shape
    chunk = row_chunk(rows, 512)

    def body(f_ref, c_ref, wv_ref, wg_ref, back_ref):
        gate = jax.nn.sigmoid(mm(f_ref[...], wg_ref[...]))
        dagg = (c_ref[...].astype(F32) * gate).astype(BF16)
        back_ref[...] = mm_nt(dagg, wv_ref[...]).astype(BF16)

    line = pl.BlockSpec((chunk, width), lambda i: (i, 0))
    whole = pl.BlockSpec((width, width), lambda i: (0, 0))
    return pl.pallas_call(
        body,
        grid=(rows // chunk,),
        out_shape=pltpu.HBM((rows, width), BF16),
        in_specs=[line, line, whole, whole],
        out_specs=line,
        compiler_params=params(),
        cost_estimate=cost(0, 0),
        name="project",
    )(*far_memory(flat, grad, w_value, w_gate))


def place_tiles(dense, tiles_ref, count, rows_ref, cols_ref, turned):
    tile = tiles_ref.shape[1]
    dense[...] = jnp.zeros(dense.shape, BF16)

    @pl.loop(0, count)
    def _(l):
        row, col = (cols_ref[l], rows_ref[l]) if turned else (rows_ref[l], cols_ref[l])
        to = (pl.ds(pl.multiple_of(row * tile, tile), tile), pl.ds(pl.multiple_of(col * tile, tile), tile))
        new = tiles_ref[l].astype(F32)
        dense[to] = (dense[to].astype(F32) + (new.T if turned else new)).astype(BF16)


def gate_terms(f, c, g, wv, wg):
    gate = jax.nn.sigmoid(mm(f, wg))
    kept = gate * mm(g, wv)
    c = c.astype(F32)
    return kept, (c * gate).astype(BF16), (c * kept * (1.0 - gate)).astype(BF16)


def local_terms(step, sums, count, rows, cols, tiles, features, grad, back, w_value, w_gate):
    _, assets, width = features.shape
    _, tile, _ = tiles.shape
    chunk = row_chunk(assets, 2 * tile)

    def body(count_ref, rows_ref, cols_ref, tiles_ref, f_ref, r_ref, c_ref, wv_ref, wg_ref, *rest):
        o_ref, base_ref, sums_ref, dense, turned = rest[-5:]
        i = pl.program_id(0)

        @pl.when(i == 0)
        def _():
            place_tiles(dense, tiles_ref, count_ref[0], rows_ref, cols_ref, False)
            place_tiles(turned, tiles_ref, count_ref[0], rows_ref, cols_ref, True)
            sums_ref[...] = jnp.zeros(sums_ref.shape, F32) if sums is None else rest[0][...]

        at = pl.ds(pl.multiple_of(i * chunk, chunk), chunk)
        g = mm(dense[at, :], f_ref[0]).astype(BF16)
        f = f_ref[0, at, :]
        kept, dagg, dgate = gate_terms(f, c_ref[0], g, wv_ref[...], wg_ref[...])
        o_ref[...] = f.astype(F32) + kept
        base_ref[...] = c_ref[0].astype(F32) + mm(turned[at, :], r_ref[0]) + mm_nt(dgate, wg_ref[...])
        sums_ref[0] += mm_tn(g, dagg)
        sums_ref[1] += mm_tn(f, dgate)

    line = pl.BlockSpec((chunk, width), lambda i: (i, 0))
    slab = pl.BlockSpec((1, assets, width), lambda i: (step, 0, 0))
    weight = pl.BlockSpec((width, width), lambda i: (0, 0))
    whole = pl.BlockSpec((2, width, width), lambda i: (0, 0, 0))
    old = [] if sums is None else [sums]
    return pl.pallas_call(
        body,
        grid=(assets // chunk,),
        out_shape=[pltpu.HBM((assets, width), F32)] * 2 + [pltpu.HBM((2, width, width), F32)],
        in_specs=[SMEM, SMEM, SMEM, pl.BlockSpec(tiles.shape, lambda i: (0, 0, 0)), slab, slab]
        + [pl.BlockSpec((1, chunk, width), lambda i: (step, i, 0)), weight, weight]
        + [whole] * len(old),
        out_specs=[line, line, whole],
        scratch_shapes=[pltpu.VMEM((assets, assets), BF16)] * 2,
        compiler_params=params(56),
        cost_estimate=cost(0, 0),
        name="local_terms",
    )(*far_memory(count, rows, cols, tiles, features, back, grad, w_value, w_gate, *old))


def add_arrived(me, sums, arrived, rows, features, grad, w_value, w_gate, shifts, n, tile):
    steps, _, width = features.shape
    count = len(shifts)

    def body(me_ref, rows_ref, s_ref, f_ref, c_ref, wv_ref, wg_ref, *rest):
        parts, (sums_ref, made_ref) = rest[:count], rest[count : count + 2]
        p_buf, f_buf, c_buf, w_buf, s_buf, made, sem, w_sem, made_sem = rest[count + 2 :]
        loads = [pltpu.make_async_copy(ref, w_buf.at[i], w_sem.at[i]) for i, ref in enumerate((wv_ref, wg_ref))]
        for j, shift in enumerate(shifts):
            row = rows_ref[source_of(me_ref[0], shift, n)]
            at = pl.ds(pl.multiple_of(row * tile, tile), tile)
            for i, (ref, buf) in enumerate(((f_ref.at[:, at, :], f_buf), (c_ref.at[:, at, :], c_buf), (parts[j], p_buf))):
                loads.append(pltpu.make_async_copy(ref, buf.at[j], sem.at[i, j]))
        old = pltpu.make_async_copy(s_ref, s_buf, w_sem.at[2])
        for load in loads:
            load.start()
        old.start()
        loads[0].wait()
        loads[1].wait()
        stores = []
        for j in range(count):
            for load in loads[2 + 3 * j : 5 + 3 * j]:
                load.wait()
            p, f, c = [flat_rows(buf[j]) for buf in (p_buf, f_buf, c_buf)]
            kept, dagg, dgate = gate_terms(f, c, p, w_buf[0], w_buf[1])
            made[j, 0] = kept.astype(BF16).reshape(steps, tile, width)
            made[j, 1] = dgate.reshape(steps, tile, width)
            store = pltpu.make_async_copy(made.at[j], made_ref.at[j], made_sem.at[j])
            store.start()
            stores.append(store)
            if j == 0:
                sums_ref[0] = mm_tn(p, dagg)
                sums_ref[1] = mm_tn(f, dgate)
            else:
                sums_ref[0] += mm_tn(p, dagg)
                sums_ref[1] += mm_tn(f, dgate)
        old.wait()
        sums_ref[...] += s_buf[...]
        for store in stores:
            store.wait()

    many = pltpu.VMEM((count, steps, tile, width), BF16)
    pair = (count, 2, steps, tile, width)
    return pl.pallas_call(
        body,
        out_shape=[pltpu.HBM(sums.shape, F32), pltpu.HBM(pair, BF16)],
        in_specs=[SMEM, SMEM] + [ANY] * (5 + count),
        out_specs=[VMEM, ANY],
        scratch_shapes=[
            many,
            many,
            many,
            pltpu.VMEM((2, width, width), BF16),
            pltpu.VMEM(sums.shape, F32),
            pltpu.VMEM(pair, BF16),
            pltpu.SemaphoreType.DMA((3, count)),
            pltpu.SemaphoreType.DMA((3,)),
            pltpu.SemaphoreType.DMA((count,)),
        ],
        compiler_params=params(48),
        cost_estimate=cost(0, 0),
        name="add_arrived",
    )(*far_memory(me, rows, sums, features, grad, w_value, w_gate, *arrived))


def settle(me, local, made, rows, groups, n, tile):
    steps = len(local)
    assets, width = local[0].shape
    blocks = assets // tile

    def body(me_ref, rows_ref, *rest):
        parts, (out_ref, acc) = rest[steps:-2], rest[-2:]
        b = pl.program_id(0)
        for t in range(steps):
            acc[t] = rest[t][...]
        for part, shifts in zip(parts, groups):
            for j, shift in enumerate(shifts):

                @pl.when(rows_ref[source_of(me_ref[0], shift, n)] == b)
                def _():
                    acc[...] += part[j, 0].astype(F32)

        out_ref[...] = acc[...].astype(BF16)

    line = pl.BlockSpec((tile, width), lambda b: (b, 0))
    pieces = [pl.BlockSpec((x.shape[0], 1) + x.shape[2:], lambda b: (0,) * 5) for x in made]
    return pl.pallas_call(
        body,
        grid=(blocks,),
        out_shape=pltpu.HBM((steps, assets, width), BF16),
        in_specs=[SMEM, SMEM] + [line] * steps + pieces,
        out_specs=pl.BlockSpec((steps, tile, width), lambda b: (0, b, 0)),
        scratch_shapes=[pltpu.VMEM((steps, tile, width), F32)],
        compiler_params=params(32),
        cost_estimate=cost(0, 0),
        name="settle",
    )(*far_memory(me, rows, *local, *made))


def finish(step, steps, grads, me, base, made, rows, groups, returned, cols, live, tiles, w_gate, n):
    assets, width = base.shape
    tile = tiles.shape[1]
    blocks = assets // tile
    sets = len(made)

    def body(me_ref, rows_ref, cols_ref, live_ref, tiles_ref, w_ref, r_ref, b_ref, *rest):
        dgates, (out_ref, acc) = rest[:sets], rest[-2:]
        b = pl.program_id(0)
        acc[...] = b_ref[...]
        for part, group in zip(dgates, groups):
            for j, shift in enumerate(group):

                @pl.when(rows_ref[source_of(me_ref[0], shift, n)] == b)
                def _():
                    acc[...] += mm_nt(part[j, 0, 0], w_ref[...])

        for of in range(n):

            @pl.when((cols_ref[of] == b) & (live_ref[of] != 0))
            def _():
                acc[...] += mm_tn(tiles_ref[of], r_ref[of])

        out_ref[0] = acc[...].astype(BF16)

    line = pl.BlockSpec((tile, width), lambda b: (b, 0))
    pieces = [pl.BlockSpec((x.shape[0], 1, 1) + x.shape[3:], lambda b: (0, 1, step, 0, 0)) for x in made]
    every = [pl.BlockSpec(x.shape, lambda b: (0, 0, 0)) for x in (tiles, returned)]
    weight = pl.BlockSpec((width, width), lambda b: (0, 0))
    old = [] if grads is None else [grads]
    return pl.pallas_call(
        body,
        grid=(blocks,),
        out_shape=pltpu.HBM((steps, assets, width), BF16),
        in_specs=[SMEM, SMEM, SMEM, SMEM, every[0], weight, every[1], line] + pieces + [ANY] * len(old),
        out_specs=pl.BlockSpec((1, tile, width), lambda b: (step, b, 0)),
        scratch_shapes=[pltpu.VMEM((tile, width), F32)],
        input_output_aliases={8 + sets: 0} if old else {},
        compiler_params=params(32),
        cost_estimate=cost(0, 0),
        name="finish",
    )(*far_memory(me, rows, cols, live, tiles, w_gate, returned, base, *made, *old))


def levels(tm, asset):
    low = max(d for d in range(1, math.isqrt(asset) + 1) if asset % d == 0)
    pair = 2 if tm % 2 == 0 else 1
    return [("tm", 1, pair, tm), ("tm", pair, tm // pair, tm), ("asset", 1, low, asset), ("asset", low, asset // low, asset)]


def member(level):
    axis, stride, size, _ = level
    return (lax.axis_index(axis) // stride) % size


def pairs_of(level, shift):
    _, stride, size, n = level
    return [(i, i + ((i // stride + shift) % size - (i // stride) % size) * stride) for i in range(n)]


def scatter_sum(x, level, wire):
    axis, _, size, _ = level
    me = member(level)
    total = lax.dynamic_index_in_dim(x, me, 0, keepdims=False)
    arrived = [
        lax.ppermute(lax.dynamic_index_in_dim(x, (me + s) % size, 0, keepdims=False).astype(wire), axis, pairs_of(level, s))
        for s in range(1, size)
    ]
    for part in arrived:
        total = total + part.astype(F32)
    return total


def spread(x, level):
    axis, _, size, _ = level
    return jnp.stack([x] + [lax.ppermute(x, axis, pairs_of(level, s)) for s in range(1, size)])


def unshuffle(x, order, shape):
    sizes = [level[2] for level in order]
    place = jnp.arange(math.prod(sizes), dtype=jnp.int32)
    index, stride = 0, 1
    for level in reversed(order):
        size = level[2]
        index = index + ((member(level) - place // stride) % size) * stride
        stride *= size
    flat = x.reshape(math.prod(sizes), -1, shape[-1])
    return jnp.take(flat, index, axis=0, mode="clip").reshape(shape).astype(F32)


def per_device(
    features,
    w_value,
    w_gate,
    cotangent,
    local_rows,
    local_cols,
    local_count,
    local_tiles,
    remote_rows,
    remote_cols,
    remote_live,
    remote_tiles,
):
    steps, assets, width = features.shape
    tile = local_tiles.shape[1]
    n = lax.axis_size("asset")
    tm = lax.axis_size("tm")
    me = lax.axis_index("asset").astype(jnp.int32).reshape(1)
    flat = features.reshape(-1, width)
    grad = cotangent.reshape(-1, width)

    far = list(range(n // 2, n))
    near = list(range(1, n // 2))
    shifts = far + near
    half = len(far) // 2
    first, second = far[:half] + near[:1], far[half:] + near[1:]
    late = far[half:]
    early = [s for s in shifts if s not in late]
    weights = (w_value, w_gate)
    graph = (local_count, local_rows, local_cols, local_tiles)

    sent = dict(zip(shifts, send_forward(me, features, remote_tiles, remote_cols, remote_live, shifts, n)))
    came = {s: exchange(sent[s], s, n) for s in first}
    back = project(flat, grad, *weights).reshape(features.shape)
    out, base = [None] * steps, [None] * steps
    out[0], base[0], sums = local_terms(0, None, *graph, features, cotangent, back, *weights)
    for s in second:
        came[s] = exchange(after(sent[s], sums, *[came[i] for i in first]), s, n)
    rest = [after(x, *[came[i] for i in first]) for x in (features, cotangent)]
    for t in range(1, steps):
        out[t], base[t], sums = local_terms(t, sums, *graph, *rest, back, *weights)
    owed = send_backward(back, remote_rows, tile)
    sums, made_early = add_arrived(
        me, sums, [came[s] for s in early], remote_rows, *rest, *weights, early, n, tile
    )
    sums, made_late = add_arrived(
        me, after(sums, *owed), [came[s] for s in late], remote_rows, *rest, *weights, late, n, tile
    )
    made, groups = (made_early, made_late), (early, late)

    order = levels(tm, n)
    sizes = [level[2] for level in order]
    rows = 2 * width // math.prod(sizes)

    def send_back(t, *before):
        return lax.all_to_all(after(owed[t], *before), "asset", 0, 0, tiled=True)

    returned = [send_back(t, *[came[s] for s in late]) for t in range(steps // 2)]
    output = settle(me, out, made, remote_rows, groups, n, tile)
    sums = scatter_sum(sums.reshape(sizes + [rows, width]), order[0], F32)
    sums = scatter_sum(sums, order[1], BF16)
    sums = after(scatter_sum(sums, order[2], BF16), output, *returned)
    sums = scatter_sum(sums, order[3], BF16).astype(BF16)
    sums = spread(sums, order[3])
    returned += [send_back(t, sums) for t in range(steps // 2, steps)]

    grad_features = None

    def finish_step(t):
        return finish(
            t, steps, grad_features, me, base[t], made, remote_rows, groups, returned[t], remote_cols, remote_live,
            remote_tiles, w_gate, n
        )

    for t in range(steps // 2):
        grad_features = finish_step(t)
    sums = spread(sums, order[2])
    sums = spread(sums, order[1])
    if grad_features is not None:
        sums = after(sums, grad_features)
    sums = spread(sums, order[0])
    scale = float(steps * assets * tm * n) ** (-0.5)
    sums = unshuffle(sums, order, (2, width, width)) * scale
    for t in range(steps // 2, steps):
        grad_features = finish_step(t)
    return output, grad_features, sums[0], sums[1]


def solution(mesh):
    return jax.shard_map(
        per_device,
        mesh=mesh,
        in_specs=(
            P("tm", "asset", None),
            P(),
            P(),
            P("tm", "asset", None),
            P("asset"),
            P("asset"),
            P("asset"),
            P("asset", None, None),
            P("asset"),
            P("asset"),
            P("asset"),
            P("asset", None, None),
        ),
        out_specs=(P("tm", "asset", None), P("tm", "asset", None), P(), P()),
        check_vma=False,
    )
```

time: 315 us -> 166 us (0.53)
  waiting for transfers between devices: 166 us -> 30 us
  Pallas kernels: 0 us -> 88.2 us
  matrix products: 65.1 us -> 0 us
  local copies, waits for them, and re-layouts: 48 us -> 8.01 us
  starting transfers between devices: 11.8 us -> 35.2 us
  between operations: 14.9 us -> 1.65 us
  other arithmetic: 8.1 us -> 2.12 us
    psum x1 -> x0, waiting for transfers between devices: 127 us -> none  [per_device(): lax.psum((partial_value, partial_gate), ('tm', 'asset'))]
    pallas_call x0 -> x10, Pallas kernels: none -> 88.2 us  [the longest x2 30.2 us: local_terms(): pl.pallas_call(body, grid=(assets // chunk,), out_shape=[pltpu.HBM((asset...]
    dot_general x14 -> x0, matrix products: 65.1 us -> none  [the longest x1 7.47 us: per_device(): jnp.einsum('bl,tlid->tbid', row_select, local_terms, preferred_element_ty...]
    all_to_all x2, waiting for transfers between devices: 38.8 us -> 9.94 us  [send_back(): return lax.all_to_all(after(owed[t], *before), 'asset', 0, 0, tiled=True)]
    ppermute x0 -> x19, starting transfers between devices: none -> 26 us  [the longest x7 13.2 us: exchange(): lax.ppermute(block, 'asset', [(i, target_of(i, shift, n)) for i in range(...]
    convert_element_type x5 -> x3, local copies, waits for them, and re-layouts: 25.9 us -> 0.08 us  [scatter_sum(): lax.dynamic_index_in_dim(x, (me + s) % size, 0, keepdims=False).astype(wire)]
    ppermute x0 -> x19, waiting for transfers between devices: none -> 20 us  [the longest x6 11.7 us: scatter_sum(): lax.ppermute(lax.dynamic_index_in_dim(x, (me + s) % size, 0, keepdims=Fal...]
    gather x5 -> x1, local copies, waits for them, and re-layouts: 16.1 us -> 0.61 us  [unshuffle(): return jnp.take(flat, index, axis=0, mode='clip').reshape(shape).astype(F32)]
  transfers between devices with their start and end apart: 3 -> 21, of which waited for: 3 -> 10; matrix products, arithmetic and copies ran while one was open for 20% -> 3% of each run, Pallas kernels for 0% -> 41%
where the time goes in v2:
time: 166 us; the launch traced here: 165 us
  Pallas kernels  88.2 us (53%)
  starting transfers between devices  35.2 us (21%)
  waiting for transfers between devices  30 us (18%)
  local copies, waits for them, and re-layouts  8.01 us (5%)
  other arithmetic  2.12 us (1%)
    pallas_call x2, Pallas kernels, local_terms(): pl.pallas_call(body, grid=(assets // chunk,), out_shape=[pltpu.HBM((asset...  30.2 us
    pallas_call x2, Pallas kernels, finish(): pl.pallas_call(body, grid=(blocks,), out_shape=pltpu.HBM((steps, assets,...  20.4 us
    pallas_call x2, Pallas kernels, add_arrived(): pl.pallas_call(body, out_shape=[pltpu.HBM(sums.shape, F32), pltpu.HBM(pai...  14.4 us
    ppermute x7, starting transfers between devices, exchange(): lax.ppermute(block, 'asset', [(i, target_of(i, shift, n)) for i in range(...  13.2 us
    ppermute x6, waiting for transfers between devices, scatter_sum(): lax.ppermute(lax.dynamic_index_in_dim(x, (me + s) % size, 0, keepdims=Fal...  11.7 us
    all_to_all x2, waiting for transfers between devices, send_back(): return lax.all_to_all(after(owed[t], *before), 'asset', 0, 0, tiled=True)  9.94 us
    all_to_all x2, starting transfers between devices, send_back(): return lax.all_to_all(after(owed[t], *before), 'asset', 0, 0, tiled=True)  9.17 us
    pallas_call x1, Pallas kernels, settle(): pl.pallas_call(body, grid=(blocks,), out_shape=pltpu.HBM((steps, assets,...  8.48 us
  transfers between devices with their start and end apart: 21, of which 10 were waited for; matrix products, arithmetic and copies ran while one was open for 3% of the time, Pallas kernels for 41%

profile of v2, /device:TPU:0, one launch (start us, length us, event | category | flops | bytes accessed | tf_op | source)
XLA Modules:
  0.0 165.1 jit_solution(1754775119170802673)
XLA Ops:
  1.9 3.9 %send_forward.1 = (bf16[2,128,512]{2,1,0:T(8,128)(2,1)}, bf16[2,128,512]{2,1,0:T(8,128)(2,1)}, bf16[2,128,512]{2,1,0:T(8,128)(2,1)}, bf16[2,128,512]{2,1,0:T(8,1...) custom-call(s32[1]{0:T(128)} %bitcast.me_ref, s32[8]{0:T(128)S(1)} %copy-done.1, ...), custom_call_target="tpu_custom_call" | custom-call | flops 234881024 | bytes 3670016 | tf_op jit(solution)/shard_map/send_forward/pallas_call | solution.py:102
  5.9 4.1 %collective-permute-start = (bf16[2,128,512]{2,1,0:T(8,128)(2,1)}, bf16[2,128,512]{2,1,0:T(8,128)(2,1)S(1)}, u32[]{:S(2)}, u32[]{:S(2)}) collective-permute-start(bf16[2,128,512]{2,1,0:T(8,128)(2,1)} %get-tuple-element.35), channel_id=1, source_target_pairs={{0,4},{1,5},{2,6},{3,7},{4,0},{5,1},{6,2},{7,3},{8,12},{9,13},{10,... | collective-permute-start | bytes 786440 | tf_op jit(solution)/shard_map/ppermute | solution.py:63
  12.2 7.3 %project.1 = bf16[2560,512]{1,0:T(8,128)(2,1)} custom-call(bf16[2560,512]{1,0:T(8,128)(2,1)} %bitcast.48, bf16[2560,512]{1,0:T(8,128)(2,1)} %bitcast.49, bf16[512,512]{1,0:T(8,128)(2,1)} %wv_ref.9, bf16[512,512]{1,0:T(8,128)(2,1)} %w_ref.3), custom_call_target="tpu_custom_call" | custom-call | tf_op jit(solution)/shard_map/project/pallas_call | solution.py:161
  19.5 14.8 %local_terms.2 = (f32[1280,512]{1,0:T(8,128)}, f32[1280,512]{1,0:T(8,128)}, f32[2,512,512]{2,1,0:T(8,128)}) custom-call(s32[1]{0:T(128)S(6)} %copy.18.count_ref, s32[20]{0:T(128)} %rows_ref.9, s32[20]{0:T(128)} %cols_ref.7, bf16[20,128,128]{2,1,0:T(8,128)(2,1)} %tiles_ref.7, bf16[2,1280,512]{2,1,0:T(8,128)(2,1)} %f_ref.6, bf16[2,1280,512]{2,1,0:T(8,128)(2,1)} %bitcast.50, ...), custom_call_target="tpu_custom_call" | custom-call | tf_op jit(solution)/shard_map/local_terms/pallas_call | solution.py:221
  37.9 3.1 %collective-permute-start.5 = (bf16[2,128,512]{2,1,0:T(8,128)(2,1)S(1)}, bf16[2,128,512]{2,1,0:T(8,128)(2,1)S(1)}, u32[]{:S(2)}, u32[]{:S(2)}) collective-permute-start(bf16[2,128,512]{2,1,0:T(8,128)(2,1)S(1)} %copy-done.15), channel_id=1, source_target_pairs={{0,6},{1,7},{2,4},{3,5},{4,2},{5,3},{6,0},{7,1},{8,14},{9,15},{10,... | collective-permute-start | bytes 786440 | tf_op jit(solution)/shard_map/ppermute | solution.py:63
  41.9 3.5 %send_backward.1 = (bf16[8,128,512]{2,1,0:T(8,128)(2,1)}, bf16[8,128,512]{2,1,0:T(8,128)(2,1)}) custom-call(s32[8]{0:T(128)S(1)} %copy-done, bf16[2,1280,512]{2,1,0:T(8,128)(2,1)} %bitcast.51), custom_call_target="tpu_custom_call" | custom-call | tf_op jit(solution)/shard_map/send_backward/pallas_call | solution.py:134
  45.4 15.4 %local_terms.3 = (f32[1280,512]{1,0:T(8,128)}, f32[1280,512]{1,0:T(8,128)}, f32[2,512,512]{2,1,0:T(8,128)}) custom-call(s32[1]{0:T(128)S(6)} %copy.18.count_ref, s32[20]{0:T(128)} %rows_ref.9, s32[20]{0:T(128)} %cols_ref.7, bf16[20,128,128]{2,1,0:T(8,128)(2,1)} %tiles_ref.7, bf16[2,1280,512]{2,1,0:T(8,128)(2,1)} %f_ref.6, bf16[2,1280,512]{2,1,0:T(8,128)(2,1)} %bitcast.52, ...), custom_call_target="tpu_custom_call" | custom-call | tf_op jit(solution)/shard_map/local_terms/pallas_call | solution.py:221
  61.6 8.8 %add_arrived.2 = (f32[2,512,512]{2,1,0:T(8,128)}, bf16[5,2,2,128,512]{4,3,2,1,0:T(8,128)(2,1)}) custom-call(s32[1]{0:T(128)} %bitcast.me_ref, s32[8]{0:T(128)S(1)} %copy-done, f32[2,512,512]{2,1,0:T(8,128)} %get-tuple-element.42.s_ref, bf16[2,1280,512]{2,1,0:T(8,128)(2,1)} %f_ref.6, bf16[2,1280,512]{2,1,0:T(8,128)(2,1)} %c_ref.4, bf16[512,512]{1,0:T(8,128)(2,1)} %wv_ref.9, ...), custom_call_target="tpu_custom_call" | custom-call | tf_op jit(solution)/shard_map/add_arrived/pallas_call | solution.py:279
  71.9 5.6 %add_arrived.3 = (f32[2,512,512]{2,1,0:T(8,128)}, bf16[2,2,2,128,512]{4,3,2,1,0:T(8,128)(2,1)}) custom-call(s32[1]{0:T(128)} %bitcast.me_ref, s32[8]{0:T(128)S(1)} %copy-done, f32[2,512,512]{2,1,0:T(8,128)} %get-tuple-element.51.s_ref, bf16[2,1280,512]{2,1,0:T(8,128)(2,1)} %f_ref.6, bf16[2,1280,512]{2,1,0:T(8,128)(2,1)} %c_ref.4, bf16[512,512]{1,0:T(8,128)(2,1)} %wv_ref.9, ...), custom_call_target="tpu_custom_call" | custom-call | tf_op jit(solution)/shard_map/add_arrived/pallas_call | solution.py:279
  78.8 5.6 %all-to-all-start = ((bf16[8,128,512]{2,1,0:T(8,128)(2,1)}), bf16[8,128,512]{2,1,0:T(8,128)(2,1)S(1)}, u32[]{:S(2)}, u32[]{:S(2)}) async-start(bf16[8,128,512]{2,1,0:T(8,128)(2,1)} %get-tuple-element.58), calls=%async_computation | async-start | bytes 2097152 | tf_op jit(solution)/shard_map/all_to_all | solution.py:481
  87.6 6.9 %collective-permute-done.8 = bf16[2,4,32,512]{3,2,1,0:T(8,128)(2,1)S(1)} collective-permute-done((bf16[2,4,32,512]{3,2,1,0:T(8,128)(2,1)S(1)}, bf16[2,4,32,512]{3,2,1,0:T(8,128)(2,1)S(1)}, u32[]{:S(2)}, u32[]{:S(2)}) %collective-permute-start.8) | collective-permute-done | bytes 262176 | tf_op jit(solution)/shard_map/ppermute | solution.py:400
  94.6 1.8 %collective-permute-start.9 = (bf16[4,32,512]{2,1,0:T(8,128)(2,1)S(1)}, bf16[4,32,512]{2,1,0:T(8,128)(2,1)S(1)}, u32[]{:S(2)}, u32[]{:S(2)}) collective-permute-start(bf16[4,32,512]{2,1,0:T(8,128)(2,1)S(1)} %fusion.1), channel_id=1, source_target_pairs={{0,1},{1,0},{2,3},{3,2},{4,5},{5,4},{6,7},{7,6},{8,9},{9,8},{10,11... | collective-permute-start | bytes 393224 | tf_op jit(solution)/shard_map/ppermute | solution.py:400
  96.4 8.5 %settle.1 = bf16[2,1280,512]{2,1,0:T(8,128)(2,1)} custom-call(s32[1]{0:T(128)} %bitcast.me_ref, s32[8]{0:T(128)S(1)} %copy-done, f32[1280,512]{1,0:T(8,128)} %get-tuple-element.34.rest_0_, f32[1280,512]{1,0:T(8,128)} %get-tuple-element.41.rest_1_, bf16[5,2,2,128,512]{4,3,2,1,0:T(8,128)(2,1)} %get-tuple-element.47.rest_2_.rest_0_, ...), custom_call_target="tpu_custom_call" | custom-call | tf_op jit(solution)/shard_map/settle/pallas_call | solution.py:322
  104.9 5.9 %all-to-all-done.r_ref = bf16[8,128,512]{2,1,0:T(8,128)(2,1)S(1)} async-done(((bf16[8,128,512]{2,1,0:T(8,128)(2,1)}), bf16[8,128,512]{2,1,0:T(8,128)(2,1)S(1)}, u32[]{:S(2)}, u32[]{:S(2)}) %all-to-all-start) | async-done | bytes 1048608 | tf_op jit(solution)/shard_map/all_to_all | solution.py:481
  111.0 3.8 %collective-permute-start.12 = (bf16[32,512]{1,0:T(8,128)(2,1)S(1)}, bf16[32,512]{1,0:T(8,128)(2,1)S(1)}, u32[]{:S(2)}, u32[]{:S(2)}) collective-permute-start(bf16[32,512]{1,0:T(8,128)(2,1)S(1)} %get-tuple-element.69), channel_id=1, source_target_pairs={{0,6},{1,7},{2,0},{3,1},{4,2},{5,3},{6,4},{7,5},{8,14},{9,15},{10,... | collective-permute-start | bytes 98312 | tf_op jit(solution)/shard_map/ppermute | solution.py:400
  114.8 1.9 %collective-permute-done.10 = bf16[32,512]{1,0:T(8,128)(2,1)S(1)} collective-permute-done((bf16[32,512]{1,0:T(8,128)(2,1)S(1)}, bf16[32,512]{1,0:T(8,128)(2,1)S(1)}, u32[]{:S(2)}, u32[]{:S(2)}) %collective-permute-start.10) | collective-permute-done | bytes 32800 | tf_op jit(solution)/shard_map/ppermute | solution.py:400
  116.7 3.0 %collective-permute-done.11 = bf16[32,512]{1,0:T(8,128)(2,1)S(1)} collective-permute-done((bf16[32,512]{1,0:T(8,128)(2,1)S(1)}, bf16[32,512]{1,0:T(8,128)(2,1)S(1)}, u32[]{:S(2)}, u32[]{:S(2)}) %collective-permute-start.11) | collective-permute-done | bytes 32800 | tf_op jit(solution)/shard_map/ppermute | solution.py:400
  122.0 1.9 %collective-permute-done.15 = bf16[32,512]{1,0:T(8,128)(2,1)S(1)} collective-permute-done((bf16[32,512]{1,0:T(8,128)(2,1)S(1)}, bf16[32,512]{1,0:T(8,128)(2,1)S(1)}, u32[]{:S(2)}, u32[]{:S(2)}) %collective-permute-start.15) | collective-permute-done | bytes 32800 | tf_op jit(solution)/shard_map/ppermute | solution.py:410
  127.8 3.6 %all-to-all-start.1 = ((bf16[8,128,512]{2,1,0:T(8,128)(2,1)}), bf16[8,128,512]{2,1,0:T(8,128)(2,1)S(1)}, u32[]{:S(2)}, u32[]{:S(2)}) async-start(bf16[8,128,512]{2,1,0:T(8,128)(2,1)} %get-tuple-element.60), calls=%async_computation.1 | async-start | bytes 2097152 | tf_op jit(solution)/shard_map/all_to_all | solution.py:481
  131.4 2.1 %collective-permute-done.16 = bf16[4,32,512]{2,1,0:T(8,128)(2,1)S(1)} collective-permute-done((bf16[4,32,512]{2,1,0:T(8,128)(2,1)S(1)}, bf16[4,32,512]{2,1,0:T(8,128)(2,1)S(1)}, u32[]{:S(2)}, u32[]{:S(2)}) %collective-permute-start.16) | collective-permute-done | bytes 131104 | tf_op jit(solution)/shard_map/ppermute | solution.py:410
  135.1 10.2 %finish.2.rest_2_ = bf16[2,1280,512]{2,1,0:T(8,128)(2,1)} custom-call(s32[1]{0:T(128)} %bitcast.me_ref, s32[8]{0:T(128)S(1)} %copy-done, s32[8]{0:T(128)S(1)} %copy-done.2, s32[8]{0:T(128)S(1)} %copy-done.4, bf16[8,128,128]{2,1,0:T(8,128)(2,1)} %tiles_ref.9, bf16[512,512]{1,0:T(8,128)(2,1)} %w_ref.3, bf16[8,128,512]{2,1,0:T(8,128)(2,1)} %copy-done.5, ...), custom_call_target="tpu_custom_call" | custom-call | tf_op jit(solution)/shard_map/finish/pallas_call | solution.py:365
  145.6 1.9 %collective-permute-done.18 = bf16[2,2,4,32,512]{4,3,2,1,0:T(8,128)(2,1)S(1)} collective-permute-done((bf16[2,2,4,32,512]{4,3,2,1,0:T(8,128)(2,1)S(1)}, bf16[2,2,4,32,512]{4,3,2,1,0:T(8,128)(2,1)S(1)}, u32[]{:S(2)}, u32[]{:S(2)}) %collective-permute-start.18) | collective-permute-done | bytes 524320 | tf_op jit(solution)/shard_map/ppermute | solution.py:410
  149.9 4.0 %all-to-all-done.1.r_ref = bf16[8,128,512]{2,1,0:T(8,128)(2,1)S(1)} async-done(((bf16[8,128,512]{2,1,0:T(8,128)(2,1)}), bf16[8,128,512]{2,1,0:T(8,128)(2,1)S(1)}, u32[]{:S(2)}, u32[]{:S(2)}) %all-to-all-start.1) | async-done | bytes 1048608 | tf_op jit(solution)/shard_map/all_to_all | solution.py:481
  154.9 10.2 %finish.3 = bf16[2,1280,512]{2,1,0:T(8,128)(2,1)} custom-call(s32[1]{0:T(128)} %bitcast.me_ref, s32[8]{0:T(128)S(1)} %copy-done, s32[8]{0:T(128)S(1)} %copy-done.2, s32[8]{0:T(128)S(1)} %copy-done.4, bf16[8,128,128]{2,1,0:T(8,128)(2,1)} %tiles_ref.9, bf16[512,512]{1,0:T(8,128)(2,1)} %w_ref.3, ...), custom_call_target="tpu_custom_call", output_to_operand_aliasing={{}: (10, {})} | custom-call | tf_op jit(solution)/shard_map/finish/pallas_call | solution.py:365
  (81 shorter events, 25.7 us)
Async XLA Ops:
  5.9 28.4 %collective-permute-start = (bf16[2,128,512]{2,1,0:T(8,128)(2,1)}, bf16[2,128,512]{2,1,0:T(8,128)(2,1)S(1)}, u32[]{:S(2)}, u32[]{:S(2)}) collective-permute-start(bf16[2,128,512]{2,1,0:T(8,128)(2,1)} %get-tuple-element.35), channel_id=1, source_target_pairs={{0,4},{1,5},{2,6},{3,7},{4,0},{5,1},{6,2},{7,3},{8,12},{9,13},{10,... | collective-permute-start | bytes 786440 | tf_op jit(solution)/shard_map/ppermute | solution.py:63
  10.0 24.4 %collective-permute-start.1 = (bf16[2,128,512]{2,1,0:T(8,128)(2,1)}, bf16[2,128,512]{2,1,0:T(8,128)(2,1)S(1)}, u32[]{:S(2)}, u32[]{:S(2)}) collective-permute-start(bf16[2,128,512]{2,1,0:T(8,128)(2,1)} %get-tuple-element.36), channel_id=1, source_target_pairs={{0,5},{1,4},{2,7},{3,6},{4,1},{5,0},{6,3},{7,2},{8,13},{9,12},{10,... | collective-permute-start | bytes 786440 | tf_op jit(solution)/shard_map/ppermute | solution.py:63
  11.3 23.1 %collective-permute-start.2 = (bf16[2,128,512]{2,1,0:T(8,128)(2,1)}, bf16[2,128,512]{2,1,0:T(8,128)(2,1)S(1)}, u32[]{:S(2)}, u32[]{:S(2)}) collective-permute-start(bf16[2,128,512]{2,1,0:T(8,128)(2,1)} %get-tuple-element.37), channel_id=1, source_target_pairs={{0,1},{1,0},{2,3},{3,2},{4,5},{5,4},{6,7},{7,6},{8,9},{9,8},{10,11... | collective-permute-start | bytes 786440 | tf_op jit(solution)/shard_map/ppermute | solution.py:63
  34.3 26.5 %copy-start.7 = (bf16[2,128,512]{2,1,0:T(8,128)(2,1)}, bf16[2,128,512]{2,1,0:T(8,128)(2,1)S(1)}, u32[]{:S(2)}) copy-start(bf16[2,128,512]{2,1,0:T(8,128)(2,1)S(1)} %collective-permute-done.rest_0_) | copy-start | bytes 786436
  34.4 26.4 %collective-permute-start.3 = (bf16[2,128,512]{2,1,0:T(8,128)(2,1)S(1)}, bf16[2,128,512]{2,1,0:T(8,128)(2,1)S(1)}, u32[]{:S(2)}, u32[]{:S(2)}) collective-permute-start(bf16[2,128,512]{2,1,0:T(8,128)(2,1)S(1)} %copy-done.17), channel_id=1, source_target_pairs={{0,2},{1,3},{2,0},{3,1},{4,6},{5,7},{6,4},{7,5},{8,10},{9,11},{10,... | collective-permute-start | bytes 786440 | tf_op jit(solution)/shard_map/ppermute | solution.py:63
  36.2 24.7 %collective-permute-start.4 = (bf16[2,128,512]{2,1,0:T(8,128)(2,1)S(1)}, bf16[2,128,512]{2,1,0:T(8,128)(2,1)S(1)}, u32[]{:S(2)}, u32[]{:S(2)}) collective-permute-start(bf16[2,128,512]{2,1,0:T(8,128)(2,1)S(1)} %copy-done.16), channel_id=1, source_target_pairs={{0,3},{1,2},{2,1},{3,0},{4,7},{5,6},{6,5},{7,4},{8,11},{9,10},{10,... | collective-permute-start | bytes 786440 | tf_op jit(solution)/shard_map/ppermute | solution.py:63
  37.9 32.5 %collective-permute-start.5 = (bf16[2,128,512]{2,1,0:T(8,128)(2,1)S(1)}, bf16[2,128,512]{2,1,0:T(8,128)(2,1)S(1)}, u32[]{:S(2)}, u32[]{:S(2)}) collective-permute-start(bf16[2,128,512]{2,1,0:T(8,128)(2,1)S(1)} %copy-done.15), channel_id=1, source_target_pairs={{0,6},{1,7},{2,4},{3,5},{4,2},{5,3},{6,0},{7,1},{8,14},{9,15},{10,... | collective-permute-start | bytes 786440 | tf_op jit(solution)/shard_map/ppermute | solution.py:63
  41.0 29.4 %collective-permute-start.6 = (bf16[2,128,512]{2,1,0:T(8,128)(2,1)S(1)}, bf16[2,128,512]{2,1,0:T(8,128)(2,1)S(1)}, u32[]{:S(2)}, u32[]{:S(2)}) collective-permute-start(bf16[2,128,512]{2,1,0:T(8,128)(2,1)S(1)} %copy-done.14), channel_id=1, source_target_pairs={{0,7},{1,6},{2,5},{3,4},{4,3},{5,2},{6,1},{7,0},{8,15},{9,14},{10,... | collective-permute-start | bytes 786440 | tf_op jit(solution)/shard_map/ppermute | solution.py:63
  78.8 5.7 %collective-permute-start.7 = (f32[2,2,4,32,512]{4,3,2,1,0:T(8,128)S(1)}, f32[2,2,4,32,512]{4,3,2,1,0:T(8,128)S(1)}, u32[]{:S(2)}, u32[]{:S(2)}) collective-permute-start(f32[2,2,4,32,512]{4,3,2,1,0:T(8,128)S(1)} %dynamic-slice_bitcast_fusion), channel_id=1, source_target_pairs={{0,8},{8,0},{16,24},{24,16},{1,9},{9,1},{17,25},{25,17},{2,10},{10... | collective-permute-start | bytes 3145736 | tf_op jit(solution)/shard_map/ppermute | solution.py:400
  78.8 32.0 %all-to-all-start = ((bf16[8,128,512]{2,1,0:T(8,128)(2,1)}), bf16[8,128,512]{2,1,0:T(8,128)(2,1)S(1)}, u32[]{:S(2)}, u32[]{:S(2)}) async-start(bf16[8,128,512]{2,1,0:T(8,128)(2,1)} %get-tuple-element.58), calls=%async_computation | async-start | bytes 2097152 | tf_op jit(solution)/shard_map/all_to_all | solution.py:481
  86.0 8.5 %collective-permute-start.8 = (bf16[2,4,32,512]{3,2,1,0:T(8,128)(2,1)S(1)}, bf16[2,4,32,512]{3,2,1,0:T(8,128)(2,1)S(1)}, u32[]{:S(2)}, u32[]{:S(2)}) collective-permute-start(bf16[2,4,32,512]{3,2,1,0:T(8,128)(2,1)S(1)} %fusion), channel_id=1, source_target_pairs={{0,16},{8,24},{16,0},{24,8},{1,17},{9,25},{17,1},{25,9},{2,18},{10... | collective-permute-start | bytes 786440 | tf_op jit(solution)/shard_map/ppermute | solution.py:400
  94.6 10.3 %collective-permute-start.9 = (bf16[4,32,512]{2,1,0:T(8,128)(2,1)S(1)}, bf16[4,32,512]{2,1,0:T(8,128)(2,1)S(1)}, u32[]{:S(2)}, u32[]{:S(2)}) collective-permute-start(bf16[4,32,512]{2,1,0:T(8,128)(2,1)S(1)} %fusion.1), channel_id=1, source_target_pairs={{0,1},{1,0},{2,3},{3,2},{4,5},{5,4},{6,7},{7,6},{8,9},{9,8},{10,11... | collective-permute-start | bytes 393224 | tf_op jit(solution)/shard_map/ppermute | solution.py:400
  104.9 30.3 %copy-start.2 = (s32[8]{0:T(128)S(1)}, s32[8]{0:T(128)}, u32[]{:S(2)}) copy-start(s32[8]{0:T(128)} %cols_ref.9) | copy-start | bytes 100
  104.9 30.3 %copy-start.4 = (s32[8]{0:T(128)S(1)}, s32[8]{0:T(128)}, u32[]{:S(2)}) copy-start(s32[8]{0:T(128)} %live_ref.5) | copy-start | bytes 100
  110.9 5.8 %collective-permute-start.10 = (bf16[32,512]{1,0:T(8,128)(2,1)S(1)}, bf16[32,512]{1,0:T(8,128)(2,1)S(1)}, u32[]{:S(2)}, u32[]{:S(2)}) collective-permute-start(bf16[32,512]{1,0:T(8,128)(2,1)S(1)} %get-tuple-element.68), channel_id=1, source_target_pairs={{0,2},{1,3},{2,4},{3,5},{4,6},{5,7},{6,0},{7,1},{8,10},{9,11},{10,... | collective-permute-start | bytes 98312 | tf_op jit(solution)/shard_map/ppermute | solution.py:400
  111.0 5.7 %collective-permute-start.12 = (bf16[32,512]{1,0:T(8,128)(2,1)S(1)}, bf16[32,512]{1,0:T(8,128)(2,1)S(1)}, u32[]{:S(2)}, u32[]{:S(2)}) collective-permute-start(bf16[32,512]{1,0:T(8,128)(2,1)S(1)} %get-tuple-element.69), channel_id=1, source_target_pairs={{0,6},{1,7},{2,0},{3,1},{4,2},{5,3},{6,4},{7,5},{8,14},{9,15},{10,... | collective-permute-start | bytes 98312 | tf_op jit(solution)/shard_map/ppermute | solution.py:400
  114.8 4.8 %collective-permute-start.11 = (bf16[32,512]{1,0:T(8,128)(2,1)S(1)}, bf16[32,512]{1,0:T(8,128)(2,1)S(1)}, u32[]{:S(2)}, u32[]{:S(2)}) collective-permute-start(bf16[32,512]{1,0:T(8,128)(2,1)S(1)} %get-tuple-element.70), channel_id=1, source_target_pairs={{0,4},{1,5},{2,6},{3,7},{4,0},{5,1},{6,2},{7,3},{8,12},{9,13},{10,... | collective-permute-start | bytes 98312 | tf_op jit(solution)/shard_map/ppermute | solution.py:400
  119.7 4.3 %collective-permute-start.15 = (bf16[32,512]{1,0:T(8,128)(2,1)S(1)}, bf16[32,512]{1,0:T(8,128)(2,1)S(1)}, u32[]{:S(2)}, u32[]{:S(2)}) collective-permute-start(bf16[32,512]{1,0:T(8,128)(2,1)S(1)} %fusion.4), channel_id=1, source_target_pairs={{0,6},{1,7},{2,0},{3,1},{4,2},{5,3},{6,4},{7,5},{8,14},{9,15},{10,... | collective-permute-start | bytes 98312 | tf_op jit(solution)/shard_map/ppermute | solution.py:410
  120.6 4.8 %collective-permute-start.14 = (bf16[32,512]{1,0:T(8,128)(2,1)S(1)}, bf16[32,512]{1,0:T(8,128)(2,1)S(1)}, u32[]{:S(2)}, u32[]{:S(2)}) collective-permute-start(bf16[32,512]{1,0:T(8,128)(2,1)S(1)} %fusion.4), channel_id=1, source_target_pairs={{0,4},{1,5},{2,6},{3,7},{4,0},{5,1},{6,2},{7,3},{8,12},{9,13},{10,... | collective-permute-start | bytes 98312 | tf_op jit(solution)/shard_map/ppermute | solution.py:410
  120.6 5.8 %collective-permute-start.13 = (bf16[32,512]{1,0:T(8,128)(2,1)S(1)}, bf16[32,512]{1,0:T(8,128)(2,1)S(1)}, u32[]{:S(2)}, u32[]{:S(2)}) collective-permute-start(bf16[32,512]{1,0:T(8,128)(2,1)S(1)} %fusion.4), channel_id=1, source_target_pairs={{0,2},{1,3},{2,4},{3,5},{4,6},{5,7},{6,0},{7,1},{8,10},{9,11},{10,... | collective-permute-start | bytes 98312 | tf_op jit(solution)/shard_map/ppermute | solution.py:410
  126.4 7.1 %collective-permute-start.16 = (bf16[4,32,512]{2,1,0:T(8,128)(2,1)S(1)}, bf16[4,32,512]{2,1,0:T(8,128)(2,1)S(1)}, u32[]{:S(2)}, u32[]{:S(2)}) collective-permute-start(bf16[4,32,512]{2,1,0:T(8,128)(2,1)S(1)} %get-tuple-element.72), channel_id=1, source_target_pairs={{0,1},{1,0},{2,3},{3,2},{4,5},{5,4},{6,7},{7,6},{8,9},{9,8},{10,11... | collective-permute-start | bytes 393224 | tf_op jit(solution)/shard_map/ppermute | solution.py:410
  127.8 26.1 %all-to-all-start.1 = ((bf16[8,128,512]{2,1,0:T(8,128)(2,1)}), bf16[8,128,512]{2,1,0:T(8,128)(2,1)S(1)}, u32[]{:S(2)}, u32[]{:S(2)}) async-start(bf16[8,128,512]{2,1,0:T(8,128)(2,1)} %get-tuple-element.60), calls=%async_computation.1 | async-start | bytes 2097152 | tf_op jit(solution)/shard_map/all_to_all | solution.py:481
  133.5 11.8 %collective-permute-start.17 = (bf16[2,4,32,512]{3,2,1,0:T(8,128)(2,1)S(1)}, bf16[2,4,32,512]{3,2,1,0:T(8,128)(2,1)S(1)}, u32[]{:S(2)}, u32[]{:S(2)}) collective-permute-start(bf16[2,4,32,512]{3,2,1,0:T(8,128)(2,1)S(1)} %get-tuple-element.67), channel_id=1, source_target_pairs={{0,16},{8,24},{16,0},{24,8},{1,17},{9,25},{17,1},{25,9},{2,18},{10... | collective-permute-start | bytes 786440 | tf_op jit(solution)/shard_map/ppermute | solution.py:410
  145.4 2.0 %collective-permute-start.18 = (bf16[2,2,4,32,512]{4,3,2,1,0:T(8,128)(2,1)S(1)}, bf16[2,2,4,32,512]{4,3,2,1,0:T(8,128)(2,1)S(1)}, u32[]{:S(2)}, u32[]{:S(2)}) collective-permute-start(bf16[2,2,4,32,512]{4,3,2,1,0:T(8,128)(2,1)S(1)} %pad_maximum_fusion.1), channel_id=1, source_target_pairs={{0,8},{8,0},{16,24},{24,16},{1,9},{9,1},{17,25},{25,17},{2,10},{10... | collective-permute-start | bytes 1572872 | tf_op jit(solution)/shard_map/ppermute | solution.py:410
  (15 other events, 176.2 us)

commit v3 on v2

v3 whole, which is shorter than its diff:
```python
import math

import jax
import jax.numpy as jnp
from jax import lax
from jax.experimental import pallas as pl
from jax.experimental.pallas import tpu as pltpu
from jax.sharding import PartitionSpec as P

F32 = jnp.float32
BF16 = jnp.bfloat16
ANY = pl.BlockSpec(memory_space=pl.ANY)
VMEM = pl.BlockSpec(memory_space=pltpu.VMEM)
SMEM = pl.BlockSpec(memory_space=pltpu.SMEM)
MIB = 1 << 20


def params(mib=40):
    return pltpu.CompilerParams(vmem_limit_bytes=mib * MIB)


def cost(flops, moved):
    return pl.CostEstimate(flops=int(flops), bytes_accessed=int(moved), transcendentals=0)


def mm(a, b):
    return lax.dot_general(a, b, (((1,), (0,)), ((), ())), preferred_element_type=F32)


def mm_tn(a, b):
    return lax.dot_general(a, b, (((0,), (0,)), ((), ())), preferred_element_type=F32)


def mm_nt(a, b):
    return lax.dot_general(a, b, (((1,), (1,)), ((), ())), preferred_element_type=F32)


def far_memory(*arrays):
    return [pltpu.with_memory_space_constraint(x, pltpu.HBM) for x in arrays]


def id_memory(n, count):
    return [pltpu.SMEM((n,), jnp.int32)] * count + [pltpu.SemaphoreType.DMA((count,))]


def id_copies(sources, buffers, sem):
    copies = [pltpu.make_async_copy(source, buffer, sem.at[i]) for i, (source, buffer) in enumerate(zip(sources, buffers))]
    for copy in copies:
        copy.start()
    return copies


def flat_rows(x):
    return x.reshape(-1, x.shape[-1])


def after(x, *others):
    return lax.optimization_barrier((x,) + others)[0]


def row_chunk(rows, most):
    return max(c for c in range(8, most + 1, 8) if rows % c == 0)


def target_of(index, shift, n):
    return index ^ shift if n & (n - 1) == 0 else (index + shift) % n


def source_of(index, shift, n):
    return index ^ shift if n & (n - 1) == 0 else (index + n - shift) % n


def exchange(block, shift, n):
    return lax.ppermute(block, "asset", [(i, target_of(i, shift, n)) for i in range(n)])


def send_forward(me, features, tiles, cols, live, shifts, n):
    steps, _, width = features.shape
    tile = tiles.shape[1]
    count = len(shifts)

    def body(me_ref, cols_in, live_in, tiles_ref, f_ref, *rest):
        outs, (weights, blocks, made, tile_sem, block_sem, made_sem) = rest[:count], rest[count : count + 6]
        cols_ref, live_ref, id_sem = rest[count + 6 :]
        ids = id_copies((cols_in, live_in), (cols_ref, live_ref), id_sem)
        loads = []
        for j, shift in enumerate(shifts):
            to = target_of(me_ref[0], shift, n)
            loads.append([pltpu.make_async_copy(tiles_ref.at[to], weights.at[j], tile_sem.at[j])])
            loads[j][0].start()
        for copy in ids:
            copy.wait()
        for j, shift in enumerate(shifts):
            start = pl.multiple_of(cols_ref[target_of(me_ref[0], shift, n)] * tile, tile)
            loads[j].append(pltpu.make_async_copy(f_ref.at[:, pl.ds(start, tile), :], blocks.at[j], block_sem.at[j]))
            loads[j][1].start()
        stores = []
        for j, shift in enumerate(shifts):
            to = target_of(me_ref[0], shift, n)
            for copy in loads[j]:
                copy.wait()
            used = weights[j] * live_ref[to].astype(F32).astype(BF16)
            for t in range(steps):
                made[j, t] = mm(used, blocks[j, t]).astype(BF16)
            store = pltpu.make_async_copy(made.at[j], outs[j], made_sem.at[j])
            store.start()
            stores.append(store)
        for store in stores:
            store.wait()

    block = pltpu.HBM((steps, tile, width), BF16)
    size = steps * tile * width
    many = pltpu.VMEM((count, steps, tile, width), BF16)
    sems = pltpu.SemaphoreType.DMA((count,))
    return pl.pallas_call(
        body,
        out_shape=[block] * count,
        in_specs=[SMEM, ANY, ANY, ANY, ANY],
        out_specs=[ANY] * count,
        scratch_shapes=[pltpu.VMEM((count, tile, tile), BF16), many, many, sems, sems, sems] + id_memory(n, 2),
        compiler_params=params(),
        cost_estimate=cost(2 * count * size * tile, 4 * count * size),
        name="send_forward",
    )(me, *far_memory(cols, live, tiles, features))


def place_tiles(dense, tiles_ref, count, rows_ref, cols_ref, turned):
    tile = tiles_ref.shape[1]
    dense[...] = jnp.zeros(dense.shape, BF16)

    @pl.loop(0, count)
    def _(l):
        row, col = (cols_ref[l], rows_ref[l]) if turned else (rows_ref[l], cols_ref[l])
        to = (pl.ds(pl.multiple_of(row * tile, tile), tile), pl.ds(pl.multiple_of(col * tile, tile), tile))
        new = tiles_ref[l].astype(F32)
        dense[to] = (dense[to].astype(F32) + (new.T if turned else new)).astype(BF16)


def gate_terms(f, c, g, wv, wg):
    gate = jax.nn.sigmoid(mm(f, wg))
    kept = gate * mm(g, wv)
    c = c.astype(F32)
    return kept, (c * gate).astype(BF16), (c * kept * (1.0 - gate)).astype(BF16)


def load_ids(sources, buffers, sem):
    for copy in id_copies(sources, buffers, sem):
        copy.wait()


def local_forward(count, rows, cols, tiles, features, grad, w_value, w_gate, wanted):
    steps, assets, width = features.shape
    tile = tiles.shape[1]
    n = wanted.shape[0]
    chunk = row_chunk(assets, 5 * tile)
    turns = assets // chunk

    def body(count_ref, rows_ref, cols_ref, wanted_ref, tiles_ref, c_ref, wv_ref, wg_ref, f_in, *rest):
        kept_ref, dgate_ref, back_ref, sums_ref = rest[:4]
        owed, (dense, f_ref, r_ref, sem, r_sem) = rest[4 : 4 + steps], rest[4 + steps :]
        t, i = pl.program_id(0), pl.program_id(1)
        loads = [pltpu.make_async_copy(f_in.at[s], f_ref.at[s], sem.at[s]) for s in range(steps)]

        @pl.when((t == 0) & (i == 0))
        def _():
            for load in loads:
                load.start()
            place_tiles(dense, tiles_ref, count_ref[0], rows_ref, cols_ref, False)
            sums_ref[...] = jnp.zeros(sums_ref.shape, F32)

        for s in range(steps):

            @pl.when((t == s) & (i == 0))
            def _():
                loads[s].wait()

        at = pl.ds(pl.multiple_of(i * chunk, chunk), chunk)
        f = f_ref[t, at, :]
        g = mm(dense[at, :], f_ref[t]).astype(BF16)
        kept, dagg, dgate = gate_terms(f, c_ref[0], g, wv_ref[...], wg_ref[...])
        back = mm_nt(dagg, wv_ref[...]).astype(BF16)
        back_ref[0] = back
        r_ref[at, :] = back
        kept_ref[0] = kept.astype(BF16)
        dgate_ref[0] = dgate
        sums_ref[0] += mm_tn(g, dagg)
        sums_ref[1] += mm_tn(f, dgate)

        @pl.when(i == turns - 1)
        def _():
            for s in range(steps):

                @pl.when(t == s)
                def _():
                    stores = []
                    for d in range(n):
                        block = pl.ds(pl.multiple_of(wanted_ref[d] * tile, tile), tile)
                        stores.append(pltpu.make_async_copy(r_ref.at[block, :], owed[s].at[d], r_sem.at[d]))
                    for store in stores:
                        store.start()
                    for store in stores:
                        store.wait()

    line = pl.BlockSpec((1, chunk, width), lambda t, i: (t, i, 0))
    weight = pl.BlockSpec((width, width), lambda t, i: (0, 0))
    return pl.pallas_call(
        body,
        grid=(steps, turns),
        out_shape=[pltpu.HBM(features.shape, BF16)] * 3
        + [pltpu.HBM((2, width, width), F32)]
        + [pltpu.HBM((n, tile, width), BF16)] * steps,
        in_specs=[SMEM] * 4 + [pl.BlockSpec(tiles.shape, lambda t, i: (0, 0, 0)), line, weight, weight, ANY],
        out_specs=[line, line, line, pl.BlockSpec((2, width, width), lambda t, i: (0, 0, 0))] + [ANY] * steps,
        scratch_shapes=[
            pltpu.VMEM((assets, assets), BF16),
            pltpu.VMEM(features.shape, BF16),
            pltpu.VMEM((assets, width), BF16),
            pltpu.SemaphoreType.DMA((steps,)),
            pltpu.SemaphoreType.DMA((n,)),
        ],
        compiler_params=params(),
        cost_estimate=cost(0, 0),
        name="local_forward",
    )(count, rows, cols, wanted, *far_memory(tiles, grad, w_value, w_gate, features))


def local_back(me, count, rows, cols, tiles, back, grad, dgate, made, places, groups, w_gate, n):
    steps, assets, width = back.shape
    tile = tiles.shape[1]
    chunk = row_chunk(assets, 5 * tile)
    per = chunk // tile
    sets = len(made)

    def body(me_ref, count_ref, rows_ref, cols_ref, places_ref, tiles_ref, c_ref, d_ref, w_ref, r_in, *rest):
        parts, (out_ref, dense, r_ref, sem, *turned) = rest[:sets], rest[sets:]
        t, i = pl.program_id(0), pl.program_id(1)
        loads = [pltpu.make_async_copy(r_in.at[s], r_ref.at[s], sem.at[s]) for s in range(steps)]

        @pl.when((t == 0) & (i == 0))
        def _():
            for load in loads:
                load.start()
            place_tiles(dense, tiles_ref, count_ref[0], rows_ref, cols_ref, True)
            for part, to in zip(parts, turned):
                to[...] = mm_nt(flat_rows(part[...]), w_ref[...]).reshape(to.shape)

        for s in range(steps):

            @pl.when((t == s) & (i == 0))
            def _():
                loads[s].wait()

        at = pl.ds(pl.multiple_of(i * chunk, chunk), chunk)
        out_ref[0] = c_ref[0].astype(F32) + mm(dense[at, :], r_ref[t]) + mm_nt(d_ref[0], w_ref[...])
        for part, shifts in zip(turned, groups):
            for j, shift in enumerate(shifts):
                place = places_ref[source_of(me_ref[0], shift, n)] - i * per

                @pl.when((place >= 0) & (place < per))
                def _():
                    out_ref[0, pl.ds(pl.multiple_of(place * tile, tile), tile), :] += part[j, t]

    line = pl.BlockSpec((1, chunk, width), lambda t, i: (t, i, 0))
    weight = pl.BlockSpec((width, width), lambda t, i: (0, 0))
    pieces = [pl.BlockSpec((x.shape[0], 1) + x.shape[2:], lambda t, i: (0, 1, 0, 0, 0)) for x in made]
    return pl.pallas_call(
        body,
        grid=(steps, assets // chunk),
        out_shape=pltpu.HBM(back.shape, F32),
        in_specs=[SMEM] * 5
        + [pl.BlockSpec(tiles.shape, lambda t, i: (0, 0, 0)), line, line, weight, ANY]
        + pieces,
        out_specs=line,
        scratch_shapes=[
            pltpu.VMEM((assets, assets), BF16),
            pltpu.VMEM(back.shape, BF16),
            pltpu.SemaphoreType.DMA((steps,)),
        ]
        + [pltpu.VMEM((x.shape[0],) + x.shape[2:], F32) for x in made],
        compiler_params=params(),
        cost_estimate=cost(0, 0),
        name="local_back",
    )(me, count, rows, cols, places, *far_memory(tiles, grad, dgate, w_gate, back, *made))


def add_arrived(me, sums, arrived, rows, features, grad, w_value, w_gate, shifts, n, tile):
    steps, _, width = features.shape
    count = len(shifts)
    most = 3
    summed = sums is not None

    def body(me_ref, rows_in, f_ref, c_ref, wv_ref, wg_ref, *rest):
        parts, rest = rest[:count], rest[count:]
        if summed:
            s_ref, made_ref, sums_ref, s_buf, *rest = rest
        else:
            made_ref, *rest = rest
        p_buf, f_buf, c_buf, w_buf, made, sem, w_sem, made_sem, rows_ref, id_sem = rest
        ids = id_copies((rows_in,), (rows_ref,), id_sem)
        first = [pltpu.make_async_copy(ref, w_buf.at[i], w_sem.at[i]) for i, ref in enumerate((wg_ref, wv_ref))]
        first += [pltpu.make_async_copy(parts[j], p_buf.at[j], sem.at[0, j]) for j in range(count)]
        for load in first:
            load.start()
        ids[0].wait()
        then = []
        for j, shift in enumerate(shifts):
            at = pl.ds(pl.multiple_of(rows_ref[source_of(me_ref[0], shift, n)] * tile, tile), tile)
            then.append(pltpu.make_async_copy(f_ref.at[:, at, :], f_buf.at[j], sem.at[1, j]))
            then.append(pltpu.make_async_copy(c_ref.at[:, at, :], c_buf.at[j], sem.at[2, j]))
        for load in then:
            load.start()
        if summed:
            old = pltpu.make_async_copy(s_ref, s_buf, w_sem.at[2])
            old.start()
        for load in first:
            load.wait()
        stores = []
        for low in range(0, count, most):
            some = slice(low, min(low + most, count))
            for load in then[2 * some.start : 2 * some.stop]:
                load.wait()
            p, f, c = [flat_rows(buf[some]) for buf in (p_buf, f_buf, c_buf)]
            kept, dagg, dgate = gate_terms(f, c, p, w_buf[1], w_buf[0])
            shape = (some.stop - some.start, steps, tile, width)
            made[some, 0] = kept.astype(BF16).reshape(shape)
            made[some, 1] = dgate.reshape(shape)
            store = pltpu.make_async_copy(made.at[some], made_ref.at[some], made_sem.at[low])
            store.start()
            stores.append(store)
            if summed and low == 0:
                old.wait()
                sums_ref[0] = s_buf[0] + mm_tn(p, dagg)
                sums_ref[1] = s_buf[1] + mm_tn(f, dgate)
            elif summed:
                sums_ref[0] += mm_tn(p, dagg)
                sums_ref[1] += mm_tn(f, dgate)
        for store in stores:
            store.wait()

    many = pltpu.VMEM((count, steps, tile, width), BF16)
    pair = (count, 2, steps, tile, width)
    operands = far_memory(rows, features, grad, w_value, w_gate) + list(arrived)
    out_shape, out_specs, scratch = [pltpu.HBM(pair, BF16)], [ANY], []
    if summed:
        operands += far_memory(sums)
        out_shape.append(pltpu.HBM(sums.shape, F32))
        out_specs.append(VMEM)
        scratch.append(pltpu.VMEM(sums.shape, F32))
    return pl.pallas_call(
        body,
        out_shape=out_shape,
        in_specs=[SMEM] + [ANY] * len(operands),
        out_specs=out_specs,
        scratch_shapes=scratch
        + [
            many,
            many,
            many,
            pltpu.VMEM((2, width, width), BF16),
            pltpu.VMEM(pair, BF16),
            pltpu.SemaphoreType.DMA((3, count)),
            pltpu.SemaphoreType.DMA((3,)),
            pltpu.SemaphoreType.DMA((count,)),
        ]
        + id_memory(n, 1),
        compiler_params=params(),
        cost_estimate=cost(0, 0),
        name="add_arrived" if summed else "arrived_terms",
    )(me, *operands)


def prepare_late(me, rows, features, grad, w_gate, shifts, n, tile):
    steps, _, width = features.shape
    count = len(shifts)

    def body(me_ref, rows_in, f_ref, c_ref, w_ref, half_ref, u_ref, f_buf, c_buf, sem, rows_ref, id_sem):
        load_ids((rows_in,), (rows_ref,), id_sem)
        loads = []
        for j, shift in enumerate(shifts):
            at = pl.ds(pl.multiple_of(rows_ref[source_of(me_ref[0], shift, n)] * tile, tile), tile)
            loads.append(pltpu.make_async_copy(f_ref.at[:, at, :], f_buf.at[j], sem.at[0, j]))
            loads.append(pltpu.make_async_copy(c_ref.at[:, at, :], c_buf.at[j], sem.at[1, j]))
        for load in loads:
            load.start()
        for load in loads:
            load.wait()
        f = flat_rows(f_buf[...])
        gate = jax.nn.sigmoid(mm(f, w_ref[...]))
        dagg = flat_rows(c_buf[...]).astype(F32) * gate
        half_ref[0] = f
        half_ref[1] = dagg.astype(BF16)
        u_ref[...] = dagg * (1.0 - gate)

    many = pltpu.VMEM((count, steps, tile, width), BF16)
    lines = count * steps * tile
    return pl.pallas_call(
        body,
        out_shape=[pltpu.HBM((2, lines, width), BF16), pltpu.HBM((lines, width), F32)],
        in_specs=[SMEM, ANY, ANY, ANY, VMEM],
        out_specs=[VMEM, VMEM],
        scratch_shapes=[many, many, pltpu.SemaphoreType.DMA((2, count))] + id_memory(n, 1),
        compiler_params=params(),
        cost_estimate=cost(0, 0),
        name="prepare_late",
    )(me, *far_memory(rows, features, grad, w_gate))


def add_late(sums, arrived, half, u, w_value, place, level, wire):
    steps, tile, width = arrived[0].shape
    count = len(arrived)
    size = level[2]
    lines = 2 * width // size

    def body(place_ref, s_ref, half_ref, u_ref, w_ref, *rest):
        parts, (keep_ref, *send_refs), rest = rest[:count], rest[count : count + size], rest[count + size :]
        p_buf, w_buf, h_buf, u_buf, total, made, sem, done_sem = rest
        first = [pltpu.make_async_copy(parts[j], p_buf.at[j], sem.at[4 + j]) for j in range(count)]
        first += [pltpu.make_async_copy(ref, buf, sem.at[i]) for i, (ref, buf) in enumerate(((w_ref, w_buf), (half_ref, h_buf)))]
        later = [pltpu.make_async_copy(ref, buf, sem.at[2 + i]) for i, (ref, buf) in enumerate(((u_ref, u_buf), (s_ref, total)))]
        for load in first + later:
            load.start()
        for load in first:
            load.wait()
        p = flat_rows(p_buf[...])
        agg = mm(p, w_buf[...])
        value = mm_tn(p, h_buf[1])
        later[0].wait()
        gate = mm_tn(h_buf[0], (agg * u_buf[...]).astype(BF16))
        later[1].wait()
        total[:width, :] += value
        total[width:, :] += gate
        made[...] = total[...].astype(wire)
        stores = []
        for i, (source, to) in enumerate([(total, keep_ref)] + [(made, ref) for ref in send_refs]):
            mine = pl.ds(pl.multiple_of(lax.rem(place_ref[0] + i, size) * lines, lines), lines)
            stores.append(pltpu.make_async_copy(source.at[mine, :], to, done_sem.at[i]))
        for store in stores:
            store.start()
        for store in stores:
            store.wait()

    return pl.pallas_call(
        body,
        out_shape=[pltpu.HBM((lines, width), F32)] + [pltpu.HBM((lines, width), wire)] * (size - 1),
        in_specs=[SMEM] + [ANY] * (4 + count),
        out_specs=[ANY] * size,
        scratch_shapes=[
            pltpu.VMEM((count, steps, tile, width), BF16),
            pltpu.VMEM((width, width), BF16),
            pltpu.VMEM(half.shape, BF16),
            pltpu.VMEM(u.shape, F32),
            pltpu.VMEM((2 * width, width), F32),
            pltpu.VMEM((2 * width, width), wire),
            pltpu.SemaphoreType.DMA((4 + count,)),
            pltpu.SemaphoreType.DMA((size,)),
        ],
        compiler_params=params(),
        cost_estimate=cost(0, 0),
        name="add_late",
    )(place, *far_memory(sums.reshape(2 * width, width), half, u, w_value), *arrived)


def settle(me, kept, features, made, rows, groups, n, tile):
    steps, assets, width = kept.shape
    blocks = assets // tile
    per = 2 if blocks % 2 == 0 else 1
    sets = len(made)

    def body(me_ref, rows_ref, k_ref, f_ref, *rest):
        parts, (out_ref, acc) = rest[:sets], rest[sets:]
        b = pl.program_id(0)
        acc[...] = f_ref[...].astype(F32) + k_ref[...].astype(F32)
        for part, shifts in zip(parts, groups):
            for j, shift in enumerate(shifts):
                place = rows_ref[source_of(me_ref[0], shift, n)] - b * per

                @pl.when((place >= 0) & (place < per))
                def _():
                    acc[:, pl.ds(pl.multiple_of(place * tile, tile), tile), :] += part[j, 0].astype(F32)

        out_ref[...] = acc[...].astype(BF16)

    line = pl.BlockSpec((steps, per * tile, width), lambda b: (0, b, 0))
    pieces = [pl.BlockSpec((x.shape[0], 1) + x.shape[2:], lambda b: (0,) * 5) for x in made]
    return pl.pallas_call(
        body,
        grid=(blocks // per,),
        out_shape=pltpu.HBM((steps, assets, width), BF16),
        in_specs=[SMEM, SMEM, line, line] + pieces,
        out_specs=line,
        scratch_shapes=[pltpu.VMEM((steps, per * tile, width), F32)],
        compiler_params=params(),
        cost_estimate=cost(0, 0),
        name="settle",
    )(me, rows, *far_memory(kept, features, *made))


def finish(step, grads, base, returned, cols, live, tiles, n):
    steps, assets, width = base.shape
    tile = tiles.shape[1]
    blocks = assets // tile
    per = 2 if blocks % 2 == 0 else 1

    def body(cols_ref, live_ref, tiles_ref, r_ref, b_ref, *rest):
        out_ref, acc = rest[-2:]
        b = pl.program_id(0)
        acc[...] = b_ref[0]
        for of in range(n):
            spot = cols_ref[of] - b * per

            @pl.when((spot >= 0) & (spot < per) & (live_ref[of] != 0))
            def _():
                acc[pl.ds(pl.multiple_of(spot * tile, tile), tile), :] += mm_tn(tiles_ref[of], r_ref[of])

        out_ref[0] = acc[...].astype(BF16)

    line = pl.BlockSpec((1, per * tile, width), lambda b: (step, b, 0))
    every = [pl.BlockSpec(x.shape, lambda b: (0, 0, 0)) for x in (tiles, returned)]
    old = [] if grads is None else far_memory(grads)
    return pl.pallas_call(
        body,
        grid=(blocks // per,),
        out_shape=pltpu.HBM((steps, assets, width), BF16),
        in_specs=[SMEM, SMEM, *every, line] + [ANY] * len(old),
        out_specs=line,
        scratch_shapes=[pltpu.VMEM((per * tile, width), F32)],
        input_output_aliases={5: 0} if old else {},
        compiler_params=params(),
        cost_estimate=cost(0, 0),
        name="finish",
    )(cols, live, *far_memory(tiles), returned, *far_memory(base), *old)


def levels(tm, asset):
    low = max(d for d in range(1, math.isqrt(asset) + 1) if asset % d == 0)
    pair = 2 if tm % 2 == 0 else 1
    return [("tm", 1, pair, tm), ("tm", pair, tm // pair, tm), ("asset", 1, low, asset), ("asset", low, asset // low, asset)]


def member(level):
    axis, stride, size, _ = level
    return (lax.axis_index(axis) // stride) % size


def pairs_of(level, shift):
    _, stride, size, n = level
    return [(i, i + ((i // stride + shift) % size - (i // stride) % size) * stride) for i in range(n)]


def scatter_sum(terms, level, wire):
    axis, _, size, _ = level
    me = member(level)

    def entry(index):
        return sum(lax.dynamic_index_in_dim(x, index, 0, keepdims=False) for x in terms)

    arrived = [lax.ppermute(entry((me + s) % size).astype(wire), axis, pairs_of(level, s)) for s in range(1, size)]
    total = entry(me)
    for part in arrived:
        total = total + part.astype(F32)
    return total


def butterfly_sum(x, level, wire):
    axis, _, size, _ = level
    if size & (size - 1):
        return lax.psum(x, axis, axis_index_groups=groups_of(level))
    shift = 1
    while shift < size:
        x = x.astype(wire)
        x = x.astype(F32) + lax.ppermute(x, axis, [(i, i ^ (shift * level[1])) for i in range(level[3])]).astype(F32)
        shift *= 2
    return x


def groups_of(level):
    _, stride, size, n = level
    return [[i + s * stride for s in range(size)] for i in range(n) if (i // stride) % size == 0]


def spread(x, level):
    axis, _, size, _ = level
    return [x] + [lax.ppermute(x, axis, pairs_of(level, s)) for s in range(1, size)]


def unshuffle(x, stacked, placed, shape):
    place = jnp.arange(math.prod(level[2] for level in placed), dtype=jnp.int32)
    digits, stride = {}, 1
    for level in reversed(placed):
        digits[level] = (place // stride) % level[2]
        stride *= level[2]
    index, stride = 0, 1
    for level in reversed(stacked):
        index = index + ((member(level) - digits[level]) % level[2]) * stride
        stride *= level[2]
    flat = x.reshape(place.shape[0], -1, shape[-1])
    return jnp.take(flat, index, axis=0, mode="clip").reshape(shape).astype(F32)


def per_device(
    features,
    w_value,
    w_gate,
    cotangent,
    local_rows,
    local_cols,
    local_count,
    local_tiles,
    remote_rows,
    remote_cols,
    remote_live,
    remote_tiles,
):
    steps, assets, width = features.shape
    tile = local_tiles.shape[1]
    n = lax.axis_size("asset")
    tm = lax.axis_size("tm")
    me = lax.axis_index("asset").astype(jnp.int32).reshape(1)
    flat = features.reshape(-1, width)
    grad = cotangent.reshape(-1, width)

    far = list(range(n // 2, n))
    near = list(range(1, n // 2))
    shifts = far + near
    lead = max(1, len(far) - 1)
    first, second = far[:lead] + near[:2], far[lead:] + near[2:]
    late = far[-2:] + near[2:]
    early = [s for s in shifts if s not in late]
    weights = (w_value, w_gate)
    graph = (local_count, local_rows, local_cols, local_tiles)

    sent = dict(zip(shifts, send_forward(me, features, remote_tiles, remote_cols, remote_live, shifts, n)))
    came = {s: exchange(sent[s], s, n) for s in first}
    kept, dgate, back, sums, *owed = local_forward(*graph, features, cotangent, *weights, remote_rows)
    for s in second:
        came[s] = exchange(after(sent[s], sums, came[far[0]], came[near[0]]), s, n)
    half_late, u_late = prepare_late(me, remote_rows, features, cotangent, w_gate, late, n, tile)
    made_early, sums = add_arrived(
        me, sums, [came[s] for s in early], remote_rows, features, cotangent, *weights, early, n, tile
    )
    pair, column, row, line = levels(tm, n)
    whole = ("tm", 1, tm, tm)
    place = member(whole).astype(jnp.int32).reshape(1)
    keep, *sends = add_late(sums, [came[s] for s in late], half_late, u_late, w_value, place, whole, BF16)

    def send_back(t, *before):
        return lax.all_to_all(after(owed[t], *before), "asset", 0, 0, tiled=True)

    returned = [send_back(t, made_early, half_late, *[came[s] for s in late]) for t in range(steps // 2)]
    (made_late,) = add_arrived(
        me, None, [came[s] for s in late], remote_rows, features, cotangent, *weights, late, n, tile
    )
    made, groups = (made_early, made_late), (early, late)
    output = settle(me, kept, features, made, remote_rows, groups, n, tile)
    base = local_back(me, *graph, back, cotangent, dgate, made, remote_rows, groups, w_gate, n)
    terms = [keep] + [lax.ppermute(x, "tm", pairs_of(whole, i + 1)) for i, x in enumerate(sends)]
    terms[1] = after(terms[1], made_late, output)
    shape = (row[2], keep.shape[0] // row[2], width)
    terms = [x.astype(F32).reshape(shape) for x in terms]
    sums = after(scatter_sum(terms, row, BF16), *returned)
    sums = butterfly_sum(sums, line, BF16).astype(BF16)
    returned += [send_back(t, sums) for t in range(steps // 2, steps)]

    grad_features = None

    def finish_step(t):
        return finish(t, grad_features, base, returned[t], remote_cols, remote_live, remote_tiles, n)

    for t in range(steps // 2):
        grad_features = finish_step(t)
    sums = jnp.stack(spread(sums, row))
    sums = jnp.stack(spread(sums, column))
    if grad_features is not None:
        sums = after(sums, grad_features)
    sums = jnp.stack(spread(sums, pair))
    scale = float(steps * assets * tm * n) ** (-0.5)
    sums = unshuffle(sums, [pair, column, row], [column, pair, row], (2, width, width)) * scale
    for t in range(steps // 2, steps):
        grad_features = finish_step(t)
    return output, grad_features, sums[0], sums[1]


def solution(mesh):
    return jax.shard_map(
        per_device,
        mesh=mesh,
        in_specs=(
            P("tm", "asset", None),
            P(),
            P(),
            P("tm", "asset", None),
            P("asset"),
            P("asset"),
            P("asset"),
            P("asset", None, None),
            P("asset"),
            P("asset"),
            P("asset"),
            P("asset", None, None),
        ),
        out_specs=(P("tm", "asset", None), P("tm", "asset", None), P(), P()),
        check_vma=False,
    )
```

time: 166 us -> 137 us (0.83)
  Pallas kernels: 88.2 us -> 75.9 us
  waiting for transfers between devices: 30 us -> 21 us
  local copies, waits for them, and re-layouts: 8.01 us -> 2.21 us
    pallas_call x10, Pallas kernels: 88.2 us -> 75.9 us  [the longest x1 19.5 us: local_forward(): pl.pallas_call(body, grid=(steps, turns), out_shape=[pltpu.HBM(features.s...]
    all_to_all x2, waiting for transfers between devices: 9.94 us -> 1.97 us  [send_back(): return lax.all_to_all(after(owed[t], *before), 'asset', 0, 0, tiled=True)]
    ppermute x6 -> x3, waiting for transfers between devices: 8.26 us -> 1.82 us  [spread(): lax.ppermute(x, axis, pairs_of(level, s))]
    unnamed x36 -> x18, local copies, waits for them, and re-layouts: 4.48 us -> 0.04 us
    ppermute x6, waiting for transfers between devices: 11.7 us -> 15.7 us  [the longest x2 10.2 us: butterfly_sum(): lax.ppermute(x, axis, [(i, i ^ shift * level[1]) for i in range(level[3])])]
    all_to_all x2, starting transfers between devices: 9.17 us -> 11.8 us  [send_back(): return lax.all_to_all(after(owed[t], *before), 'asset', 0, 0, tiled=True)]
    ppermute x6 -> x3, starting transfers between devices: 5.51 us -> 2.92 us  [spread(): lax.ppermute(x, axis, pairs_of(level, s))]
  transfers between devices with their start and end apart: 21 -> 18, of which waited for: 10 -> 7; matrix products, arithmetic and copies ran while one was open for 3% -> 2% of each run, Pallas kernels for 41% -> 49%
where the time goes in v3:
time: 137 us
  Pallas kernels  75.9 us (55%)
  starting transfers between devices  34.8 us (25%)
  waiting for transfers between devices  21 us (15%)
  local copies, waits for them, and re-layouts  2.21 us (2%)
  between operations  1.65 us (1%)
    pallas_call x1, Pallas kernels, local_forward(): pl.pallas_call(body, grid=(steps, turns), out_shape=[pltpu.HBM(features.s...  19.5 us
    pallas_call x1, Pallas kernels, local_back(): pl.pallas_call(body, grid=(steps, assets // chunk), out_shape=pltpu.HBM(b...  12.8 us
    ppermute x7, starting transfers between devices, exchange(): lax.ppermute(block, 'asset', [(i, target_of(i, shift, n)) for i in range(...  12.3 us
    pallas_call x2, Pallas kernels, add_arrived(): pl.pallas_call(body, out_shape=out_shape, in_specs=[SMEM] + [ANY] * len(o...  12.1 us
    all_to_all x2, starting transfers between devices, send_back(): return lax.all_to_all(after(owed[t], *before), 'asset', 0, 0, tiled=True)  11.8 us
    pallas_call x2, Pallas kernels, finish(): pl.pallas_call(body, grid=(blocks // per,), out_shape=pltpu.HBM((steps, a...  10.4 us
    ppermute x2, waiting for transfers between devices, butterfly_sum(): lax.ppermute(x, axis, [(i, i ^ shift * level[1]) for i in range(level[3])])  10.2 us
    pallas_call x1, Pallas kernels, settle(): pl.pallas_call(body, grid=(blocks // per,), out_shape=pltpu.HBM((steps, a...  6.77 us
  transfers between devices with their start and end apart: 18, of which 7 were waited for; matrix products, arithmetic and copies ran while one was open for 2% of the time, Pallas kernels for 49%

profile of v3, /device:TPU:0, one launch (start us, length us, event | category | flops | bytes accessed | tf_op | source)
XLA Modules:
  0.0 136.5 jit_solution(13596673326918209210)
XLA Ops:
  0.7 4.2 %send_forward.1 = (bf16[2,128,512]{2,1,0:T(8,128)(2,1)}, bf16[2,128,512]{2,1,0:T(8,128)(2,1)}, bf16[2,128,512]{2,1,0:T(8,128)(2,1)}, bf16[2,128,512]{2,1,0:T(8,1...) custom-call(s32[1]{0:T(128)} %bitcast.me_ref, s32[8]{0:T(128)} %cols_ref.7, ...), custom_call_target="tpu_custom_call" | custom-call | flops 234881024 | bytes 3670016 | tf_op jit(solution)/shard_map/send_forward/pallas_call | solution.py:115
  4.9 4.1 %collective-permute-start = (bf16[2,128,512]{2,1,0:T(8,128)(2,1)}, bf16[2,128,512]{2,1,0:T(8,128)(2,1)S(1)}, u32[]{:S(2)}, u32[]{:S(2)}) collective-permute-start(bf16[2,128,512]{2,1,0:T(8,128)(2,1)} %get-tuple-element.33), channel_id=1, source_target_pairs={{0,4},{1,5},{2,6},{3,7},{4,0},{5,1},{6,2},{7,3},{8,12},{9,13},{10,... | collective-permute-start | bytes 786440 | tf_op jit(solution)/shard_map/ppermute | solution.py:74
  10.5 1.8 %collective-permute-start.3 = (bf16[2,128,512]{2,1,0:T(8,128)(2,1)}, bf16[2,128,512]{2,1,0:T(8,128)(2,1)S(1)}, u32[]{:S(2)}, u32[]{:S(2)}) collective-permute-start(bf16[2,128,512]{2,1,0:T(8,128)(2,1)} %get-tuple-element.36), channel_id=1, source_target_pairs={{0,2},{1,3},{2,0},{3,1},{4,6},{5,7},{6,4},{7,5},{8,10},{9,11},{10,... | collective-permute-start | bytes 786440 | tf_op jit(solution)/shard_map/ppermute | solution.py:74
  12.4 2.5 %collective-permute-start.4 = (bf16[2,128,512]{2,1,0:T(8,128)(2,1)}, bf16[2,128,512]{2,1,0:T(8,128)(2,1)S(1)}, u32[]{:S(2)}, u32[]{:S(2)}) collective-permute-start(bf16[2,128,512]{2,1,0:T(8,128)(2,1)} %get-tuple-element.39), channel_id=1, source_target_pairs={{0,6},{1,7},{2,4},{3,5},{4,2},{5,3},{6,0},{7,1},{8,14},{9,15},{10,... | collective-permute-start | bytes 786440 | tf_op jit(solution)/shard_map/ppermute | solution.py:74
  15.5 19.5 %local_forward.1 = (bf16[2,1280,512]{2,1,0:T(8,128)(2,1)}, bf16[2,1280,512]{2,1,0:T(8,128)(2,1)}, bf16[2,1280,512]{2,1,0:T(8,128)(2,1)}, f32[2,512,512]{2,1,0:T(...) custom-call(s32[1]{0:T(128)S(6)} %copy.18.count_ref, s32[20]{0:T(128)S(1)} %copy-done.4, ...), custom_call_target="tpu_custom_call" | custom-call | tf_op jit(solution)/shard_map/local_forward/pallas_call | solution.py:206
  35.1 2.3 %collective-permute-start.5 = (bf16[2,128,512]{2,1,0:T(8,128)(2,1)S(1)}, bf16[2,128,512]{2,1,0:T(8,128)(2,1)S(1)}, u32[]{:S(2)}, u32[]{:S(2)}) collective-permute-start(bf16[2,128,512]{2,1,0:T(8,128)(2,1)S(1)} %copy-done.8), channel_id=1, source_target_pairs={{0,7},{1,6},{2,5},{3,4},{4,3},{5,2},{6,1},{7,0},{8,15},{9,14},{10,... | collective-permute-start | bytes 786440 | tf_op jit(solution)/shard_map/ppermute | solution.py:74
  37.5 5.5 %prepare_late.1 = (bf16[2,768,512]{2,1,0:T(8,128)(2,1)}, f32[768,512]{1,0:T(8,128)}) custom-call(s32[1]{0:T(128)} %bitcast.me_ref, s32[8]{0:T(128)} %places_ref.1, bf16[2,1280,512]{2,1,0:T(8,128)(2,1)} %f_ref.9, bf16[2,1280,512]{2,1,0:T(8,128)(2,1)} %c_ref.9, bf16[512,512]{1,0:T(8,128)(2,1)} %w_ref.5), custom_call_target="tpu_custom_call" | custom-call | tf_op jit(solution)/shard_map/prepare_late/pallas_call | solution.py:396
  44.3 7.5 %add_arrived.1 = (bf16[4,2,2,128,512]{4,3,2,1,0:T(8,128)(2,1)}, f32[2,512,512]{2,1,0:T(8,128)}) custom-call(s32[1]{0:T(128)} %bitcast.me_ref, s32[8]{0:T(128)} %places_ref.1, bf16[2,1280,512]{2,1,0:T(8,128)(2,1)} %f_ref.9, bf16[2,1280,512]{2,1,0:T(8,128)(2,1)} %c_ref.9, bf16[512,512]{1,0:T(8,128)(2,1)} %w_ref.4, bf16[512,512]{1,0:T(8,128)(2,1)} %w_ref.5, ...), custom_call_target="tpu_custom_call" | custom-call | tf_op jit(solution)/shard_map/add_arrived/pallas_call | solution.py:349
  51.9 7.9 %all-to-all-start = ((bf16[8,128,512]{2,1,0:T(8,128)(2,1)}), bf16[8,128,512]{2,1,0:T(8,128)(2,1)S(1)}, u32[]{:S(2)}, u32[]{:S(2)}) async-start(bf16[8,128,512]{2,1,0:T(8,128)(2,1)} %get-tuple-element.54), calls=%async_computation | async-start | bytes 2097152 | tf_op jit(solution)/shard_map/all_to_all | solution.py:647
  59.7 4.6 %add_late.1 = (f32[256,512]{1,0:T(8,128)}, bf16[256,512]{1,0:T(8,128)(2,1)}, bf16[256,512]{1,0:T(8,128)(2,1)}, bf16[256,512]{1,0:T(8,128)(2,1)}) custom-call(s32[1]{0:T(128)} %bitcast.1.place_ref, f32[1024,512]{1,0:T(8,128)} %bitcast.27, bf16[2,768,512]{2,1,0:T(8,128)(2,1)} %get-tuple-element.46.half_ref, f32[768,512]{1,0:T(8,128)} %get-tuple-element.47.u_ref, ...), custom_call_target="tpu_custom_call" | custom-call | tf_op jit(solution)/shard_map/add_late/pallas_call | solution.py:442
  66.2 4.7 %arrived_terms.1.rest_1_ = bf16[3,2,2,128,512]{4,3,2,1,0:T(8,128)(2,1)} custom-call(s32[1]{0:T(128)} %bitcast.me_ref, s32[8]{0:T(128)} %places_ref.1, bf16[2,1280,512]{2,1,0:T(8,128)(2,1)} %f_ref.9, bf16[2,1280,512]{2,1,0:T(8,128)(2,1)} %c_ref.9, bf16[512,512]{1,0:T(8,128)(2,1)} %w_ref.4, bf16[512,512]{1,0:T(8,128)(2,1)} %w_ref.5, ...), custom_call_target="tpu_custom_call" | custom-call | tf_op jit(solution)/shard_map/arrived_terms/pallas_call | solution.py:349
  70.8 6.8 %settle.1 = bf16[2,1280,512]{2,1,0:T(8,128)(2,1)} custom-call(s32[1]{0:T(128)} %bitcast.me_ref, s32[8]{0:T(128)S(1)} %copy-done.1, bf16[2,1280,512]{2,1,0:T(8,128)(2,1)} %get-tuple-element.32.k_ref, bf16[2,1280,512]{2,1,0:T(8,128)(2,1)} %f_ref.9, bf16[4,2,2,128,512]{4,3,2,1,0:T(8,128)(2,1)} %get-tuple-element.38.rest_0_, ...), custom_call_target="tpu_custom_call" | custom-call | tf_op jit(solution)/shard_map/settle/pallas_call | solution.py:485
  79.1 2.1 %collective-permute-start.10 = (bf16[128,512]{1,0:T(8,128)(2,1)S(1)}, bf16[128,512]{1,0:T(8,128)(2,1)S(1)}, u32[]{:S(2)}, u32[]{:S(2)}) collective-permute-start(bf16[128,512]{1,0:T(8,128)(2,1)S(1)} %fusion), channel_id=1, source_target_pairs={{0,1},{1,0},{2,3},{3,2},{4,5},{5,4},{6,7},{7,6},{8,9},{9,8},{10,11... | collective-permute-start | bytes 393224 | tf_op jit(solution)/shard_map/ppermute | solution.py:557
  81.2 4.3 %collective-permute-done.10 = bf16[128,512]{1,0:T(8,128)(2,1)S(1)} collective-permute-done((bf16[128,512]{1,0:T(8,128)(2,1)S(1)}, bf16[128,512]{1,0:T(8,128)(2,1)S(1)}, u32[]{:S(2)}, u32[]{:S(2)}) %collective-permute-start.10) | collective-permute-done | bytes 131104 | tf_op jit(solution)/shard_map/ppermute | solution.py:557
  85.7 2.1 %collective-permute-start.11 = (bf16[128,512]{1,0:T(8,128)(2,1)S(1)}, bf16[128,512]{1,0:T(8,128)(2,1)S(1)}, u32[]{:S(2)}, u32[]{:S(2)}) collective-permute-start(bf16[128,512]{1,0:T(8,128)(2,1)S(1)} %bitcast_add_fusion), channel_id=1, source_target_pairs={{0,2},{1,3},{2,0},{3,1},{4,6},{5,7},{6,4},{7,5},{8,10},{9,11},{10,... | collective-permute-start | bytes 393224 | tf_op jit(solution)/shard_map/ppermute | solution.py:571
  87.8 3.5 %collective-permute-done.11 = bf16[128,512]{1,0:T(8,128)(2,1)S(1)} collective-permute-done((bf16[128,512]{1,0:T(8,128)(2,1)S(1)}, bf16[128,512]{1,0:T(8,128)(2,1)S(1)}, u32[]{:S(2)}, u32[]{:S(2)}) %collective-permute-start.11) | collective-permute-done | bytes 131104 | tf_op jit(solution)/shard_map/ppermute | solution.py:571
  93.1 6.7 %collective-permute-done.12 = bf16[128,512]{1,0:T(8,128)(2,1)S(1)} collective-permute-done((bf16[128,512]{1,0:T(8,128)(2,1)S(1)}, bf16[128,512]{1,0:T(8,128)(2,1)S(1)}, u32[]{:S(2)}, u32[]{:S(2)}) %collective-permute-start.12) | collective-permute-done | bytes 131104 | tf_op jit(solution)/shard_map/ppermute | solution.py:571
  99.8 1.9 %collective-permute-start.13 = (bf16[128,512]{1,0:T(8,128)(2,1)S(1)}, bf16[128,512]{1,0:T(8,128)(2,1)S(1)}, u32[]{:S(2)}, u32[]{:S(2)}) collective-permute-start(bf16[128,512]{1,0:T(8,128)(2,1)S(1)} %add_convert_fusion), channel_id=1, source_target_pairs={{0,1},{1,0},{2,3},{3,2},{4,5},{5,4},{6,7},{7,6},{8,9},{9,8},{10,11... | collective-permute-start | bytes 393224 | tf_op jit(solution)/shard_map/ppermute | solution.py:583
  101.7 3.9 %all-to-all-start.1 = ((bf16[8,128,512]{2,1,0:T(8,128)(2,1)}), bf16[8,128,512]{2,1,0:T(8,128)(2,1)S(1)}, u32[]{:S(2)}, u32[]{:S(2)}) async-start(bf16[8,128,512]{2,1,0:T(8,128)(2,1)} %get-tuple-element.56), calls=%async_computation.1 | async-start | bytes 2097152 | tf_op jit(solution)/shard_map/all_to_all | solution.py:647
  106.7 12.8 %local_back.1.b_ref = f32[2,1280,512]{2,1,0:T(8,128)} custom-call(s32[1]{0:T(128)} %bitcast.me_ref, s32[1]{0:T(128)S(6)} %copy.18.count_ref, s32[20]{0:T(128)S(1)} %copy-done.4, s32[20]{0:T(128)S(1)} %copy-done.5, s32[8]{0:T(128)S(1)} %copy-done.1, bf16[20,128,128]{2,1,0:T(8,128)(2,1)} %tiles_ref.7, bf16[2,1280,512]{2,1,0:T(8,128)(2,1)} %c_ref.9, ...), custom_call_target="tpu_custom_call" | custom-call | tf_op jit(solution)/shard_map/local_back/pallas_call | solution.py:266
  119.5 5.2 %finish.2.rest_0_ = bf16[2,1280,512]{2,1,0:T(8,128)(2,1)} custom-call(s32[8]{0:T(128)S(1)} %copy-done.2, s32[8]{0:T(128)S(1)} %copy-done.3, bf16[8,128,128]{2,1,0:T(8,128)(2,1)} %tiles_ref.9, bf16[8,128,512]{2,1,0:T(8,128)(2,1)S(1)} %all-to-all-done.r_ref, f32[2,1280,512]{2,1,0:T(8,128)} %local_back.1.b_ref), custom_call_target="tpu_custom_call" | custom-call | tf_op jit(solution)/shard_map/finish/pallas_call | solution.py:520
  124.9 1.8 %collective-permute-done.15 = bf16[2,2,128,512]{3,2,1,0:T(8,128)(2,1)S(1)} collective-permute-done((bf16[2,2,128,512]{3,2,1,0:T(8,128)(2,1)S(1)}, bf16[2,2,128,512]{3,2,1,0:T(8,128)(2,1)S(1)}, u32[]{:S(2)}, u32[]{:S(2)}) %collective-permute-start.15) | collective-permute-done | bytes 524320 | tf_op jit(solution)/shard_map/ppermute | solution.py:583
  129.3 2.0 %all-to-all-done.1.r_ref = bf16[8,128,512]{2,1,0:T(8,128)(2,1)S(1)} async-done(((bf16[8,128,512]{2,1,0:T(8,128)(2,1)}), bf16[8,128,512]{2,1,0:T(8,128)(2,1)S(1)}, u32[]{:S(2)}, u32[]{:S(2)}) %all-to-all-start.1) | async-done | bytes 1048608 | tf_op jit(solution)/shard_map/all_to_all | solution.py:647
  131.3 5.2 %finish.3 = bf16[2,1280,512]{2,1,0:T(8,128)(2,1)} custom-call(s32[8]{0:T(128)S(1)} %copy-done.2, s32[8]{0:T(128)S(1)} %copy-done.3, bf16[8,128,128]{2,1,0:T(8,128)(2,1)} %tiles_ref.9, bf16[8,128,512]{2,1,0:T(8,128)(2,1)S(1)} %all-to-all-done.1.r_ref, f32[2,1280,512]{2,1,0:T(8,128)} %local_back.1.b_ref, ...), custom_call_target="tpu_custom_call", output_to_operand_aliasing={{}: (5, {})} | custom-call | tf_op jit(solution)/shard_map/finish/pallas_call | solution.py:520
  (55 shorter events, 12.0 us)
Async XLA Ops:
  0.6 14.9 %copy-start = (s32[8]{0:T(128)S(1)}, s32[8]{0:T(128)}, u32[]{:S(2)}) copy-start(s32[8]{0:T(128)} %places_ref.1) | copy-start | bytes 100
  0.6 14.9 %copy-start.4 = (s32[20]{0:T(128)S(1)}, s32[20]{0:T(128)}, u32[]{:S(2)}) copy-start(s32[20]{0:T(128)} %rows_ref.5) | copy-start | bytes 244
  0.7 14.9 %copy-start.5 = (s32[20]{0:T(128)S(1)}, s32[20]{0:T(128)}, u32[]{:S(2)}) copy-start(s32[20]{0:T(128)} %cols_ref.5) | copy-start | bytes 244
  4.9 30.2 %collective-permute-start = (bf16[2,128,512]{2,1,0:T(8,128)(2,1)}, bf16[2,128,512]{2,1,0:T(8,128)(2,1)S(1)}, u32[]{:S(2)}, u32[]{:S(2)}) collective-permute-start(bf16[2,128,512]{2,1,0:T(8,128)(2,1)} %get-tuple-element.33), channel_id=1, source_target_pairs={{0,4},{1,5},{2,6},{3,7},{4,0},{5,1},{6,2},{7,3},{8,12},{9,13},{10,... | collective-permute-start | bytes 786440 | tf_op jit(solution)/shard_map/ppermute | solution.py:74
  9.0 26.1 %collective-permute-start.2 = (bf16[2,128,512]{2,1,0:T(8,128)(2,1)}, bf16[2,128,512]{2,1,0:T(8,128)(2,1)S(1)}, u32[]{:S(2)}, u32[]{:S(2)}) collective-permute-start(bf16[2,128,512]{2,1,0:T(8,128)(2,1)} %get-tuple-element.35), channel_id=1, source_target_pairs={{0,1},{1,0},{2,3},{3,2},{4,5},{5,4},{6,7},{7,6},{8,9},{9,8},{10,11... | collective-permute-start | bytes 786440 | tf_op jit(solution)/shard_map/ppermute | solution.py:74
  10.5 33.8 %collective-permute-start.1 = (bf16[2,128,512]{2,1,0:T(8,128)(2,1)}, bf16[2,128,512]{2,1,0:T(8,128)(2,1)S(1)}, u32[]{:S(2)}, u32[]{:S(2)}) collective-permute-start(bf16[2,128,512]{2,1,0:T(8,128)(2,1)} %get-tuple-element.34), channel_id=1, source_target_pairs={{0,5},{1,4},{2,7},{3,6},{4,1},{5,0},{6,3},{7,2},{8,13},{9,12},{10,... | collective-permute-start | bytes 786440 | tf_op jit(solution)/shard_map/ppermute | solution.py:74
  10.5 33.8 %collective-permute-start.3 = (bf16[2,128,512]{2,1,0:T(8,128)(2,1)}, bf16[2,128,512]{2,1,0:T(8,128)(2,1)S(1)}, u32[]{:S(2)}, u32[]{:S(2)}) collective-permute-start(bf16[2,128,512]{2,1,0:T(8,128)(2,1)} %get-tuple-element.36), channel_id=1, source_target_pairs={{0,2},{1,3},{2,0},{3,1},{4,6},{5,7},{6,4},{7,5},{8,10},{9,11},{10,... | collective-permute-start | bytes 786440 | tf_op jit(solution)/shard_map/ppermute | solution.py:74
  12.4 39.5 %collective-permute-start.4 = (bf16[2,128,512]{2,1,0:T(8,128)(2,1)}, bf16[2,128,512]{2,1,0:T(8,128)(2,1)S(1)}, u32[]{:S(2)}, u32[]{:S(2)}) collective-permute-start(bf16[2,128,512]{2,1,0:T(8,128)(2,1)} %get-tuple-element.39), channel_id=1, source_target_pairs={{0,6},{1,7},{2,4},{3,5},{4,2},{5,3},{6,0},{7,1},{8,14},{9,15},{10,... | collective-permute-start | bytes 786440 | tf_op jit(solution)/shard_map/ppermute | solution.py:74
  15.5 19.6 %copy-start.8 = (bf16[2,128,512]{2,1,0:T(8,128)(2,1)S(1)}, bf16[2,128,512]{2,1,0:T(8,128)(2,1)}, u32[]{:S(2)}) copy-start(bf16[2,128,512]{2,1,0:T(8,128)(2,1)} %get-tuple-element.41) | copy-start | bytes 786436
  15.5 21.9 %copy-start.7 = (bf16[2,128,512]{2,1,0:T(8,128)(2,1)S(1)}, bf16[2,128,512]{2,1,0:T(8,128)(2,1)}, u32[]{:S(2)}) copy-start(bf16[2,128,512]{2,1,0:T(8,128)(2,1)} %get-tuple-element.43) | copy-start | bytes 786436
  35.1 16.7 %collective-permute-start.5 = (bf16[2,128,512]{2,1,0:T(8,128)(2,1)S(1)}, bf16[2,128,512]{2,1,0:T(8,128)(2,1)S(1)}, u32[]{:S(2)}, u32[]{:S(2)}) collective-permute-start(bf16[2,128,512]{2,1,0:T(8,128)(2,1)S(1)} %copy-done.8), channel_id=1, source_target_pairs={{0,7},{1,6},{2,5},{3,4},{4,3},{5,2},{6,1},{7,0},{8,15},{9,14},{10,... | collective-permute-start | bytes 786440 | tf_op jit(solution)/shard_map/ppermute | solution.py:74
  37.5 14.4 %collective-permute-start.6 = (bf16[2,128,512]{2,1,0:T(8,128)(2,1)S(1)}, bf16[2,128,512]{2,1,0:T(8,128)(2,1)S(1)}, u32[]{:S(2)}, u32[]{:S(2)}) collective-permute-start(bf16[2,128,512]{2,1,0:T(8,128)(2,1)S(1)} %copy-done.7), channel_id=1, source_target_pairs={{0,3},{1,2},{2,1},{3,0},{4,7},{5,6},{6,5},{7,4},{8,11},{9,10},{10,... | collective-permute-start | bytes 786440 | tf_op jit(solution)/shard_map/ppermute | solution.py:74
  51.9 33.8 %all-to-all-start = ((bf16[8,128,512]{2,1,0:T(8,128)(2,1)}), bf16[8,128,512]{2,1,0:T(8,128)(2,1)S(1)}, u32[]{:S(2)}, u32[]{:S(2)}) async-start(bf16[8,128,512]{2,1,0:T(8,128)(2,1)} %get-tuple-element.54), calls=%async_computation | async-start | bytes 2097152 | tf_op jit(solution)/shard_map/all_to_all | solution.py:647
  64.3 13.3 %collective-permute-start.9 = (bf16[256,512]{1,0:T(8,128)(2,1)}, bf16[256,512]{1,0:T(8,128)(2,1)S(1)}, u32[]{:S(2)}, u32[]{:S(2)}) collective-permute-start(bf16[256,512]{1,0:T(8,128)(2,1)} %get-tuple-element.52), channel_id=1, source_target_pairs={{0,24},{8,0},{16,8},{24,16},{1,25},{9,1},{17,9},{25,17},{2,26},{10... | collective-permute-start | bytes 786440 | tf_op jit(solution)/shard_map/ppermute | solution.py:656
  65.3 13.6 %collective-permute-start.8 = (bf16[256,512]{1,0:T(8,128)(2,1)}, bf16[256,512]{1,0:T(8,128)(2,1)S(1)}, u32[]{:S(2)}, u32[]{:S(2)}) collective-permute-start(bf16[256,512]{1,0:T(8,128)(2,1)} %get-tuple-element.51), channel_id=1, source_target_pairs={{0,16},{8,24},{16,0},{24,8},{1,17},{9,25},{17,1},{25,9},{2,18},{10... | collective-permute-start | bytes 786440 | tf_op jit(solution)/shard_map/ppermute | solution.py:656
  66.0 12.9 %collective-permute-start.7 = (bf16[256,512]{1,0:T(8,128)(2,1)}, bf16[256,512]{1,0:T(8,128)(2,1)S(1)}, u32[]{:S(2)}, u32[]{:S(2)}) collective-permute-start(bf16[256,512]{1,0:T(8,128)(2,1)} %get-tuple-element.49), channel_id=1, source_target_pairs={{0,8},{8,16},{16,24},{24,0},{1,9},{9,17},{17,25},{25,1},{2,10},{10... | collective-permute-start | bytes 786440 | tf_op jit(solution)/shard_map/ppermute | solution.py:656
  79.1 6.4 %collective-permute-start.10 = (bf16[128,512]{1,0:T(8,128)(2,1)S(1)}, bf16[128,512]{1,0:T(8,128)(2,1)S(1)}, u32[]{:S(2)}, u32[]{:S(2)}) collective-permute-start(bf16[128,512]{1,0:T(8,128)(2,1)S(1)} %fusion), channel_id=1, source_target_pairs={{0,1},{1,0},{2,3},{3,2},{4,5},{5,4},{6,7},{7,6},{8,9},{9,8},{10,11... | collective-permute-start | bytes 393224 | tf_op jit(solution)/shard_map/ppermute | solution.py:557
  85.7 5.6 %collective-permute-start.11 = (bf16[128,512]{1,0:T(8,128)(2,1)S(1)}, bf16[128,512]{1,0:T(8,128)(2,1)S(1)}, u32[]{:S(2)}, u32[]{:S(2)}) collective-permute-start(bf16[128,512]{1,0:T(8,128)(2,1)S(1)} %bitcast_add_fusion), channel_id=1, source_target_pairs={{0,2},{1,3},{2,0},{3,1},{4,6},{5,7},{6,4},{7,5},{8,10},{9,11},{10,... | collective-permute-start | bytes 393224 | tf_op jit(solution)/shard_map/ppermute | solution.py:571
  91.3 8.5 %collective-permute-start.12 = (bf16[128,512]{1,0:T(8,128)(2,1)S(1)}, bf16[128,512]{1,0:T(8,128)(2,1)S(1)}, u32[]{:S(2)}, u32[]{:S(2)}) collective-permute-start(bf16[128,512]{1,0:T(8,128)(2,1)S(1)} %add_convert_fusion.1), channel_id=1, source_target_pairs={{0,4},{1,5},{2,6},{3,7},{4,0},{5,1},{6,2},{7,3},{8,12},{9,13},{10,... | collective-permute-start | bytes 393224 | tf_op jit(solution)/shard_map/ppermute | solution.py:571
  99.8 5.8 %collective-permute-start.13 = (bf16[128,512]{1,0:T(8,128)(2,1)S(1)}, bf16[128,512]{1,0:T(8,128)(2,1)S(1)}, u32[]{:S(2)}, u32[]{:S(2)}) collective-permute-start(bf16[128,512]{1,0:T(8,128)(2,1)S(1)} %add_convert_fusion), channel_id=1, source_target_pairs={{0,1},{1,0},{2,3},{3,2},{4,5},{5,4},{6,7},{7,6},{8,9},{9,8},{10,11... | collective-permute-start | bytes 393224 | tf_op jit(solution)/shard_map/ppermute | solution.py:583
  101.7 29.5 %all-to-all-start.1 = ((bf16[8,128,512]{2,1,0:T(8,128)(2,1)}), bf16[8,128,512]{2,1,0:T(8,128)(2,1)S(1)}, u32[]{:S(2)}, u32[]{:S(2)}) async-start(bf16[8,128,512]{2,1,0:T(8,128)(2,1)} %get-tuple-element.56), calls=%async_computation.1 | async-start | bytes 2097152 | tf_op jit(solution)/shard_map/all_to_all | solution.py:647
  105.7 19.0 %collective-permute-start.14 = (bf16[2,128,512]{2,1,0:T(8,128)(2,1)S(1)}, bf16[2,128,512]{2,1,0:T(8,128)(2,1)S(1)}, u32[]{:S(2)}, u32[]{:S(2)}) collective-permute-start(bf16[2,128,512]{2,1,0:T(8,128)(2,1)S(1)} %get-tuple-element.63), channel_id=1, source_target_pairs={{0,16},{8,24},{16,0},{24,8},{1,17},{9,25},{17,1},{25,9},{2,18},{10... | collective-permute-start | bytes 786440 | tf_op jit(solution)/shard_map/ppermute | solution.py:583
  106.7 12.8 %copy-start.3 = (s32[8]{0:T(128)S(1)}, s32[8]{0:T(128)}, u32[]{:S(2)}) copy-start(s32[8]{0:T(128)} %live_ref.3) | copy-start | bytes 100
  124.8 2.0 %collective-permute-start.15 = (bf16[2,2,128,512]{3,2,1,0:T(8,128)(2,1)S(1)}, bf16[2,2,128,512]{3,2,1,0:T(8,128)(2,1)S(1)}, u32[]{:S(2)}, u32[]{:S(2)}) collective-permute-start(bf16[2,2,128,512]{3,2,1,0:T(8,128)(2,1)S(1)} %pad_maximum_fusion.1), channel_id=1, source_target_pairs={{0,8},{8,0},{16,24},{24,16},{1,9},{9,1},{17,25},{25,17},{2,10},{10... | collective-permute-start | bytes 1572872 | tf_op jit(solution)/shard_map/ppermute | solution.py:583
  (3 other events, 18.8 us)

commit v4 on v3

--- a/solution.py
+++ b/solution.py
@@ -287,7 +287,7 @@
     steps, _, width = features.shape
     count = len(shifts)
     most = 3
-    summed = sums is not None
+    summed = True
 
     def body(me_ref, rows_in, f_ref, c_ref, wv_ref, wg_ref, *rest):
         parts, rest = rest[:count], rest[count:]
@@ -369,95 +369,79 @@
     )(me, *operands)
 
 
-def prepare_late(me, rows, features, grad, w_gate, shifts, n, tile):
+def add_late(me, sums, arrived, rows, features, grad, w_value, w_gate, shifts, n, tile, place, level, wire):
     steps, _, width = features.shape
     count = len(shifts)
-
-    def body(me_ref, rows_in, f_ref, c_ref, w_ref, half_ref, u_ref, f_buf, c_buf, sem, rows_ref, id_sem):
-        load_ids((rows_in,), (rows_ref,), id_sem)
-        loads = []
+    size = level[2]
+    lines = 2 * width // size
+
+    def body(me_ref, place_ref, rows_in, f_ref, c_ref, wv_ref, wg_ref, s_ref, *rest):
+        parts, (keep_ref, *send_refs), made_ref, rest = rest[:count], rest[count : count + size], rest[count + size], rest[count + size + 1 :]
+        p_buf, f_buf, c_buf, w_buf, total, wired, made, sem, w_sem, done_sem, rows_ref, id_sem = rest
+        ids = id_copies((rows_in,), (rows_ref,), id_sem)
+        first = [pltpu.make_async_copy(ref, w_buf.at[i], w_sem.at[i]) for i, ref in enumerate((wg_ref, wv_ref))]
+        first += [pltpu.make_async_copy(parts[j], p_buf.at[j], sem.at[0, j]) for j in range(count)]
+        old = pltpu.make_async_copy(s_ref, total, w_sem.at[2])
+        for load in first:
+            load.start()
+        ids[0].wait()
+        then = []
         for j, shift in enumerate(shifts):
             at = pl.ds(pl.multiple_of(rows_ref[source_of(me_ref[0], shift, n)] * tile, tile), tile)
-            loads.append(pltpu.make_async_copy(f_ref.at[:, at, :], f_buf.at[j], sem.at[0, j]))
-            loads.append(pltpu.make_async_copy(c_ref.at[:, at, :], c_buf.at[j], sem.at[1, j]))
-        for load in loads:
+            then.append(pltpu.make_async_copy(f_ref.at[:, at, :], f_buf.at[j], sem.at[1, j]))
+            then.append(pltpu.make_async_copy(c_ref.at[:, at, :], c_buf.at[j], sem.at[2, j]))
+        for load in then:
             load.start()
-        for load in loads:
+        old.start()
+        for load in first + then:
             load.wait()
-        f = flat_rows(f_buf[...])
-        gate = jax.nn.sigmoid(mm(f, w_ref[...]))
-        dagg = flat_rows(c_buf[...]).astype(F32) * gate
-        half_ref[0] = f
-        half_ref[1] = dagg.astype(BF16)
-        u_ref[...] = dagg * (1.0 - gate)
+        p, f, c = [flat_rows(buf[...]) for buf in (p_buf, f_buf, c_buf)]
+        kept, dagg, dgate = gate_terms(f, c, p, w_buf[1], w_buf[0])
+        value = mm_tn(p, dagg)
+        gate = mm_tn(f, dgate)
+        old.wait()
+        total[:width, :] += value
+        total[width:, :] += gate
+        wired[...] = total[...].astype(wire)
+        stores = []
+        for i, (source, to) in enumerate([(total, keep_ref)] + [(wired, ref) for ref in send_refs]):
+            mine = pl.ds(pl.multiple_of(lax.rem(place_ref[0] + i, size) * lines, lines), lines)
+            stores.append(pltpu.make_async_copy(source.at[mine, :], to, done_sem.at[i]))
+            stores[-1].start()
+        shape = (count, steps, tile, width)
+        made[:, 0] = kept.astype(BF16).reshape(shape)
+        made[:, 1] = dgate.reshape(shape)
+        stores.append(pltpu.make_async_copy(made, made_ref, done_sem.at[size]))
+        stores[-1].start()
+        for store in stores:
+            store.wait()
 
     many = pltpu.VMEM((count, steps, tile, width), BF16)
-    lines = count * steps * tile
+    pair = (count, 2, steps, tile, width)
     return pl.pallas_call(
         body,
-        out_shape=[pltpu.HBM((2, lines, width), BF16), pltpu.HBM((lines, width), F32)],
-        in_specs=[SMEM, ANY, ANY, ANY, VMEM],
-        out_specs=[VMEM, VMEM],
-        scratch_shapes=[many, many, pltpu.SemaphoreType.DMA((2, count))] + id_memory(n, 1),
-        compiler_params=params(),
-        cost_estimate=cost(0, 0),
-        name="prepare_late",
-    )(me, *far_memory(rows, features, grad, w_gate))
-
-
-def add_late(sums, arrived, half, u, w_value, place, level, wire):
-    steps, tile, width = arrived[0].shape
-    count = len(arrived)
-    size = level[2]
-    lines = 2 * width // size
-
-    def body(place_ref, s_ref, half_ref, u_ref, w_ref, *rest):
-        parts, (keep_ref, *send_refs), rest = rest[:count], rest[count : count + size], rest[count + size :]
-        p_buf, w_buf, h_buf, u_buf, total, made, sem, done_sem = rest
-        first = [pltpu.make_async_copy(parts[j], p_buf.at[j], sem.at[4 + j]) for j in range(count)]
-        first += [pltpu.make_async_copy(ref, buf, sem.at[i]) for i, (ref, buf) in enumerate(((w_ref, w_buf), (half_ref, h_buf)))]
-        later = [pltpu.make_async_copy(ref, buf, sem.at[2 + i]) for i, (ref, buf) in enumerate(((u_ref, u_buf), (s_ref, total)))]
-        for load in first + later:
-            load.start()
-        for load in first:
-            load.wait()
-        p = flat_rows(p_buf[...])
-        agg = mm(p, w_buf[...])
-        value = mm_tn(p, h_buf[1])
-        later[0].wait()
-        gate = mm_tn(h_buf[0], (agg * u_buf[...]).astype(BF16))
-        later[1].wait()
-        total[:width, :] += value
-        total[width:, :] += gate
-        made[...] = total[...].astype(wire)
-        stores = []
-        for i, (source, to) in enumerate([(total, keep_ref)] + [(made, ref) for ref in send_refs]):
-            mine = pl.ds(pl.multiple_of(lax.rem(place_ref[0] + i, size) * lines, lines), lines)
-            stores.append(pltpu.make_async_copy(source.at[mine, :], to, done_sem.at[i]))
-        for store in stores:
-            store.start()
-        for store in stores:
-            store.wait()
-
-    return pl.pallas_call(
-        body,
-        out_shape=[pltpu.HBM((lines, width), F32)] + [pltpu.HBM((lines, width), wire)] * (size - 1),
-        in_specs=[SMEM] + [ANY] * (4 + count),
-        out_specs=[ANY] * size,
+        out_shape=[pltpu.HBM((lines, width), F32)]
+        + [pltpu.HBM((lines, width), wire)] * (size - 1)
+        + [pltpu.HBM(pair, BF16)],
+        in_specs=[SMEM, SMEM] + [ANY] * (6 + count),
+        out_specs=[ANY] * (size + 1),
         scratch_shapes=[
-            pltpu.VMEM((count, steps, tile, width), BF16),
-            pltpu.VMEM((width, width), BF16),
-            pltpu.VMEM(half.shape, BF16),
-            pltpu.VMEM(u.shape, F32),
+            many,
+            many,
+            many,
+            pltpu.VMEM((2, width, width), BF16),
             pltpu.VMEM((2 * width, width), F32),
             pltpu.VMEM((2 * width, width), wire),
-            pltpu.SemaphoreType.DMA((4 + count,)),
-            pltpu.SemaphoreType.DMA((size,)),
-        ],
+            pltpu.VMEM(pair, BF16),
+            pltpu.SemaphoreType.DMA((3, count)),
+            pltpu.SemaphoreType.DMA((3,)),
+            pltpu.SemaphoreType.DMA((size + 1,)),
+        ]
+        + id_memory(n, 1),
         compiler_params=params(),
         cost_estimate=cost(0, 0),
         name="add_late",
-    )(place, *far_memory(sums.reshape(2 * width, width), half, u, w_value), *arrived)
+    )(me, place, *far_memory(rows, features, grad, w_value, w_gate, sums.reshape(2 * width, width)), *arrived)
 
 
 def settle(me, kept, features, made, rows, groups, n, tile):
@@ -619,7 +603,7 @@
     flat = features.reshape(-1, width)
     grad = cotangent.reshape(-1, width)
 
-    far = list(range(n // 2, n))
+    far = list(range(n // 2, n))[::-1]
     near = list(range(1, n // 2))
     shifts = far + near
     lead = max(1, len(far) - 1)
@@ -634,27 +618,25 @@
     kept, dgate, back, sums, *owed = local_forward(*graph, features, cotangent, *weights, remote_rows)
     for s in second:
         came[s] = exchange(after(sent[s], sums, came[far[0]], came[near[0]]), s, n)
-    half_late, u_late = prepare_late(me, remote_rows, features, cotangent, w_gate, late, n, tile)
     made_early, sums = add_arrived(
         me, sums, [came[s] for s in early], remote_rows, features, cotangent, *weights, early, n, tile
     )
     pair, column, row, line = levels(tm, n)
     whole = ("tm", 1, tm, tm)
     place = member(whole).astype(jnp.int32).reshape(1)
-    keep, *sends = add_late(sums, [came[s] for s in late], half_late, u_late, w_value, place, whole, BF16)
+    keep, *sends, made_late = add_late(
+        me, sums, [came[s] for s in late], remote_rows, features, cotangent, *weights, late, n, tile, place, whole, BF16
+    )
 
     def send_back(t, *before):
         return lax.all_to_all(after(owed[t], *before), "asset", 0, 0, tiled=True)
 
-    returned = [send_back(t, made_early, half_late, *[came[s] for s in late]) for t in range(steps // 2)]
-    (made_late,) = add_arrived(
-        me, None, [came[s] for s in late], remote_rows, features, cotangent, *weights, late, n, tile
-    )
+    returned = [send_back(t, made_early, *[came[s] for s in late]) for t in range(steps // 2)]
     made, groups = (made_early, made_late), (early, late)
     output = settle(me, kept, features, made, remote_rows, groups, n, tile)
     base = local_back(me, *graph, back, cotangent, dgate, made, remote_rows, groups, w_gate, n)
     terms = [keep] + [lax.ppermute(x, "tm", pairs_of(whole, i + 1)) for i, x in enumerate(sends)]
-    terms[1] = after(terms[1], made_late, output)
+    terms[1] = after(terms[1], base)
     shape = (row[2], keep.shape[0] // row[2], width)
     terms = [x.astype(F32).reshape(shape) for x in terms]
     sums = after(scatter_sum(terms, row, BF16), *returned)
@@ -671,7 +653,7 @@
     sums = jnp.stack(spread(sums, row))
     sums = jnp.stack(spread(sums, column))
     if grad_features is not None:
-        sums = after(sums, grad_features)
+        sums = after(sums, grad_features, output)
     sums = jnp.stack(spread(sums, pair))
     scale = float(steps * assets * tm * n) ** (-0.5)
     sums = unshuffle(sums, [pair, column, row], [column, pair, row], (2, width, width)) * scale

time: 137 us -> 134 us (0.978)
  Pallas kernels: 75.9 us -> 67.7 us
  waiting for transfers between devices: 21 us -> 27.1 us
    ppermute x7, waiting for transfers between devices: 1.42 us -> 10.7 us  [exchange(): lax.ppermute(block, 'asset', [(i, target_of(i, shift, n)) for i in range(...]
    pallas_call x1 -> x0, Pallas kernels: 5.45 us -> none  [prepare_late(): pl.pallas_call(body, out_shape=[pltpu.HBM((2, lines, width), BF16), pltpu...]
    pallas_call x2 -> x1, Pallas kernels: 12.1 us -> 7.38 us  [add_arrived(): pl.pallas_call(body, out_shape=out_shape, in_specs=[SMEM] + [ANY] * len(o...]
    all_to_all x2, starting transfers between devices: 11.8 us -> 7.35 us  [send_back(): return lax.all_to_all(after(owed[t], *before), 'asset', 0, 0, tiled=True)]
    ppermute x2, waiting for transfers between devices: 10.2 us -> 6.48 us  [butterfly_sum(): lax.ppermute(x, axis, [(i, i ^ shift * level[1]) for i in range(level[3])])]
    ppermute x3, waiting for transfers between devices: 1.82 us -> 5.36 us  [spread(): lax.ppermute(x, axis, pairs_of(level, s))]
    pallas_call x1, Pallas kernels: 4.6 us -> 6.45 us  [add_late(): pl.pallas_call(body, out_shape=[pltpu.HBM((lines, width), F32)] + [pltpu....]
    ppermute x1, waiting for transfers between devices: 4.35 us -> 2.95 us  [scatter_sum(): lax.ppermute(entry((me + s) % size).astype(wire), axis, pairs_of(level, s))]
  transfers between devices with their start and end apart: 18 -> 18, of which waited for: 7 -> 8; matrix products, arithmetic and copies ran while one was open for 2% -> 2% of each run, Pallas kernels for 49% -> 44%
where the time goes in v4:
time: 134 us; the launch traced here: 133 us
  Pallas kernels  67.7 us (51%)
  starting transfers between devices  33.7 us (25%)
  waiting for transfers between devices  27.1 us (20%)
  local copies, waits for them, and re-layouts  2.22 us (2%)
  between operations  1.65 us (1%)
    pallas_call x1, Pallas kernels, local_forward(): pl.pallas_call(body, grid=(steps, turns), out_shape=[pltpu.HBM(features.s...  19.6 us
    pallas_call x1, Pallas kernels, local_back(): pl.pallas_call(body, grid=(steps, assets // chunk), out_shape=pltpu.HBM(b...  13.1 us
    ppermute x7, starting transfers between devices, exchange(): lax.ppermute(block, 'asset', [(i, target_of(i, shift, n)) for i in range(...  12.6 us
    ppermute x7, waiting for transfers between devices, exchange(): lax.ppermute(block, 'asset', [(i, target_of(i, shift, n)) for i in range(...  10.7 us
    pallas_call x2, Pallas kernels, finish(): pl.pallas_call(body, grid=(blocks // per,), out_shape=pltpu.HBM((steps, a...  10.4 us
    pallas_call x1, Pallas kernels, add_arrived(): pl.pallas_call(body, out_shape=out_shape, in_specs=[SMEM] + [ANY] * len(o...  7.38 us
    all_to_all x2, starting transfers between devices, send_back(): return lax.all_to_all(after(owed[t], *before), 'asset', 0, 0, tiled=True)  7.35 us
    pallas_call x1, Pallas kernels, settle(): pl.pallas_call(body, grid=(blocks // per,), out_shape=pltpu.HBM((steps, a...  6.59 us
  transfers between devices with their start and end apart: 18, of which 8 were waited for; matrix products, arithmetic and copies ran while one was open for 2% of the time, Pallas kernels for 44%

profile of v4, /device:TPU:0, one launch (start us, length us, event | category | flops | bytes accessed | tf_op | source)
XLA Modules:
  0.0 133.4 jit_solution(6469025114090114466)
XLA Ops:
  0.7 4.2 %send_forward.1 = (bf16[2,128,512]{2,1,0:T(8,128)(2,1)}, bf16[2,128,512]{2,1,0:T(8,128)(2,1)}, bf16[2,128,512]{2,1,0:T(8,128)(2,1)}, bf16[2,128,512]{2,1,0:T(8,1...) custom-call(s32[1]{0:T(128)} %bitcast.me_ref, s32[8]{0:T(128)} %cols_ref.7, ...), custom_call_target="tpu_custom_call" | custom-call | flops 234881024 | bytes 3670016 | tf_op jit(solution)/shard_map/send_forward/pallas_call | solution.py:115
  4.9 6.0 %collective-permute-start = (bf16[2,128,512]{2,1,0:T(8,128)(2,1)}, bf16[2,128,512]{2,1,0:T(8,128)(2,1)S(1)}, u32[]{:S(2)}, u32[]{:S(2)}) collective-permute-start(bf16[2,128,512]{2,1,0:T(8,128)(2,1)} %get-tuple-element.32), channel_id=1, source_target_pairs={{0,7},{1,6},{2,5},{3,4},{4,3},{5,2},{6,1},{7,0},{8,15},{9,14},{10,... | collective-permute-start | bytes 786440 | tf_op jit(solution)/shard_map/ppermute | solution.py:74
  11.6 5.2 %collective-permute-start.4 = (bf16[2,128,512]{2,1,0:T(8,128)(2,1)}, bf16[2,128,512]{2,1,0:T(8,128)(2,1)S(1)}, u32[]{:S(2)}, u32[]{:S(2)}) collective-permute-start(bf16[2,128,512]{2,1,0:T(8,128)(2,1)} %get-tuple-element.39), channel_id=1, source_target_pairs={{0,5},{1,4},{2,7},{3,6},{4,1},{5,0},{6,3},{7,2},{8,13},{9,12},{10,... | collective-permute-start | bytes 786440 | tf_op jit(solution)/shard_map/ppermute | solution.py:74
  17.5 19.6 %local_forward.1 = (bf16[2,1280,512]{2,1,0:T(8,128)(2,1)}, bf16[2,1280,512]{2,1,0:T(8,128)(2,1)}, bf16[2,1280,512]{2,1,0:T(8,128)(2,1)}, f32[2,512,512]{2,1,0:T(...) custom-call(s32[1]{0:T(128)S(6)} %copy.18.count_ref, s32[20]{0:T(128)S(1)} %copy-done.4, ...), custom_call_target="tpu_custom_call" | custom-call | tf_op jit(solution)/shard_map/local_forward/pallas_call | solution.py:206
  37.8 7.4 %add_arrived.1 = (bf16[4,2,2,128,512]{4,3,2,1,0:T(8,128)(2,1)}, f32[2,512,512]{2,1,0:T(8,128)}) custom-call(s32[1]{0:T(128)} %bitcast.me_ref, s32[8]{0:T(128)} %places_ref.1, bf16[2,1280,512]{2,1,0:T(8,128)(2,1)} %f_ref.7, bf16[2,1280,512]{2,1,0:T(8,128)(2,1)} %c_ref.7, bf16[512,512]{1,0:T(8,128)(2,1)} %wv_ref.5, bf16[512,512]{1,0:T(8,128)(2,1)} %w_ref.1, ...), custom_call_target="tpu_custom_call" | custom-call | tf_op jit(solution)/shard_map/add_arrived/pallas_call | solution.py:349
  45.2 6.0 %collective-permute-done.4.rest_0_ = bf16[2,128,512]{2,1,0:T(8,128)(2,1)S(1)} collective-permute-done((bf16[2,128,512]{2,1,0:T(8,128)(2,1)}, bf16[2,128,512]{2,1,0:T(8,128)(2,1)S(1)}, u32[]{:S(2)}, u32[]{:S(2)}) %collective-permute-start.4) | collective-permute-done | bytes 262176 | tf_op jit(solution)/shard_map/ppermute | solution.py:74
  51.3 4.7 %collective-permute-done.5.rest_1_ = bf16[2,128,512]{2,1,0:T(8,128)(2,1)S(1)} collective-permute-done((bf16[2,128,512]{2,1,0:T(8,128)(2,1)S(1)}, bf16[2,128,512]{2,1,0:T(8,128)(2,1)S(1)}, u32[]{:S(2)}, u32[]{:S(2)}) %collective-permute-start.5) | collective-permute-done | bytes 262176 | tf_op jit(solution)/shard_map/ppermute | solution.py:74
  56.0 3.8 %all-to-all-start = ((bf16[8,128,512]{2,1,0:T(8,128)(2,1)}), bf16[8,128,512]{2,1,0:T(8,128)(2,1)S(1)}, u32[]{:S(2)}, u32[]{:S(2)}) async-start(bf16[8,128,512]{2,1,0:T(8,128)(2,1)} %get-tuple-element.54), calls=%async_computation | async-start | bytes 2097152 | tf_op jit(solution)/shard_map/all_to_all | solution.py:632
  59.7 6.5 %add_late.1 = (f32[256,512]{1,0:T(8,128)}, bf16[256,512]{1,0:T(8,128)(2,1)}, bf16[256,512]{1,0:T(8,128)(2,1)}, bf16[256,512]{1,0:T(8,128)(2,1)}, bf16[3,2,2,128,512]{4,3,2,1,0:T(8,128)(2,1)}) custom-call(s32[1]{0:T(128)} %bitcast.me_ref, s32[1]{0:T(128)} %bitcast.1.place_ref, s32[8]{0:T(128)} %places_ref.1, bf16[2,1280,512]{2,1,0:T(8,128)(2,1)} %f_ref.7, ...), custom_call_target="tpu_custom_call" | custom-call | tf_op jit(solution)/shard_map/add_late/pallas_call | solution.py:421
  69.3 13.1 %local_back.1.b_ref = f32[2,1280,512]{2,1,0:T(8,128)} custom-call(s32[1]{0:T(128)} %bitcast.me_ref, s32[1]{0:T(128)S(6)} %copy.18.count_ref, s32[20]{0:T(128)S(1)} %copy-done.4, s32[20]{0:T(128)S(1)} %copy-done.5, s32[8]{0:T(128)S(1)} %copy-done.1, bf16[20,128,128]{2,1,0:T(8,128)(2,1)} %tiles_ref.7, bf16[2,1280,512]{2,1,0:T(8,128)(2,1)} %c_ref.7, ...), custom_call_target="tpu_custom_call" | custom-call | tf_op jit(solution)/shard_map/local_back/pallas_call | solution.py:266
  82.7 2.2 %collective-permute-start.10 = (bf16[128,512]{1,0:T(8,128)(2,1)S(1)}, bf16[128,512]{1,0:T(8,128)(2,1)S(1)}, u32[]{:S(2)}, u32[]{:S(2)}) collective-permute-start(bf16[128,512]{1,0:T(8,128)(2,1)S(1)} %fusion), channel_id=1, source_target_pairs={{0,1},{1,0},{2,3},{3,2},{4,5},{5,4},{6,7},{7,6},{8,9},{9,8},{10,11... | collective-permute-start | bytes 393224 | tf_op jit(solution)/shard_map/ppermute | solution.py:541
  84.9 2.9 %collective-permute-done.10 = bf16[128,512]{1,0:T(8,128)(2,1)S(1)} collective-permute-done((bf16[128,512]{1,0:T(8,128)(2,1)S(1)}, bf16[128,512]{1,0:T(8,128)(2,1)S(1)}, u32[]{:S(2)}, u32[]{:S(2)}) %collective-permute-start.10) | collective-permute-done | bytes 131104 | tf_op jit(solution)/shard_map/ppermute | solution.py:541
  87.9 2.2 %collective-permute-start.11 = (bf16[128,512]{1,0:T(8,128)(2,1)S(1)}, bf16[128,512]{1,0:T(8,128)(2,1)S(1)}, u32[]{:S(2)}, u32[]{:S(2)}) collective-permute-start(bf16[128,512]{1,0:T(8,128)(2,1)S(1)} %bitcast_add_fusion), channel_id=1, source_target_pairs={{0,2},{1,3},{2,0},{3,1},{4,6},{5,7},{6,4},{7,5},{8,10},{9,11},{10,... | collective-permute-start | bytes 393224 | tf_op jit(solution)/shard_map/ppermute | solution.py:555
  90.1 2.9 %collective-permute-done.11 = bf16[128,512]{1,0:T(8,128)(2,1)S(1)} collective-permute-done((bf16[128,512]{1,0:T(8,128)(2,1)S(1)}, bf16[128,512]{1,0:T(8,128)(2,1)S(1)}, u32[]{:S(2)}, u32[]{:S(2)}) %collective-permute-start.11) | collective-permute-done | bytes 131104 | tf_op jit(solution)/shard_map/ppermute | solution.py:555
  93.1 2.4 %collective-permute-start.12 = (bf16[128,512]{1,0:T(8,128)(2,1)S(1)}, bf16[128,512]{1,0:T(8,128)(2,1)S(1)}, u32[]{:S(2)}, u32[]{:S(2)}) collective-permute-start(bf16[128,512]{1,0:T(8,128)(2,1)S(1)} %add_convert_fusion.1), channel_id=1, source_target_pairs={{0,4},{1,5},{2,6},{3,7},{4,0},{5,1},{6,2},{7,3},{8,12},{9,13},{10,... | collective-permute-start | bytes 393224 | tf_op jit(solution)/shard_map/ppermute | solution.py:555
  95.5 3.5 %collective-permute-done.12 = bf16[128,512]{1,0:T(8,128)(2,1)S(1)} collective-permute-done((bf16[128,512]{1,0:T(8,128)(2,1)S(1)}, bf16[128,512]{1,0:T(8,128)(2,1)S(1)}, u32[]{:S(2)}, u32[]{:S(2)}) %collective-permute-start.12) | collective-permute-done | bytes 131104 | tf_op jit(solution)/shard_map/ppermute | solution.py:555
  99.1 3.8 %collective-permute-start.13 = (bf16[128,512]{1,0:T(8,128)(2,1)S(1)}, bf16[128,512]{1,0:T(8,128)(2,1)S(1)}, u32[]{:S(2)}, u32[]{:S(2)}) collective-permute-start(bf16[128,512]{1,0:T(8,128)(2,1)S(1)} %add_convert_fusion), channel_id=1, source_target_pairs={{0,1},{1,0},{2,3},{3,2},{4,5},{5,4},{6,7},{7,6},{8,9},{9,8},{10,11... | collective-permute-start | bytes 393224 | tf_op jit(solution)/shard_map/ppermute | solution.py:567
  102.9 3.6 %all-to-all-start.1 = ((bf16[8,128,512]{2,1,0:T(8,128)(2,1)}), bf16[8,128,512]{2,1,0:T(8,128)(2,1)S(1)}, u32[]{:S(2)}, u32[]{:S(2)}) async-start(bf16[8,128,512]{2,1,0:T(8,128)(2,1)} %get-tuple-element.56), calls=%async_computation.1 | async-start | bytes 2097152 | tf_op jit(solution)/shard_map/all_to_all | solution.py:632
  106.5 3.5 %collective-permute-done.13 = bf16[128,512]{1,0:T(8,128)(2,1)S(1)} collective-permute-done((bf16[128,512]{1,0:T(8,128)(2,1)S(1)}, bf16[128,512]{1,0:T(8,128)(2,1)S(1)}, u32[]{:S(2)}, u32[]{:S(2)}) %collective-permute-start.13) | collective-permute-done | bytes 131104 | tf_op jit(solution)/shard_map/ppermute | solution.py:567
  110.1 6.6 %settle.1 = bf16[2,1280,512]{2,1,0:T(8,128)(2,1)} custom-call(s32[1]{0:T(128)} %bitcast.me_ref, s32[8]{0:T(128)S(1)} %copy-done.1, bf16[2,1280,512]{2,1,0:T(8,128)(2,1)} %get-tuple-element.31.k_ref, bf16[2,1280,512]{2,1,0:T(8,128)(2,1)} %f_ref.7, bf16[4,2,2,128,512]{4,3,2,1,0:T(8,128)(2,1)} %get-tuple-element.37.rest_0_, ...), custom_call_target="tpu_custom_call" | custom-call | tf_op jit(solution)/shard_map/settle/pallas_call | solution.py:469
  116.7 5.2 %finish.2.rest_0_ = bf16[2,1280,512]{2,1,0:T(8,128)(2,1)} custom-call(s32[8]{0:T(128)S(1)} %copy-done.2, s32[8]{0:T(128)S(1)} %copy-done.3, bf16[8,128,128]{2,1,0:T(8,128)(2,1)} %tiles_ref.9, bf16[8,128,512]{2,1,0:T(8,128)(2,1)S(1)} %all-to-all-done.r_ref, f32[2,1280,512]{2,1,0:T(8,128)} %local_back.1.b_ref), custom_call_target="tpu_custom_call" | custom-call | tf_op jit(solution)/shard_map/finish/pallas_call | solution.py:504
  122.2 1.8 %collective-permute-done.15 = bf16[2,2,128,512]{3,2,1,0:T(8,128)(2,1)S(1)} collective-permute-done((bf16[2,2,128,512]{3,2,1,0:T(8,128)(2,1)S(1)}, bf16[2,2,128,512]{3,2,1,0:T(8,128)(2,1)S(1)}, u32[]{:S(2)}, u32[]{:S(2)}) %collective-permute-start.15) | collective-permute-done | bytes 524320 | tf_op jit(solution)/shard_map/ppermute | solution.py:567
  126.6 1.6 %all-to-all-done.1.r_ref = bf16[8,128,512]{2,1,0:T(8,128)(2,1)S(1)} async-done(((bf16[8,128,512]{2,1,0:T(8,128)(2,1)}), bf16[8,128,512]{2,1,0:T(8,128)(2,1)S(1)}, u32[]{:S(2)}, u32[]{:S(2)}) %all-to-all-start.1) | async-done | bytes 1048608 | tf_op jit(solution)/shard_map/all_to_all | solution.py:632
  128.2 5.2 %finish.3 = bf16[2,1280,512]{2,1,0:T(8,128)(2,1)} custom-call(s32[8]{0:T(128)S(1)} %copy-done.2, s32[8]{0:T(128)S(1)} %copy-done.3, bf16[8,128,128]{2,1,0:T(8,128)(2,1)} %tiles_ref.9, bf16[8,128,512]{2,1,0:T(8,128)(2,1)S(1)} %all-to-all-done.1.r_ref, f32[2,1280,512]{2,1,0:T(8,128)} %local_back.1.b_ref, ...), custom_call_target="tpu_custom_call", output_to_operand_aliasing={{}: (5, {})} | custom-call | tf_op jit(solution)/shard_map/finish/pallas_call | solution.py:504
  (53 shorter events, 7.7 us)
Async XLA Ops:
  0.6 16.8 %copy-start = (s32[8]{0:T(128)S(1)}, s32[8]{0:T(128)}, u32[]{:S(2)}) copy-start(s32[8]{0:T(128)} %places_ref.1) | copy-start | bytes 100
  0.6 16.8 %copy-start.5 = (s32[20]{0:T(128)S(1)}, s32[20]{0:T(128)}, u32[]{:S(2)}) copy-start(s32[20]{0:T(128)} %cols_ref.5) | copy-start | bytes 244
  0.7 16.8 %copy-start.4 = (s32[20]{0:T(128)S(1)}, s32[20]{0:T(128)}, u32[]{:S(2)}) copy-start(s32[20]{0:T(128)} %rows_ref.5) | copy-start | bytes 244
  4.9 32.2 %collective-permute-start = (bf16[2,128,512]{2,1,0:T(8,128)(2,1)}, bf16[2,128,512]{2,1,0:T(8,128)(2,1)S(1)}, u32[]{:S(2)}, u32[]{:S(2)}) collective-permute-start(bf16[2,128,512]{2,1,0:T(8,128)(2,1)} %get-tuple-element.32), channel_id=1, source_target_pairs={{0,7},{1,6},{2,5},{3,4},{4,3},{5,2},{6,1},{7,0},{8,15},{9,14},{10,... | collective-permute-start | bytes 786440 | tf_op jit(solution)/shard_map/ppermute | solution.py:74
  11.0 26.1 %collective-permute-start.2 = (bf16[2,128,512]{2,1,0:T(8,128)(2,1)}, bf16[2,128,512]{2,1,0:T(8,128)(2,1)S(1)}, u32[]{:S(2)}, u32[]{:S(2)}) collective-permute-start(bf16[2,128,512]{2,1,0:T(8,128)(2,1)} %get-tuple-element.34), channel_id=1, source_target_pairs={{0,1},{1,0},{2,3},{3,2},{4,5},{5,4},{6,7},{7,6},{8,9},{9,8},{10,11... | collective-permute-start | bytes 786440 | tf_op jit(solution)/shard_map/ppermute | solution.py:74
  11.5 26.4 %collective-permute-start.1 = (bf16[2,128,512]{2,1,0:T(8,128)(2,1)}, bf16[2,128,512]{2,1,0:T(8,128)(2,1)S(1)}, u32[]{:S(2)}, u32[]{:S(2)}) collective-permute-start(bf16[2,128,512]{2,1,0:T(8,128)(2,1)} %get-tuple-element.33), channel_id=1, source_target_pairs={{0,6},{1,7},{2,4},{3,5},{4,2},{5,3},{6,0},{7,1},{8,14},{9,15},{10,... | collective-permute-start | bytes 786440 | tf_op jit(solution)/shard_map/ppermute | solution.py:74
  11.6 26.3 %collective-permute-start.3 = (bf16[2,128,512]{2,1,0:T(8,128)(2,1)}, bf16[2,128,512]{2,1,0:T(8,128)(2,1)S(1)}, u32[]{:S(2)}, u32[]{:S(2)}) collective-permute-start(bf16[2,128,512]{2,1,0:T(8,128)(2,1)} %get-tuple-element.35), channel_id=1, source_target_pairs={{0,2},{1,3},{2,0},{3,1},{4,6},{5,7},{6,4},{7,5},{8,10},{9,11},{10,... | collective-permute-start | bytes 786440 | tf_op jit(solution)/shard_map/ppermute | solution.py:74
  11.6 39.7 %collective-permute-start.4 = (bf16[2,128,512]{2,1,0:T(8,128)(2,1)}, bf16[2,128,512]{2,1,0:T(8,128)(2,1)S(1)}, u32[]{:S(2)}, u32[]{:S(2)}) collective-permute-start(bf16[2,128,512]{2,1,0:T(8,128)(2,1)} %get-tuple-element.39), channel_id=1, source_target_pairs={{0,5},{1,4},{2,7},{3,6},{4,1},{5,0},{6,3},{7,2},{8,13},{9,12},{10,... | collective-permute-start | bytes 786440 | tf_op jit(solution)/shard_map/ppermute | solution.py:74
  17.5 19.6 %copy-start.8 = (bf16[2,128,512]{2,1,0:T(8,128)(2,1)S(1)}, bf16[2,128,512]{2,1,0:T(8,128)(2,1)}, u32[]{:S(2)}) copy-start(bf16[2,128,512]{2,1,0:T(8,128)(2,1)} %get-tuple-element.41) | copy-start | bytes 786436
  17.5 19.7 %copy-start.7 = (bf16[2,128,512]{2,1,0:T(8,128)(2,1)S(1)}, bf16[2,128,512]{2,1,0:T(8,128)(2,1)}, u32[]{:S(2)}) copy-start(bf16[2,128,512]{2,1,0:T(8,128)(2,1)} %get-tuple-element.43) | copy-start | bytes 786436
  37.1 18.8 %collective-permute-start.5 = (bf16[2,128,512]{2,1,0:T(8,128)(2,1)S(1)}, bf16[2,128,512]{2,1,0:T(8,128)(2,1)S(1)}, u32[]{:S(2)}, u32[]{:S(2)}) collective-permute-start(bf16[2,128,512]{2,1,0:T(8,128)(2,1)S(1)} %copy-done.8), channel_id=1, source_target_pairs={{0,4},{1,5},{2,6},{3,7},{4,0},{5,1},{6,2},{7,3},{8,12},{9,13},{10,... | collective-permute-start | bytes 786440 | tf_op jit(solution)/shard_map/ppermute | solution.py:74
  37.2 18.7 %collective-permute-start.6 = (bf16[2,128,512]{2,1,0:T(8,128)(2,1)S(1)}, bf16[2,128,512]{2,1,0:T(8,128)(2,1)S(1)}, u32[]{:S(2)}, u32[]{:S(2)}) collective-permute-start(bf16[2,128,512]{2,1,0:T(8,128)(2,1)S(1)} %copy-done.7), channel_id=1, source_target_pairs={{0,3},{1,2},{2,1},{3,0},{4,7},{5,6},{6,5},{7,4},{8,11},{9,10},{10,... | collective-permute-start | bytes 786440 | tf_op jit(solution)/shard_map/ppermute | solution.py:74
  56.0 32.0 %all-to-all-start = ((bf16[8,128,512]{2,1,0:T(8,128)(2,1)}), bf16[8,128,512]{2,1,0:T(8,128)(2,1)S(1)}, u32[]{:S(2)}, u32[]{:S(2)}) async-start(bf16[8,128,512]{2,1,0:T(8,128)(2,1)} %get-tuple-element.54), calls=%async_computation | async-start | bytes 2097152 | tf_op jit(solution)/shard_map/all_to_all | solution.py:632
  66.2 16.2 %collective-permute-start.7 = (bf16[256,512]{1,0:T(8,128)(2,1)}, bf16[256,512]{1,0:T(8,128)(2,1)S(1)}, u32[]{:S(2)}, u32[]{:S(2)}) collective-permute-start(bf16[256,512]{1,0:T(8,128)(2,1)} %get-tuple-element.47), channel_id=1, source_target_pairs={{0,8},{8,16},{16,24},{24,0},{1,9},{9,17},{17,25},{25,1},{2,10},{10... | collective-permute-start | bytes 786440 | tf_op jit(solution)/shard_map/ppermute | solution.py:638
  66.3 16.2 %collective-permute-start.8 = (bf16[256,512]{1,0:T(8,128)(2,1)}, bf16[256,512]{1,0:T(8,128)(2,1)S(1)}, u32[]{:S(2)}, u32[]{:S(2)}) collective-permute-start(bf16[256,512]{1,0:T(8,128)(2,1)} %get-tuple-element.51), channel_id=1, source_target_pairs={{0,16},{8,24},{16,0},{24,8},{1,17},{9,25},{17,1},{25,9},{2,18},{10... | collective-permute-start | bytes 786440 | tf_op jit(solution)/shard_map/ppermute | solution.py:638
  67.9 14.6 %collective-permute-start.9 = (bf16[256,512]{1,0:T(8,128)(2,1)}, bf16[256,512]{1,0:T(8,128)(2,1)S(1)}, u32[]{:S(2)}, u32[]{:S(2)}) collective-permute-start(bf16[256,512]{1,0:T(8,128)(2,1)} %get-tuple-element.52), channel_id=1, source_target_pairs={{0,24},{8,0},{16,8},{24,16},{1,25},{9,1},{17,9},{25,17},{2,26},{10... | collective-permute-start | bytes 786440 | tf_op jit(solution)/shard_map/ppermute | solution.py:638
  69.3 13.3 %copy-start.6 = (f32[256,512]{1,0:T(8,128)S(1)}, f32[256,512]{1,0:T(8,128)}, u32[]{:S(2)}) copy-start(f32[256,512]{1,0:T(8,128)} %get-tuple-element.46) | copy-start | bytes 1572868
  82.7 5.1 %collective-permute-start.10 = (bf16[128,512]{1,0:T(8,128)(2,1)S(1)}, bf16[128,512]{1,0:T(8,128)(2,1)S(1)}, u32[]{:S(2)}, u32[]{:S(2)}) collective-permute-start(bf16[128,512]{1,0:T(8,128)(2,1)S(1)} %fusion), channel_id=1, source_target_pairs={{0,1},{1,0},{2,3},{3,2},{4,5},{5,4},{6,7},{7,6},{8,9},{9,8},{10,11... | collective-permute-start | bytes 393224 | tf_op jit(solution)/shard_map/ppermute | solution.py:541
  87.9 5.1 %collective-permute-start.11 = (bf16[128,512]{1,0:T(8,128)(2,1)S(1)}, bf16[128,512]{1,0:T(8,128)(2,1)S(1)}, u32[]{:S(2)}, u32[]{:S(2)}) collective-permute-start(bf16[128,512]{1,0:T(8,128)(2,1)S(1)} %bitcast_add_fusion), channel_id=1, source_target_pairs={{0,2},{1,3},{2,0},{3,1},{4,6},{5,7},{6,4},{7,5},{8,10},{9,11},{10,... | collective-permute-start | bytes 393224 | tf_op jit(solution)/shard_map/ppermute | solution.py:555
  93.1 5.9 %collective-permute-start.12 = (bf16[128,512]{1,0:T(8,128)(2,1)S(1)}, bf16[128,512]{1,0:T(8,128)(2,1)S(1)}, u32[]{:S(2)}, u32[]{:S(2)}) collective-permute-start(bf16[128,512]{1,0:T(8,128)(2,1)S(1)} %add_convert_fusion.1), channel_id=1, source_target_pairs={{0,4},{1,5},{2,6},{3,7},{4,0},{5,1},{6,2},{7,3},{8,12},{9,13},{10,... | collective-permute-start | bytes 393224 | tf_op jit(solution)/shard_map/ppermute | solution.py:555
  99.1 10.9 %collective-permute-start.13 = (bf16[128,512]{1,0:T(8,128)(2,1)S(1)}, bf16[128,512]{1,0:T(8,128)(2,1)S(1)}, u32[]{:S(2)}, u32[]{:S(2)}) collective-permute-start(bf16[128,512]{1,0:T(8,128)(2,1)S(1)} %add_convert_fusion), channel_id=1, source_target_pairs={{0,1},{1,0},{2,3},{3,2},{4,5},{5,4},{6,7},{7,6},{8,9},{9,8},{10,11... | collective-permute-start | bytes 393224 | tf_op jit(solution)/shard_map/ppermute | solution.py:567
  102.9 25.3 %all-to-all-start.1 = ((bf16[8,128,512]{2,1,0:T(8,128)(2,1)}), bf16[8,128,512]{2,1,0:T(8,128)(2,1)S(1)}, u32[]{:S(2)}, u32[]{:S(2)}) async-start(bf16[8,128,512]{2,1,0:T(8,128)(2,1)} %get-tuple-element.56), calls=%async_computation.1 | async-start | bytes 2097152 | tf_op jit(solution)/shard_map/all_to_all | solution.py:632
  110.0 11.9 %collective-permute-start.14 = (bf16[2,128,512]{2,1,0:T(8,128)(2,1)S(1)}, bf16[2,128,512]{2,1,0:T(8,128)(2,1)S(1)}, u32[]{:S(2)}, u32[]{:S(2)}) collective-permute-start(bf16[2,128,512]{2,1,0:T(8,128)(2,1)S(1)} %get-tuple-element.61), channel_id=1, source_target_pairs={{0,16},{8,24},{16,0},{24,8},{1,17},{9,25},{17,1},{25,9},{2,18},{10... | collective-permute-start | bytes 786440 | tf_op jit(solution)/shard_map/ppermute | solution.py:567
  122.0 2.0 %collective-permute-start.15 = (bf16[2,2,128,512]{3,2,1,0:T(8,128)(2,1)S(1)}, bf16[2,2,128,512]{3,2,1,0:T(8,128)(2,1)S(1)}, u32[]{:S(2)}, u32[]{:S(2)}) collective-permute-start(bf16[2,2,128,512]{3,2,1,0:T(8,128)(2,1)S(1)} %pad_maximum_fusion.1), channel_id=1, source_target_pairs={{0,8},{8,0},{16,24},{24,16},{1,9},{9,1},{17,25},{25,17},{2,10},{10... | collective-permute-start | bytes 1572872 | tf_op jit(solution)/shard_map/ppermute | solution.py:567
  (3 other events, 22.7 us)

commit v5 on v4

--- a/solution.py
+++ b/solution.py
@@ -229,20 +229,24 @@
     tile = tiles.shape[1]
     chunk = row_chunk(assets, 5 * tile)
     per = chunk // tile
-    sets = len(made)
-
-    def body(me_ref, count_ref, rows_ref, cols_ref, places_ref, tiles_ref, c_ref, d_ref, w_ref, r_in, *rest):
-        parts, (out_ref, dense, r_ref, sem, *turned) = rest[:sets], rest[sets:]
+    shapes = [(x.shape[0],) + x.shape[2:] for x in made]
+
+    def body(me_ref, count_ref, rows_ref, cols_ref, places_ref, c_ref, d_ref, tiles_in, w_in, r_in, early_in, late_in, *rest):
+        out_ref, dense, tiles_ref, w_ref, r_ref, early_ref, late_ref, turned, sem, r_sem = rest
         t, i = pl.program_id(0), pl.program_id(1)
-        loads = [pltpu.make_async_copy(r_in.at[s], r_ref.at[s], sem.at[s]) for s in range(steps)]
+        loads = [pltpu.make_async_copy(r_in.at[s], r_ref.at[s], r_sem.at[s]) for s in range(steps)]
+        sides = ((tiles_in, tiles_ref), (w_in, w_ref), (late_in.at[:, 1], late_ref), (early_in.at[:, 1], early_ref))
+        others = [pltpu.make_async_copy(source, to, sem.at[k]) for k, (source, to) in enumerate(sides)]
 
         @pl.when((t == 0) & (i == 0))
         def _():
-            for load in loads:
+            for load in others[:1] + loads[:1] + others[1:] + loads[1:]:
                 load.start()
+            others[0].wait()
             place_tiles(dense, tiles_ref, count_ref[0], rows_ref, cols_ref, True)
-            for part, to in zip(parts, turned):
-                to[...] = mm_nt(flat_rows(part[...]), w_ref[...]).reshape(to.shape)
+            for load in others[1:]:
+                load.wait()
+            turned[...] = mm_nt(flat_rows(late_ref[...]), w_ref[...]).reshape(turned.shape)
 
         for s in range(steps):
 
@@ -252,35 +256,36 @@
 
         at = pl.ds(pl.multiple_of(i * chunk, chunk), chunk)
         out_ref[0] = c_ref[0].astype(F32) + mm(dense[at, :], r_ref[t]) + mm_nt(d_ref[0], w_ref[...])
-        for part, shifts in zip(turned, groups):
+        for part, shifts in zip((early_ref, turned), groups):
             for j, shift in enumerate(shifts):
                 place = places_ref[source_of(me_ref[0], shift, n)] - i * per
 
                 @pl.when((place >= 0) & (place < per))
                 def _():
-                    out_ref[0, pl.ds(pl.multiple_of(place * tile, tile), tile), :] += part[j, t]
+                    out_ref[0, pl.ds(pl.multiple_of(place * tile, tile), tile), :] += part[j, t].astype(F32)
 
     line = pl.BlockSpec((1, chunk, width), lambda t, i: (t, i, 0))
-    weight = pl.BlockSpec((width, width), lambda t, i: (0, 0))
-    pieces = [pl.BlockSpec((x.shape[0], 1) + x.shape[2:], lambda t, i: (0, 1, 0, 0, 0)) for x in made]
     return pl.pallas_call(
         body,
         grid=(steps, assets // chunk),
         out_shape=pltpu.HBM(back.shape, F32),
-        in_specs=[SMEM] * 5
-        + [pl.BlockSpec(tiles.shape, lambda t, i: (0, 0, 0)), line, line, weight, ANY]
-        + pieces,
+        in_specs=[SMEM] * 5 + [line, line] + [ANY] * 5,
         out_specs=line,
         scratch_shapes=[
             pltpu.VMEM((assets, assets), BF16),
+            pltpu.VMEM(tiles.shape, BF16),
+            pltpu.VMEM(w_gate.shape, BF16),
             pltpu.VMEM(back.shape, BF16),
+            pltpu.VMEM(shapes[0], BF16),
+            pltpu.VMEM(shapes[1], BF16),
+            pltpu.VMEM(shapes[1], F32),
+            pltpu.SemaphoreType.DMA((4,)),
             pltpu.SemaphoreType.DMA((steps,)),
-        ]
-        + [pltpu.VMEM((x.shape[0],) + x.shape[2:], F32) for x in made],
+        ],
         compiler_params=params(),
         cost_estimate=cost(0, 0),
         name="local_back",
-    )(me, count, rows, cols, places, *far_memory(tiles, grad, dgate, w_gate, back, *made))
+    )(me, count, rows, cols, places, *far_memory(grad, dgate, tiles, w_gate, back, *made))
 
 
 def add_arrived(me, sums, arrived, rows, features, grad, w_value, w_gate, shifts, n, tile):
@@ -323,7 +328,7 @@
             kept, dagg, dgate = gate_terms(f, c, p, w_buf[1], w_buf[0])
             shape = (some.stop - some.start, steps, tile, width)
             made[some, 0] = kept.astype(BF16).reshape(shape)
-            made[some, 1] = dgate.reshape(shape)
+            made[some, 1] = mm_nt(dgate, w_buf[0]).astype(BF16).reshape(shape)
             store = pltpu.make_async_copy(made.at[some], made_ref.at[some], made_sem.at[low])
             store.start()
             stores.append(store)
@@ -444,15 +449,16 @@
     )(me, place, *far_memory(rows, features, grad, w_value, w_gate, sums.reshape(2 * width, width)), *arrived)
 
 
-def settle(me, kept, features, made, rows, groups, n, tile):
+def settle(me, kept, features, base, made, rows, groups, n, tile):
     steps, assets, width = kept.shape
     blocks = assets // tile
     per = 2 if blocks % 2 == 0 else 1
     sets = len(made)
 
-    def body(me_ref, rows_ref, k_ref, f_ref, *rest):
-        parts, (out_ref, acc) = rest[:sets], rest[sets:]
+    def body(me_ref, rows_ref, k_ref, f_ref, b_ref, *rest):
+        parts, (out_ref, grads_ref, acc) = rest[:sets], rest[sets:]
         b = pl.program_id(0)
+        grads_ref[...] = b_ref[...].astype(BF16)
         acc[...] = f_ref[...].astype(F32) + k_ref[...].astype(F32)
         for part, shifts in zip(parts, groups):
             for j, shift in enumerate(shifts):
@@ -469,50 +475,73 @@
     return pl.pallas_call(
         body,
         grid=(blocks // per,),
-        out_shape=pltpu.HBM((steps, assets, width), BF16),
-        in_specs=[SMEM, SMEM, line, line] + pieces,
-        out_specs=line,
+        out_shape=[pltpu.HBM((steps, assets, width), BF16)] * 2,
+        in_specs=[SMEM, SMEM, line, line, line] + pieces,
+        out_specs=[line, line],
         scratch_shapes=[pltpu.VMEM((steps, per * tile, width), F32)],
         compiler_params=params(),
         cost_estimate=cost(0, 0),
         name="settle",
-    )(me, rows, *far_memory(kept, features, *made))
+    )(me, rows, *far_memory(kept, features, base, *made))
 
 
 def finish(step, grads, base, returned, cols, live, tiles, n):
     steps, assets, width = base.shape
     tile = tiles.shape[1]
-    blocks = assets // tile
-    per = 2 if blocks % 2 == 0 else 1
-
-    def body(cols_ref, live_ref, tiles_ref, r_ref, b_ref, *rest):
-        out_ref, acc = rest[-2:]
-        b = pl.program_id(0)
-        acc[...] = b_ref[0]
+
+    def body(cols_ref, live_ref, r_in, tiles_in, b_in, _, out_ref, r_ref, tiles_ref, b_ref, made, sem, b_sem, done_sem):
+        others = [pltpu.make_async_copy(tiles_in, tiles_ref, sem.at[0]), pltpu.make_async_copy(r_in, r_ref, sem.at[1])]
+        for load in others:
+            load.start()
+        places = [pl.ds(pl.multiple_of(cols_ref[of] * tile, tile), tile) for of in range(n)]
+        blocks = [pltpu.make_async_copy(b_in.at[step, places[of], :], b_ref.at[of], b_sem.at[of]) for of in range(n)]
+        for load in blocks:
+            load.start()
+        owner = []
         for of in range(n):
-            spot = cols_ref[of] - b * per
-
-            @pl.when((spot >= 0) & (spot < per) & (live_ref[of] != 0))
+            first = jnp.int32(of)
+            for other in reversed(range(of)):
+                first = jnp.where(cols_ref[other] == cols_ref[of], other, first)
+            owner.append(first)
+        for load in others + blocks:
+            load.wait()
+        for of in range(n):
+            used = tiles_ref[of] * live_ref[of].astype(F32).astype(BF16)
+            b_ref[owner[of]] += mm_tn(used, r_ref[of])
+        stores = [pltpu.make_async_copy(made.at[of], out_ref.at[step, places[of], :], done_sem.at[of]) for of in range(n)]
+        for of in range(n):
+
+            @pl.when(owner[of] == of)
             def _():
-                acc[pl.ds(pl.multiple_of(spot * tile, tile), tile), :] += mm_tn(tiles_ref[of], r_ref[of])
-
-        out_ref[0] = acc[...].astype(BF16)
-
-    line = pl.BlockSpec((1, per * tile, width), lambda b: (step, b, 0))
-    every = [pl.BlockSpec(x.shape, lambda b: (0, 0, 0)) for x in (tiles, returned)]
-    old = [] if grads is None else far_memory(grads)
+                made[of] = b_ref[of].astype(BF16)
+                stores[of].start()
+
+        for of in range(n):
+
+            @pl.when(owner[of] == of)
+            def _():
+                stores[of].wait()
+
+    block = pltpu.VMEM((n, tile, width), BF16)
     return pl.pallas_call(
         body,
-        grid=(blocks // per,),
-        out_shape=pltpu.HBM((steps, assets, width), BF16),
-        in_specs=[SMEM, SMEM, *every, line] + [ANY] * len(old),
-        out_specs=line,
-        scratch_shapes=[pltpu.VMEM((per * tile, width), F32)],
-        input_output_aliases={5: 0} if old else {},
+        out_shape=pltpu.HBM(grads.shape, BF16),
+        in_specs=[SMEM, SMEM] + [ANY] * 4,
+        out_specs=ANY,
+        scratch_shapes=[
+            block,
+            pltpu.VMEM(tiles.shape, BF16),
+            pltpu.VMEM((n, tile, width), F32),
+            block,
+            pltpu.SemaphoreType.DMA((2,)),
+            pltpu.SemaphoreType.DMA((n,)),
+            pltpu.SemaphoreType.DMA((n,)),
+        ],
+        input_output_aliases={5: 0},
         compiler_params=params(),
         cost_estimate=cost(0, 0),
         name="finish",
-    )(cols, live, *far_memory(tiles), returned, *far_memory(base), *old)
+    )(cols, live, returned, *far_memory(tiles, base, grads))
 
 
 def levels(tm, asset):
@@ -633,8 +662,8 @@
 
     returned = [send_back(t, made_early, *[came[s] for s in late]) for t in range(steps // 2)]
     made, groups = (made_early, made_late), (early, late)
-    output = settle(me, kept, features, made, remote_rows, groups, n, tile)
     base = local_back(me, *graph, back, cotangent, dgate, made, remote_rows, groups, w_gate, n)
+    output, grad_features = settle(me, kept, features, base, made, remote_rows, groups, n, tile)
     terms = [keep] + [lax.ppermute(x, "tm", pairs_of(whole, i + 1)) for i, x in enumerate(sends)]
     terms[1] = after(terms[1], base)
     shape = (row[2], keep.shape[0] // row[2], width)
@@ -643,8 +672,6 @@
     sums = butterfly_sum(sums, line, BF16).astype(BF16)
     returned += [send_back(t, sums) for t in range(steps // 2, steps)]
 
-    grad_features = None
-
     def finish_step(t):
         return finish(t, grad_features, base, returned[t], remote_cols, remote_live, remote_tiles, n)
 
@@ -652,8 +679,7 @@
         grad_features = finish_step(t)
     sums = jnp.stack(spread(sums, row))
     sums = jnp.stack(spread(sums, column))
-    if grad_features is not None:
-        sums = after(sums, grad_features, output)
+    sums = after(sums, grad_features, output)
     sums = jnp.stack(spread(sums, pair))
     scale = float(steps * assets * tm * n) ** (-0.5)
     sums = unshuffle(sums, [pair, column, row], [column, pair, row], (2, width, width)) * scale

time: 134 us -> 133 us (level)
  starting transfers between devices: 33.7 us -> 31.1 us
    ppermute x3, waiting for transfers between devices: 5.36 us -> 2.71 us  [spread(): lax.ppermute(x, axis, pairs_of(level, s))]
    ppermute x3, starting transfers between devices: 3.97 us -> 1.43 us  [spread(): lax.ppermute(x, axis, pairs_of(level, s))]
    all_to_all x2, waiting for transfers between devices: 1.6 us -> 3.33 us  [send_back(): return lax.all_to_all(after(owed[t], *before), 'asset', 0, 0, tiled=True)]
    ppermute x2, waiting for transfers between devices: 6.48 us -> 7.95 us  [butterfly_sum(): lax.ppermute(x, axis, [(i, i ^ shift * level[1]) for i in range(level[3])])]
  transfers between devices with their start and end apart: 18 -> 18, of which waited for: 8 -> 8; matrix products, arithmetic and copies ran while one was open for 2% -> 2% of each run, Pallas kernels for 44% -> 45%
where the time goes in v5:
time: 133 us; the launch traced here: 132 us
  Pallas kernels  67.6 us (51%)
  starting transfers between devices  31.1 us (23%)
  waiting for transfers between devices  28.2 us (21%)
  local copies, waits for them, and re-layouts  2.22 us (2%)
  between operations  1.82 us (1%)
    pallas_call x1, Pallas kernels, local_forward(): pl.pallas_call(body, grid=(steps, turns), out_shape=[pltpu.HBM(features.s...  19.6 us
    pallas_call x1, Pallas kernels, local_back(): pl.pallas_call(body, grid=(steps, assets // chunk), out_shape=pltpu.HBM(b...  13.1 us
    ppermute x7, starting transfers between devices, exchange(): lax.ppermute(block, 'asset', [(i, target_of(i, shift, n)) for i in range(...  12.6 us
    ppermute x7, waiting for transfers between devices, exchange(): lax.ppermute(block, 'asset', [(i, target_of(i, shift, n)) for i in range(...  10.2 us
    pallas_call x1, Pallas kernels, settle(): pl.pallas_call(body, grid=(blocks // per,), out_shape=[pltpu.HBM((steps,...  8.9 us
    all_to_all x2, starting transfers between devices, send_back(): return lax.all_to_all(after(owed[t], *before), 'asset', 0, 0, tiled=True)  8.65 us
    ppermute x2, waiting for transfers between devices, butterfly_sum(): lax.ppermute(x, axis, [(i, i ^ shift * level[1]) for i in range(level[3])])  7.95 us
    pallas_call x1, Pallas kernels, add_arrived(): pl.pallas_call(body, out_shape=out_shape, in_specs=[SMEM] + [ANY] * len(o...  7.93 us
  transfers between devices with their start and end apart: 18, of which 8 were waited for; matrix products, arithmetic and copies ran while one was open for 2% of the time, Pallas kernels for 45%

profile of v5, /device:TPU:0, one launch (start us, length us, event | category | flops | bytes accessed | tf_op | source)
XLA Modules:
  0.0 131.9 jit_solution(6356733588572735698)
XLA Ops:
  0.7 4.2 %send_forward.1 = (bf16[2,128,512]{2,1,0:T(8,128)(2,1)}, bf16[2,128,512]{2,1,0:T(8,128)(2,1)}, bf16[2,128,512]{2,1,0:T(8,128)(2,1)}, bf16[2,128,512]{2,1,0:T(8,1...) custom-call(s32[1]{0:T(128)} %bitcast.me_ref, s32[8]{0:T(128)} %cols_ref.7, ...), custom_call_target="tpu_custom_call" | custom-call | flops 234881024 | bytes 3670016 | tf_op jit(solution)/shard_map/send_forward/pallas_call | solution.py:115
  4.9 6.0 %collective-permute-start = (bf16[2,128,512]{2,1,0:T(8,128)(2,1)}, bf16[2,128,512]{2,1,0:T(8,128)(2,1)S(1)}, u32[]{:S(2)}, u32[]{:S(2)}) collective-permute-start(bf16[2,128,512]{2,1,0:T(8,128)(2,1)} %get-tuple-element.36), channel_id=1, source_target_pairs={{0,7},{1,6},{2,5},{3,4},{4,3},{5,2},{6,1},{7,0},{8,15},{9,14},{10,... | collective-permute-start | bytes 786440 | tf_op jit(solution)/shard_map/ppermute | solution.py:74
  11.6 5.2 %collective-permute-start.4 = (bf16[2,128,512]{2,1,0:T(8,128)(2,1)}, bf16[2,128,512]{2,1,0:T(8,128)(2,1)S(1)}, u32[]{:S(2)}, u32[]{:S(2)}) collective-permute-start(bf16[2,128,512]{2,1,0:T(8,128)(2,1)} %get-tuple-element.43), channel_id=1, source_target_pairs={{0,5},{1,4},{2,7},{3,6},{4,1},{5,0},{6,3},{7,2},{8,13},{9,12},{10,... | collective-permute-start | bytes 786440 | tf_op jit(solution)/shard_map/ppermute | solution.py:74
  17.5 19.6 %local_forward.1 = (bf16[2,1280,512]{2,1,0:T(8,128)(2,1)}, bf16[2,1280,512]{2,1,0:T(8,128)(2,1)}, bf16[2,1280,512]{2,1,0:T(8,128)(2,1)}, f32[2,512,512]{2,1,0:T(...) custom-call(s32[1]{0:T(128)S(6)} %copy.20.count_ref, s32[20]{0:T(128)S(1)} %copy-done.4, ...), custom_call_target="tpu_custom_call" | custom-call | tf_op jit(solution)/shard_map/local_forward/pallas_call | solution.py:206
  37.8 7.9 %add_arrived.1 = (bf16[4,2,2,128,512]{4,3,2,1,0:T(8,128)(2,1)}, f32[2,512,512]{2,1,0:T(8,128)}) custom-call(s32[1]{0:T(128)} %bitcast.me_ref, s32[8]{0:T(128)} %rows_ref.5, bf16[2,1280,512]{2,1,0:T(8,128)(2,1)} %f_ref.7, bf16[2,1280,512]{2,1,0:T(8,128)(2,1)} %c_ref.7, bf16[512,512]{1,0:T(8,128)(2,1)} %wv_ref.5, bf16[512,512]{1,0:T(8,128)(2,1)} %w_in.1, ...), custom_call_target="tpu_custom_call" | custom-call | tf_op jit(solution)/shard_map/add_arrived/pallas_call | solution.py:354
  45.8 5.5 %collective-permute-done.4.rest_0_ = bf16[2,128,512]{2,1,0:T(8,128)(2,1)S(1)} collective-permute-done((bf16[2,128,512]{2,1,0:T(8,128)(2,1)}, bf16[2,128,512]{2,1,0:T(8,128)(2,1)S(1)}, u32[]{:S(2)}, u32[]{:S(2)}) %collective-permute-start.4) | collective-permute-done | bytes 262176 | tf_op jit(solution)/shard_map/ppermute | solution.py:74
  51.3 4.7 %collective-permute-done.5.rest_1_ = bf16[2,128,512]{2,1,0:T(8,128)(2,1)S(1)} collective-permute-done((bf16[2,128,512]{2,1,0:T(8,128)(2,1)S(1)}, bf16[2,128,512]{2,1,0:T(8,128)(2,1)S(1)}, u32[]{:S(2)}, u32[]{:S(2)}) %collective-permute-start.5) | collective-permute-done | bytes 262176 | tf_op jit(solution)/shard_map/ppermute | solution.py:74
  56.0 3.8 %all-to-all-start = ((bf16[8,128,512]{2,1,0:T(8,128)(2,1)}), bf16[8,128,512]{2,1,0:T(8,128)(2,1)S(1)}, u32[]{:S(2)}, u32[]{:S(2)}) async-start(bf16[8,128,512]{2,1,0:T(8,128)(2,1)} %get-tuple-element.57), calls=%async_computation | async-start | bytes 2097152 | tf_op jit(solution)/shard_map/all_to_all | solution.py:661
  59.8 6.4 %add_late.1 = (f32[256,512]{1,0:T(8,128)}, bf16[256,512]{1,0:T(8,128)(2,1)}, bf16[256,512]{1,0:T(8,128)(2,1)}, bf16[256,512]{1,0:T(8,128)(2,1)}, bf16[3,2,2,128,512]{4,3,2,1,0:T(8,128)(2,1)}) custom-call(s32[1]{0:T(128)} %bitcast.me_ref, s32[1]{0:T(128)} %bitcast.1.place_ref, s32[8]{0:T(128)} %rows_ref.5, bf16[2,1280,512]{2,1,0:T(8,128)(2,1)} %f_ref.7, ...), custom_call_target="tpu_custom_call" | custom-call | tf_op jit(solution)/shard_map/add_late/pallas_call | solution.py:426
  66.3 1.6 %collective-permute-start.8 = (bf16[256,512]{1,0:T(8,128)(2,1)}, bf16[256,512]{1,0:T(8,128)(2,1)S(1)}, u32[]{:S(2)}, u32[]{:S(2)}) collective-permute-start(bf16[256,512]{1,0:T(8,128)(2,1)} %get-tuple-element.54), channel_id=1, source_target_pairs={{0,16},{8,24},{16,0},{24,8},{1,17},{9,25},{17,1},{25,9},{2,18},{10... | collective-permute-start | bytes 786440 | tf_op jit(solution)/shard_map/ppermute | solution.py:667
  67.9 1.4 %collective-permute-start.9 = (bf16[256,512]{1,0:T(8,128)(2,1)}, bf16[256,512]{1,0:T(8,128)(2,1)S(1)}, u32[]{:S(2)}, u32[]{:S(2)}) collective-permute-start(bf16[256,512]{1,0:T(8,128)(2,1)} %get-tuple-element.55), channel_id=1, source_target_pairs={{0,24},{8,0},{16,8},{24,16},{1,25},{9,1},{17,9},{25,17},{2,26},{10... | collective-permute-start | bytes 786440 | tf_op jit(solution)/shard_map/ppermute | solution.py:667
  69.3 13.1 %local_back.1.b_ref.b_in = f32[2,1280,512]{2,1,0:T(8,128)} custom-call(s32[1]{0:T(128)} %bitcast.me_ref, s32[1]{0:T(128)S(6)} %copy.20.count_ref, s32[20]{0:T(128)S(1)} %copy-done.4, s32[20]{0:T(128)S(1)} %copy-done.5, s32[8]{0:T(128)S(1)} %copy-done.1, bf16[2,1280,512]{2,1,0:T(8,128)(2,1)} %c_ref.7, bf16[2,1280,512]{2,1,0:T(8,128)(2,1)} %get-tuple-element.34.d_ref, ...), custom_call_target="tpu_custom_call" | custom-call | tf_op jit(solution)/shard_map/local_back/pallas_call | solution.py:268
  83.7 4.0 %collective-permute-done.10 = bf16[128,512]{1,0:T(8,128)(2,1)S(1)} collective-permute-done((bf16[128,512]{1,0:T(8,128)(2,1)S(1)}, bf16[128,512]{1,0:T(8,128)(2,1)S(1)}, u32[]{:S(2)}, u32[]{:S(2)}) %collective-permute-start.10) | collective-permute-done | bytes 131104 | tf_op jit(solution)/shard_map/ppermute | solution.py:570
  87.8 1.9 %collective-permute-start.11 = (bf16[128,512]{1,0:T(8,128)(2,1)S(1)}, bf16[128,512]{1,0:T(8,128)(2,1)S(1)}, u32[]{:S(2)}, u32[]{:S(2)}) collective-permute-start(bf16[128,512]{1,0:T(8,128)(2,1)S(1)} %bitcast_add_fusion), channel_id=1, source_target_pairs={{0,2},{1,3},{2,0},{3,1},{4,6},{5,7},{6,4},{7,5},{8,10},{9,11},{10,... | collective-permute-start | bytes 393224 | tf_op jit(solution)/shard_map/ppermute | solution.py:584
  89.7 3.1 %collective-permute-done.11 = bf16[128,512]{1,0:T(8,128)(2,1)S(1)} collective-permute-done((bf16[128,512]{1,0:T(8,128)(2,1)S(1)}, bf16[128,512]{1,0:T(8,128)(2,1)S(1)}, u32[]{:S(2)}, u32[]{:S(2)}) %collective-permute-start.11) | collective-permute-done | bytes 131104 | tf_op jit(solution)/shard_map/ppermute | solution.py:584
  92.9 2.5 %collective-permute-start.12 = (bf16[128,512]{1,0:T(8,128)(2,1)S(1)}, bf16[128,512]{1,0:T(8,128)(2,1)S(1)}, u32[]{:S(2)}, u32[]{:S(2)}) collective-permute-start(bf16[128,512]{1,0:T(8,128)(2,1)S(1)} %add_convert_fusion.1), channel_id=1, source_target_pairs={{0,4},{1,5},{2,6},{3,7},{4,0},{5,1},{6,2},{7,3},{8,12},{9,13},{10,... | collective-permute-start | bytes 393224 | tf_op jit(solution)/shard_map/ppermute | solution.py:584
  95.4 4.8 %collective-permute-done.12 = bf16[128,512]{1,0:T(8,128)(2,1)S(1)} collective-permute-done((bf16[128,512]{1,0:T(8,128)(2,1)S(1)}, bf16[128,512]{1,0:T(8,128)(2,1)S(1)}, u32[]{:S(2)}, u32[]{:S(2)}) %collective-permute-start.12) | collective-permute-done | bytes 131104 | tf_op jit(solution)/shard_map/ppermute | solution.py:584
  101.5 4.9 %all-to-all-start.1 = ((bf16[8,128,512]{2,1,0:T(8,128)(2,1)}), bf16[8,128,512]{2,1,0:T(8,128)(2,1)S(1)}, u32[]{:S(2)}, u32[]{:S(2)}) async-start(bf16[8,128,512]{2,1,0:T(8,128)(2,1)} %get-tuple-element.59), calls=%async_computation.1 | async-start | bytes 2097152 | tf_op jit(solution)/shard_map/all_to_all | solution.py:661
  107.4 8.9 %settle.1 = (bf16[2,1280,512]{2,1,0:T(8,128)(2,1)}, bf16[2,1280,512]{2,1,0:T(8,128)(2,1)}) custom-call(s32[1]{0:T(128)} %bitcast.me_ref, s32[8]{0:T(128)S(1)} %copy-done.1, bf16[2,1280,512]{2,1,0:T(8,128)(2,1)} %get-tuple-element.33.k_ref, bf16[2,1280,512]{2,1,0:T(8,128)(2,1)} %f_ref.7, f32[2,1280,512]{2,1,0:T(8,128)} %local_back.1.b_ref.b_in, ...), custom_call_target="tpu_custom_call" | custom-call | tf_op jit(solution)/shard_map/settle/pallas_call | solution.py:475
  116.4 3.7 %finish.2._ = bf16[2,1280,512]{2,1,0:T(8,128)(2,1)} custom-call(s32[8]{0:T(128)S(1)} %copy-done.2, s32[8]{0:T(128)S(1)} %copy-done.3, bf16[8,128,512]{2,1,0:T(8,128)(2,1)S(1)} %all-to-all-done.r_in, bf16[8,128,128]{2,1,0:T(8,128)(2,1)} %tiles_in.5, f32[2,1280,512]{2,1,0:T(8,128)} %local_back.1.b_ref.b_in, ...), custom_call_target="tpu_custom_call", output_to_operand_aliasing={{}: (5, {})} | custom-call | tf_op jit(solution)/shard_map/finish/pallas_call | solution.py:526
  120.3 1.8 %collective-permute-done.15 = bf16[2,2,128,512]{3,2,1,0:T(8,128)(2,1)S(1)} collective-permute-done((bf16[2,2,128,512]{3,2,1,0:T(8,128)(2,1)S(1)}, bf16[2,2,128,512]{3,2,1,0:T(8,128)(2,1)S(1)}, u32[]{:S(2)}, u32[]{:S(2)}) %collective-permute-start.15) | collective-permute-done | bytes 524320 | tf_op jit(solution)/shard_map/ppermute | solution.py:596
  123.1 1.6 %fusion.15 = (f32[4,128,512]{2,1,0:T(8,128)}, f32[4,128,512]{2,1,0:T(8,128)}) fusion(f32[8,128,512]{2,1,0:T(8,128)S(1)} %convert_multiply_fusion), kind=kLoop, calls=%fused_computation.46 | loop fusion | bytes 4194304 | tf_op jit(solution)/shard_map/slice | solution.py:688
  124.7 3.3 %all-to-all-done.1.r_in = bf16[8,128,512]{2,1,0:T(8,128)(2,1)S(1)} async-done(((bf16[8,128,512]{2,1,0:T(8,128)(2,1)}), bf16[8,128,512]{2,1,0:T(8,128)(2,1)S(1)}, u32[]{:S(2)}, u32[]{:S(2)}) %all-to-all-start.1) | async-done | bytes 1048608 | tf_op jit(solution)/shard_map/all_to_all | solution.py:661
  128.0 3.7 %finish.3 = bf16[2,1280,512]{2,1,0:T(8,128)(2,1)} custom-call(s32[8]{0:T(128)S(1)} %copy-done.2, s32[8]{0:T(128)S(1)} %copy-done.3, bf16[8,128,512]{2,1,0:T(8,128)(2,1)S(1)} %all-to-all-done.1.r_in, bf16[8,128,128]{2,1,0:T(8,128)(2,1)} %tiles_in.5, f32[2,1280,512]{2,1,0:T(8,128)} %local_back.1.b_ref.b_in, ...), custom_call_target="tpu_custom_call", output_to_operand_aliasing={{}: (5, {})} | custom-call | tf_op jit(solution)/shard_map/finish/pallas_call | solution.py:526
  (53 shorter events, 6.3 us)
Async XLA Ops:
  0.6 16.8 %copy-start = (s32[8]{0:T(128)S(1)}, s32[8]{0:T(128)}, u32[]{:S(2)}) copy-start(s32[8]{0:T(128)} %rows_ref.5) | copy-start | bytes 100
  0.6 16.8 %copy-start.5 = (s32[20]{0:T(128)S(1)}, s32[20]{0:T(128)}, u32[]{:S(2)}) copy-start(s32[20]{0:T(128)} %cols_ref.5) | copy-start | bytes 244
  0.7 16.8 %copy-start.4 = (s32[20]{0:T(128)S(1)}, s32[20]{0:T(128)}, u32[]{:S(2)}) copy-start(s32[20]{0:T(128)} %rows_ref.4) | copy-start | bytes 244
  4.9 32.2 %collective-permute-start = (bf16[2,128,512]{2,1,0:T(8,128)(2,1)}, bf16[2,128,512]{2,1,0:T(8,128)(2,1)S(1)}, u32[]{:S(2)}, u32[]{:S(2)}) collective-permute-start(bf16[2,128,512]{2,1,0:T(8,128)(2,1)} %get-tuple-element.36), channel_id=1, source_target_pairs={{0,7},{1,6},{2,5},{3,4},{4,3},{5,2},{6,1},{7,0},{8,15},{9,14},{10,... | collective-permute-start | bytes 786440 | tf_op jit(solution)/shard_map/ppermute | solution.py:74
  11.0 26.2 %collective-permute-start.2 = (bf16[2,128,512]{2,1,0:T(8,128)(2,1)}, bf16[2,128,512]{2,1,0:T(8,128)(2,1)S(1)}, u32[]{:S(2)}, u32[]{:S(2)}) collective-permute-start(bf16[2,128,512]{2,1,0:T(8,128)(2,1)} %get-tuple-element.38), channel_id=1, source_target_pairs={{0,1},{1,0},{2,3},{3,2},{4,5},{5,4},{6,7},{7,6},{8,9},{9,8},{10,11... | collective-permute-start | bytes 786440 | tf_op jit(solution)/shard_map/ppermute | solution.py:74
  11.5 26.4 %collective-permute-start.1 = (bf16[2,128,512]{2,1,0:T(8,128)(2,1)}, bf16[2,128,512]{2,1,0:T(8,128)(2,1)S(1)}, u32[]{:S(2)}, u32[]{:S(2)}) collective-permute-start(bf16[2,128,512]{2,1,0:T(8,128)(2,1)} %get-tuple-element.37), channel_id=1, source_target_pairs={{0,6},{1,7},{2,4},{3,5},{4,2},{5,3},{6,0},{7,1},{8,14},{9,15},{10,... | collective-permute-start | bytes 786440 | tf_op jit(solution)/shard_map/ppermute | solution.py:74
  11.6 26.3 %collective-permute-start.3 = (bf16[2,128,512]{2,1,0:T(8,128)(2,1)}, bf16[2,128,512]{2,1,0:T(8,128)(2,1)S(1)}, u32[]{:S(2)}, u32[]{:S(2)}) collective-permute-start(bf16[2,128,512]{2,1,0:T(8,128)(2,1)} %get-tuple-element.39), channel_id=1, source_target_pairs={{0,2},{1,3},{2,0},{3,1},{4,6},{5,7},{6,4},{7,5},{8,10},{9,11},{10,... | collective-permute-start | bytes 786440 | tf_op jit(solution)/shard_map/ppermute | solution.py:74
  11.6 39.7 %collective-permute-start.4 = (bf16[2,128,512]{2,1,0:T(8,128)(2,1)}, bf16[2,128,512]{2,1,0:T(8,128)(2,1)S(1)}, u32[]{:S(2)}, u32[]{:S(2)}) collective-permute-start(bf16[2,128,512]{2,1,0:T(8,128)(2,1)} %get-tuple-element.43), channel_id=1, source_target_pairs={{0,5},{1,4},{2,7},{3,6},{4,1},{5,0},{6,3},{7,2},{8,13},{9,12},{10,... | collective-permute-start | bytes 786440 | tf_op jit(solution)/shard_map/ppermute | solution.py:74
  17.5 19.6 %copy-start.8 = (bf16[2,128,512]{2,1,0:T(8,128)(2,1)S(1)}, bf16[2,128,512]{2,1,0:T(8,128)(2,1)}, u32[]{:S(2)}) copy-start(bf16[2,128,512]{2,1,0:T(8,128)(2,1)} %get-tuple-element.45) | copy-start | bytes 786436
  17.5 19.7 %copy-start.7 = (bf16[2,128,512]{2,1,0:T(8,128)(2,1)S(1)}, bf16[2,128,512]{2,1,0:T(8,128)(2,1)}, u32[]{:S(2)}) copy-start(bf16[2,128,512]{2,1,0:T(8,128)(2,1)} %get-tuple-element.47) | copy-start | bytes 786436
  37.1 18.8 %collective-permute-start.5 = (bf16[2,128,512]{2,1,0:T(8,128)(2,1)S(1)}, bf16[2,128,512]{2,1,0:T(8,128)(2,1)S(1)}, u32[]{:S(2)}, u32[]{:S(2)}) collective-permute-start(bf16[2,128,512]{2,1,0:T(8,128)(2,1)S(1)} %copy-done.8), channel_id=1, source_target_pairs={{0,4},{1,5},{2,6},{3,7},{4,0},{5,1},{6,2},{7,3},{8,12},{9,13},{10,... | collective-permute-start | bytes 786440 | tf_op jit(solution)/shard_map/ppermute | solution.py:74
  37.2 18.7 %collective-permute-start.6 = (bf16[2,128,512]{2,1,0:T(8,128)(2,1)S(1)}, bf16[2,128,512]{2,1,0:T(8,128)(2,1)S(1)}, u32[]{:S(2)}, u32[]{:S(2)}) collective-permute-start(bf16[2,128,512]{2,1,0:T(8,128)(2,1)S(1)} %copy-done.7), channel_id=1, source_target_pairs={{0,3},{1,2},{2,1},{3,0},{4,7},{5,6},{6,5},{7,4},{8,11},{9,10},{10,... | collective-permute-start | bytes 786440 | tf_op jit(solution)/shard_map/ppermute | solution.py:74
  56.0 31.8 %all-to-all-start = ((bf16[8,128,512]{2,1,0:T(8,128)(2,1)}), bf16[8,128,512]{2,1,0:T(8,128)(2,1)S(1)}, u32[]{:S(2)}, u32[]{:S(2)}) async-start(bf16[8,128,512]{2,1,0:T(8,128)(2,1)} %get-tuple-element.57), calls=%async_computation | async-start | bytes 2097152 | tf_op jit(solution)/shard_map/all_to_all | solution.py:661
  66.2 16.1 %collective-permute-start.7 = (bf16[256,512]{1,0:T(8,128)(2,1)}, bf16[256,512]{1,0:T(8,128)(2,1)S(1)}, u32[]{:S(2)}, u32[]{:S(2)}) collective-permute-start(bf16[256,512]{1,0:T(8,128)(2,1)} %get-tuple-element.52), channel_id=1, source_target_pairs={{0,8},{8,16},{16,24},{24,0},{1,9},{9,17},{17,25},{25,1},{2,10},{10... | collective-permute-start | bytes 786440 | tf_op jit(solution)/shard_map/ppermute | solution.py:667
  66.3 16.1 %collective-permute-start.8 = (bf16[256,512]{1,0:T(8,128)(2,1)}, bf16[256,512]{1,0:T(8,128)(2,1)S(1)}, u32[]{:S(2)}, u32[]{:S(2)}) collective-permute-start(bf16[256,512]{1,0:T(8,128)(2,1)} %get-tuple-element.54), channel_id=1, source_target_pairs={{0,16},{8,24},{16,0},{24,8},{1,17},{9,25},{17,1},{25,9},{2,18},{10... | collective-permute-start | bytes 786440 | tf_op jit(solution)/shard_map/ppermute | solution.py:667
  67.9 14.6 %collective-permute-start.9 = (bf16[256,512]{1,0:T(8,128)(2,1)}, bf16[256,512]{1,0:T(8,128)(2,1)S(1)}, u32[]{:S(2)}, u32[]{:S(2)}) collective-permute-start(bf16[256,512]{1,0:T(8,128)(2,1)} %get-tuple-element.55), channel_id=1, source_target_pairs={{0,24},{8,0},{16,8},{24,16},{1,25},{9,1},{17,9},{25,17},{2,26},{10... | collective-permute-start | bytes 786440 | tf_op jit(solution)/shard_map/ppermute | solution.py:667
  69.3 13.3 %copy-start.6 = (f32[256,512]{1,0:T(8,128)S(1)}, f32[256,512]{1,0:T(8,128)}, u32[]{:S(2)}) copy-start(f32[256,512]{1,0:T(8,128)} %get-tuple-element.51) | copy-start | bytes 1572868
  82.6 5.0 %collective-permute-start.10 = (bf16[128,512]{1,0:T(8,128)(2,1)S(1)}, bf16[128,512]{1,0:T(8,128)(2,1)S(1)}, u32[]{:S(2)}, u32[]{:S(2)}) collective-permute-start(bf16[128,512]{1,0:T(8,128)(2,1)S(1)} %fusion), channel_id=1, source_target_pairs={{0,1},{1,0},{2,3},{3,2},{4,5},{5,4},{6,7},{7,6},{8,9},{9,8},{10,11... | collective-permute-start | bytes 393224 | tf_op jit(solution)/shard_map/ppermute | solution.py:570
  87.8 5.0 %collective-permute-start.11 = (bf16[128,512]{1,0:T(8,128)(2,1)S(1)}, bf16[128,512]{1,0:T(8,128)(2,1)S(1)}, u32[]{:S(2)}, u32[]{:S(2)}) collective-permute-start(bf16[128,512]{1,0:T(8,128)(2,1)S(1)} %bitcast_add_fusion), channel_id=1, source_target_pairs={{0,2},{1,3},{2,0},{3,1},{4,6},{5,7},{6,4},{7,5},{8,10},{9,11},{10,... | collective-permute-start | bytes 393224 | tf_op jit(solution)/shard_map/ppermute | solution.py:584
  92.9 7.3 %collective-permute-start.12 = (bf16[128,512]{1,0:T(8,128)(2,1)S(1)}, bf16[128,512]{1,0:T(8,128)(2,1)S(1)}, u32[]{:S(2)}, u32[]{:S(2)}) collective-permute-start(bf16[128,512]{1,0:T(8,128)(2,1)S(1)} %add_convert_fusion.1), channel_id=1, source_target_pairs={{0,4},{1,5},{2,6},{3,7},{4,0},{5,1},{6,2},{7,3},{8,12},{9,13},{10,... | collective-permute-start | bytes 393224 | tf_op jit(solution)/shard_map/ppermute | solution.py:584
  100.3 7.0 %collective-permute-start.13 = (bf16[128,512]{1,0:T(8,128)(2,1)S(1)}, bf16[128,512]{1,0:T(8,128)(2,1)S(1)}, u32[]{:S(2)}, u32[]{:S(2)}) collective-permute-start(bf16[128,512]{1,0:T(8,128)(2,1)S(1)} %add_convert_fusion), channel_id=1, source_target_pairs={{0,1},{1,0},{2,3},{3,2},{4,5},{5,4},{6,7},{7,6},{8,9},{9,8},{10,11... | collective-permute-start | bytes 393224 | tf_op jit(solution)/shard_map/ppermute | solution.py:596
  101.5 26.5 %all-to-all-start.1 = ((bf16[8,128,512]{2,1,0:T(8,128)(2,1)}), bf16[8,128,512]{2,1,0:T(8,128)(2,1)S(1)}, u32[]{:S(2)}, u32[]{:S(2)}) async-start(bf16[8,128,512]{2,1,0:T(8,128)(2,1)} %get-tuple-element.59), calls=%async_computation.1 | async-start | bytes 2097152 | tf_op jit(solution)/shard_map/all_to_all | solution.py:661
  107.3 12.7 %collective-permute-start.14 = (bf16[2,128,512]{2,1,0:T(8,128)(2,1)S(1)}, bf16[2,128,512]{2,1,0:T(8,128)(2,1)S(1)}, u32[]{:S(2)}, u32[]{:S(2)}) collective-permute-start(bf16[2,128,512]{2,1,0:T(8,128)(2,1)S(1)} %get-tuple-element.65), channel_id=1, source_target_pairs={{0,16},{8,24},{16,0},{24,8},{1,17},{9,25},{17,1},{25,9},{2,18},{10... | collective-permute-start | bytes 786440 | tf_op jit(solution)/shard_map/ppermute | solution.py:596
  120.1 2.0 %collective-permute-start.15 = (bf16[2,2,128,512]{3,2,1,0:T(8,128)(2,1)S(1)}, bf16[2,2,128,512]{3,2,1,0:T(8,128)(2,1)S(1)}, u32[]{:S(2)}, u32[]{:S(2)}) collective-permute-start(bf16[2,2,128,512]{3,2,1,0:T(8,128)(2,1)S(1)} %pad_maximum_fusion.1), channel_id=1, source_target_pairs={{0,8},{8,0},{16,24},{24,16},{1,9},{9,1},{17,25},{25,17},{2,10},{10... | collective-permute-start | bytes 1572872 | tf_op jit(solution)/shard_map/ppermute | solution.py:596
  (3 other events, 27.4 us)

commit v6 on v5

--- a/solution.py
+++ b/solution.py
@@ -503,9 +503,10 @@
             for other in reversed(range(of)):
                 first = jnp.where(cols_ref[other] == cols_ref[of], other, first)
             owner.append(first)
-        for load in others + blocks:
+        for load in others:
             load.wait()
         for of in range(n):
+            blocks[of].wait()
             used = tiles_ref[of] * live_ref[of].astype(F32).astype(BF16)
             b_ref[owner[of]] += mm_tn(used, r_ref[of])
         stores = [pltpu.make_async_copy(made.at[of], out_ref.at[step, places[of], :], done_sem.at[of]) for of in range(n)]

time: 133 us -> 134 us (level)
  waiting for transfers between devices: 28.2 us -> 25.8 us
  starting transfers between devices: 31.1 us -> 33 us
    pallas_call x2, Pallas kernels: 7.41 us -> 8.97 us  [finish(): pl.pallas_call(body, out_shape=pltpu.HBM(grads.shape, BF16), in_specs=[SM...]
where the time goes in v6:
time: 134 us; the launch traced here: 132 us
  Pallas kernels  68.7 us (51%)
  starting transfers between devices  33 us (25%)
  waiting for transfers between devices  25.8 us (19%)
  local copies, waits for them, and re-layouts  2.21 us (2%)
  between operations  1.8 us (1%)
    pallas_call x1, Pallas kernels, local_forward(): pl.pallas_call(body, grid=(steps, turns), out_shape=[pltpu.HBM(features.s...  19.6 us
    pallas_call x1, Pallas kernels, local_back(): pl.pallas_call(body, grid=(steps, assets // chunk), out_shape=pltpu.HBM(b...  12.6 us
    ppermute x7, starting transfers between devices, exchange(): lax.ppermute(block, 'asset', [(i, target_of(i, shift, n)) for i in range(...  12.6 us
    ppermute x7, waiting for transfers between devices, exchange(): lax.ppermute(block, 'asset', [(i, target_of(i, shift, n)) for i in range(...  10.2 us
    pallas_call x2, Pallas kernels, finish(): pl.pallas_call(body, out_shape=pltpu.HBM(grads.shape, BF16), in_specs=[SM...  8.97 us
    pallas_call x1, Pallas kernels, settle(): pl.pallas_call(body, grid=(blocks // per,), out_shape=[pltpu.HBM((steps,...  8.93 us
    pallas_call x1, Pallas kernels, add_arrived(): pl.pallas_call(body, out_shape=out_shape, in_specs=[SMEM] + [ANY] * len(o...  7.93 us
    all_to_all x2, starting transfers between devices, send_back(): return lax.all_to_all(after(owed[t], *before), 'asset', 0, 0, tiled=True)  7.83 us
  transfers between devices with their start and end apart: 18, of which 8 were waited for; matrix products, arithmetic and copies ran while one was open for 2% of the time, Pallas kernels for 45%

profile of v6, /device:TPU:0, one launch (start us, length us, event | category | flops | bytes accessed | tf_op | source)
XLA Modules:
  0.0 132.5 jit_solution(11505386479187081585)
XLA Ops:
  0.7 4.2 %send_forward.1 = (bf16[2,128,512]{2,1,0:T(8,128)(2,1)}, bf16[2,128,512]{2,1,0:T(8,128)(2,1)}, bf16[2,128,512]{2,1,0:T(8,128)(2,1)}, bf16[2,128,512]{2,1,0:T(8,1...) custom-call(s32[1]{0:T(128)} %bitcast.me_ref, s32[8]{0:T(128)} %cols_ref.7, ...), custom_call_target="tpu_custom_call" | custom-call | flops 234881024 | bytes 3670016 | tf_op jit(solution)/shard_map/send_forward/pallas_call | solution.py:115
  4.9 6.0 %collective-permute-start = (bf16[2,128,512]{2,1,0:T(8,128)(2,1)}, bf16[2,128,512]{2,1,0:T(8,128)(2,1)S(1)}, u32[]{:S(2)}, u32[]{:S(2)}) collective-permute-start(bf16[2,128,512]{2,1,0:T(8,128)(2,1)} %get-tuple-element.36), channel_id=1, source_target_pairs={{0,7},{1,6},{2,5},{3,4},{4,3},{5,2},{6,1},{7,0},{8,15},{9,14},{10,... | collective-permute-start | bytes 786440 | tf_op jit(solution)/shard_map/ppermute | solution.py:74
  11.6 5.2 %collective-permute-start.4 = (bf16[2,128,512]{2,1,0:T(8,128)(2,1)}, bf16[2,128,512]{2,1,0:T(8,128)(2,1)S(1)}, u32[]{:S(2)}, u32[]{:S(2)}) collective-permute-start(bf16[2,128,512]{2,1,0:T(8,128)(2,1)} %get-tuple-element.43), channel_id=1, source_target_pairs={{0,5},{1,4},{2,7},{3,6},{4,1},{5,0},{6,3},{7,2},{8,13},{9,12},{10,... | collective-permute-start | bytes 786440 | tf_op jit(solution)/shard_map/ppermute | solution.py:74
  17.5 19.6 %local_forward.1 = (bf16[2,1280,512]{2,1,0:T(8,128)(2,1)}, bf16[2,1280,512]{2,1,0:T(8,128)(2,1)}, bf16[2,1280,512]{2,1,0:T(8,128)(2,1)}, f32[2,512,512]{2,1,0:T(...) custom-call(s32[1]{0:T(128)S(6)} %copy.20.count_ref, s32[20]{0:T(128)S(1)} %copy-done.4, ...), custom_call_target="tpu_custom_call" | custom-call | tf_op jit(solution)/shard_map/local_forward/pallas_call | solution.py:206
  37.8 7.9 %add_arrived.1 = (bf16[4,2,2,128,512]{4,3,2,1,0:T(8,128)(2,1)}, f32[2,512,512]{2,1,0:T(8,128)}) custom-call(s32[1]{0:T(128)} %bitcast.me_ref, s32[8]{0:T(128)} %rows_ref.5, bf16[2,1280,512]{2,1,0:T(8,128)(2,1)} %f_ref.7, bf16[2,1280,512]{2,1,0:T(8,128)(2,1)} %c_ref.7, bf16[512,512]{1,0:T(8,128)(2,1)} %wv_ref.5, bf16[512,512]{1,0:T(8,128)(2,1)} %w_in.1, ...), custom_call_target="tpu_custom_call" | custom-call | tf_op jit(solution)/shard_map/add_arrived/pallas_call | solution.py:354
  45.8 5.5 %collective-permute-done.4.rest_0_ = bf16[2,128,512]{2,1,0:T(8,128)(2,1)S(1)} collective-permute-done((bf16[2,128,512]{2,1,0:T(8,128)(2,1)}, bf16[2,128,512]{2,1,0:T(8,128)(2,1)S(1)}, u32[]{:S(2)}, u32[]{:S(2)}) %collective-permute-start.4) | collective-permute-done | bytes 262176 | tf_op jit(solution)/shard_map/ppermute | solution.py:74
  51.3 4.7 %collective-permute-done.5.rest_1_ = bf16[2,128,512]{2,1,0:T(8,128)(2,1)S(1)} collective-permute-done((bf16[2,128,512]{2,1,0:T(8,128)(2,1)S(1)}, bf16[2,128,512]{2,1,0:T(8,128)(2,1)S(1)}, u32[]{:S(2)}, u32[]{:S(2)}) %collective-permute-start.5) | collective-permute-done | bytes 262176 | tf_op jit(solution)/shard_map/ppermute | solution.py:74
  56.0 3.8 %all-to-all-start = ((bf16[8,128,512]{2,1,0:T(8,128)(2,1)}), bf16[8,128,512]{2,1,0:T(8,128)(2,1)S(1)}, u32[]{:S(2)}, u32[]{:S(2)}) async-start(bf16[8,128,512]{2,1,0:T(8,128)(2,1)} %get-tuple-element.57), calls=%async_computation | async-start | bytes 2097152 | tf_op jit(solution)/shard_map/all_to_all | solution.py:662
  59.8 6.4 %add_late.1 = (f32[256,512]{1,0:T(8,128)}, bf16[256,512]{1,0:T(8,128)(2,1)}, bf16[256,512]{1,0:T(8,128)(2,1)}, bf16[256,512]{1,0:T(8,128)(2,1)}, bf16[3,2,2,128,512]{4,3,2,1,0:T(8,128)(2,1)}) custom-call(s32[1]{0:T(128)} %bitcast.me_ref, s32[1]{0:T(128)} %bitcast.1.place_ref, s32[8]{0:T(128)} %rows_ref.5, bf16[2,1280,512]{2,1,0:T(8,128)(2,1)} %f_ref.7, ...), custom_call_target="tpu_custom_call" | custom-call | tf_op jit(solution)/shard_map/add_late/pallas_call | solution.py:426
  66.3 1.6 %collective-permute-start.8 = (bf16[256,512]{1,0:T(8,128)(2,1)}, bf16[256,512]{1,0:T(8,128)(2,1)S(1)}, u32[]{:S(2)}, u32[]{:S(2)}) collective-permute-start(bf16[256,512]{1,0:T(8,128)(2,1)} %get-tuple-element.54), channel_id=1, source_target_pairs={{0,16},{8,24},{16,0},{24,8},{1,17},{9,25},{17,1},{25,9},{2,18},{10... | collective-permute-start | bytes 786440 | tf_op jit(solution)/shard_map/ppermute | solution.py:668
  69.3 12.6 %local_back.1.b_ref.b_in = f32[2,1280,512]{2,1,0:T(8,128)} custom-call(s32[1]{0:T(128)} %bitcast.me_ref, s32[1]{0:T(128)S(6)} %copy.20.count_ref, s32[20]{0:T(128)S(1)} %copy-done.4, s32[20]{0:T(128)S(1)} %copy-done.5, s32[8]{0:T(128)S(1)} %copy-done.1, bf16[2,1280,512]{2,1,0:T(8,128)(2,1)} %c_ref.7, bf16[2,1280,512]{2,1,0:T(8,128)(2,1)} %get-tuple-element.34.d_ref, ...), custom_call_target="tpu_custom_call" | custom-call | tf_op jit(solution)/shard_map/local_back/pallas_call | solution.py:268
  82.2 2.2 %collective-permute-start.10 = (bf16[128,512]{1,0:T(8,128)(2,1)S(1)}, bf16[128,512]{1,0:T(8,128)(2,1)S(1)}, u32[]{:S(2)}, u32[]{:S(2)}) collective-permute-start(bf16[128,512]{1,0:T(8,128)(2,1)S(1)} %fusion), channel_id=1, source_target_pairs={{0,1},{1,0},{2,3},{3,2},{4,5},{5,4},{6,7},{7,6},{8,9},{9,8},{10,11... | collective-permute-start | bytes 393224 | tf_op jit(solution)/shard_map/ppermute | solution.py:571
  84.4 2.9 %collective-permute-done.10 = bf16[128,512]{1,0:T(8,128)(2,1)S(1)} collective-permute-done((bf16[128,512]{1,0:T(8,128)(2,1)S(1)}, bf16[128,512]{1,0:T(8,128)(2,1)S(1)}, u32[]{:S(2)}, u32[]{:S(2)}) %collective-permute-start.10) | collective-permute-done | bytes 131104 | tf_op jit(solution)/shard_map/ppermute | solution.py:571
  87.5 1.8 %collective-permute-start.11 = (bf16[128,512]{1,0:T(8,128)(2,1)S(1)}, bf16[128,512]{1,0:T(8,128)(2,1)S(1)}, u32[]{:S(2)}, u32[]{:S(2)}) collective-permute-start(bf16[128,512]{1,0:T(8,128)(2,1)S(1)} %bitcast_add_fusion), channel_id=1, source_target_pairs={{0,2},{1,3},{2,0},{3,1},{4,6},{5,7},{6,4},{7,5},{8,10},{9,11},{10,... | collective-permute-start | bytes 393224 | tf_op jit(solution)/shard_map/ppermute | solution.py:585
  89.3 3.2 %collective-permute-done.11 = bf16[128,512]{1,0:T(8,128)(2,1)S(1)} collective-permute-done((bf16[128,512]{1,0:T(8,128)(2,1)S(1)}, bf16[128,512]{1,0:T(8,128)(2,1)S(1)}, u32[]{:S(2)}, u32[]{:S(2)}) %collective-permute-start.11) | collective-permute-done | bytes 131104 | tf_op jit(solution)/shard_map/ppermute | solution.py:585
  92.5 2.9 %collective-permute-start.12 = (bf16[128,512]{1,0:T(8,128)(2,1)S(1)}, bf16[128,512]{1,0:T(8,128)(2,1)S(1)}, u32[]{:S(2)}, u32[]{:S(2)}) collective-permute-start(bf16[128,512]{1,0:T(8,128)(2,1)S(1)} %add_convert_fusion.1), channel_id=1, source_target_pairs={{0,4},{1,5},{2,6},{3,7},{4,0},{5,1},{6,2},{7,3},{8,12},{9,13},{10,... | collective-permute-start | bytes 393224 | tf_op jit(solution)/shard_map/ppermute | solution.py:585
  95.4 4.5 %collective-permute-done.12 = bf16[128,512]{1,0:T(8,128)(2,1)S(1)} collective-permute-done((bf16[128,512]{1,0:T(8,128)(2,1)S(1)}, bf16[128,512]{1,0:T(8,128)(2,1)S(1)}, u32[]{:S(2)}, u32[]{:S(2)}) %collective-permute-start.12) | collective-permute-done | bytes 131104 | tf_op jit(solution)/shard_map/ppermute | solution.py:585
  99.9 2.3 %collective-permute-start.13 = (bf16[128,512]{1,0:T(8,128)(2,1)S(1)}, bf16[128,512]{1,0:T(8,128)(2,1)S(1)}, u32[]{:S(2)}, u32[]{:S(2)}) collective-permute-start(bf16[128,512]{1,0:T(8,128)(2,1)S(1)} %add_convert_fusion), channel_id=1, source_target_pairs={{0,1},{1,0},{2,3},{3,2},{4,5},{5,4},{6,7},{7,6},{8,9},{9,8},{10,11... | collective-permute-start | bytes 393224 | tf_op jit(solution)/shard_map/ppermute | solution.py:597
  102.2 4.0 %all-to-all-start.1 = ((bf16[8,128,512]{2,1,0:T(8,128)(2,1)}), bf16[8,128,512]{2,1,0:T(8,128)(2,1)S(1)}, u32[]{:S(2)}, u32[]{:S(2)}) async-start(bf16[8,128,512]{2,1,0:T(8,128)(2,1)} %get-tuple-element.59), calls=%async_computation.1 | async-start | bytes 2097152 | tf_op jit(solution)/shard_map/all_to_all | solution.py:662
  107.6 8.9 %settle.1 = (bf16[2,1280,512]{2,1,0:T(8,128)(2,1)}, bf16[2,1280,512]{2,1,0:T(8,128)(2,1)}) custom-call(s32[1]{0:T(128)} %bitcast.me_ref, s32[8]{0:T(128)S(1)} %copy-done.1, bf16[2,1280,512]{2,1,0:T(8,128)(2,1)} %get-tuple-element.33.k_ref, bf16[2,1280,512]{2,1,0:T(8,128)(2,1)} %f_ref.7, f32[2,1280,512]{2,1,0:T(8,128)} %local_back.1.b_ref.b_in, ...), custom_call_target="tpu_custom_call" | custom-call | tf_op jit(solution)/shard_map/settle/pallas_call | solution.py:475
  116.5 4.5 %finish.2._ = bf16[2,1280,512]{2,1,0:T(8,128)(2,1)} custom-call(s32[8]{0:T(128)S(1)} %copy-done.2, s32[8]{0:T(128)S(1)} %copy-done.3, bf16[8,128,512]{2,1,0:T(8,128)(2,1)S(1)} %all-to-all-done.r_in, bf16[8,128,128]{2,1,0:T(8,128)(2,1)} %tiles_in.5, f32[2,1280,512]{2,1,0:T(8,128)} %local_back.1.b_ref.b_in, ...), custom_call_target="tpu_custom_call", output_to_operand_aliasing={{}: (5, {})} | custom-call | tf_op jit(solution)/shard_map/finish/pallas_call | solution.py:527
  121.2 1.8 %collective-permute-done.15 = bf16[2,2,128,512]{3,2,1,0:T(8,128)(2,1)S(1)} collective-permute-done((bf16[2,2,128,512]{3,2,1,0:T(8,128)(2,1)S(1)}, bf16[2,2,128,512]{3,2,1,0:T(8,128)(2,1)S(1)}, u32[]{:S(2)}, u32[]{:S(2)}) %collective-permute-start.15) | collective-permute-done | bytes 524320 | tf_op jit(solution)/shard_map/ppermute | solution.py:597
  125.6 2.2 %all-to-all-done.1.r_in = bf16[8,128,512]{2,1,0:T(8,128)(2,1)S(1)} async-done(((bf16[8,128,512]{2,1,0:T(8,128)(2,1)}), bf16[8,128,512]{2,1,0:T(8,128)(2,1)S(1)}, u32[]{:S(2)}, u32[]{:S(2)}) %all-to-all-start.1) | async-done | bytes 1048608 | tf_op jit(solution)/shard_map/all_to_all | solution.py:662
  127.8 4.5 %finish.3 = bf16[2,1280,512]{2,1,0:T(8,128)(2,1)} custom-call(s32[8]{0:T(128)S(1)} %copy-done.2, s32[8]{0:T(128)S(1)} %copy-done.3, bf16[8,128,512]{2,1,0:T(8,128)(2,1)S(1)} %all-to-all-done.1.r_in, bf16[8,128,128]{2,1,0:T(8,128)(2,1)} %tiles_in.5, f32[2,1280,512]{2,1,0:T(8,128)} %local_back.1.b_ref.b_in, ...), custom_call_target="tpu_custom_call", output_to_operand_aliasing={{}: (5, {})} | custom-call | tf_op jit(solution)/shard_map/finish/pallas_call | solution.py:527
  (53 shorter events, 7.3 us)
Async XLA Ops:
  0.6 16.8 %copy-start = (s32[8]{0:T(128)S(1)}, s32[8]{0:T(128)}, u32[]{:S(2)}) copy-start(s32[8]{0:T(128)} %rows_ref.5) | copy-start | bytes 100
  0.6 16.8 %copy-start.5 = (s32[20]{0:T(128)S(1)}, s32[20]{0:T(128)}, u32[]{:S(2)}) copy-start(s32[20]{0:T(128)} %cols_ref.5) | copy-start | bytes 244
  0.7 16.8 %copy-start.4 = (s32[20]{0:T(128)S(1)}, s32[20]{0:T(128)}, u32[]{:S(2)}) copy-start(s32[20]{0:T(128)} %rows_ref.4) | copy-start | bytes 244
  4.9 32.2 %collective-permute-start = (bf16[2,128,512]{2,1,0:T(8,128)(2,1)}, bf16[2,128,512]{2,1,0:T(8,128)(2,1)S(1)}, u32[]{:S(2)}, u32[]{:S(2)}) collective-permute-start(bf16[2,128,512]{2,1,0:T(8,128)(2,1)} %get-tuple-element.36), channel_id=1, source_target_pairs={{0,7},{1,6},{2,5},{3,4},{4,3},{5,2},{6,1},{7,0},{8,15},{9,14},{10,... | collective-permute-start | bytes 786440 | tf_op jit(solution)/shard_map/ppermute | solution.py:74
  11.0 26.2 %collective-permute-start.2 = (bf16[2,128,512]{2,1,0:T(8,128)(2,1)}, bf16[2,128,512]{2,1,0:T(8,128)(2,1)S(1)}, u32[]{:S(2)}, u32[]{:S(2)}) collective-permute-start(bf16[2,128,512]{2,1,0:T(8,128)(2,1)} %get-tuple-element.38), channel_id=1, source_target_pairs={{0,1},{1,0},{2,3},{3,2},{4,5},{5,4},{6,7},{7,6},{8,9},{9,8},{10,11... | collective-permute-start | bytes 786440 | tf_op jit(solution)/shard_map/ppermute | solution.py:74
  11.5 26.4 %collective-permute-start.1 = (bf16[2,128,512]{2,1,0:T(8,128)(2,1)}, bf16[2,128,512]{2,1,0:T(8,128)(2,1)S(1)}, u32[]{:S(2)}, u32[]{:S(2)}) collective-permute-start(bf16[2,128,512]{2,1,0:T(8,128)(2,1)} %get-tuple-element.37), channel_id=1, source_target_pairs={{0,6},{1,7},{2,4},{3,5},{4,2},{5,3},{6,0},{7,1},{8,14},{9,15},{10,... | collective-permute-start | bytes 786440 | tf_op jit(solution)/shard_map/ppermute | solution.py:74
  11.6 26.3 %collective-permute-start.3 = (bf16[2,128,512]{2,1,0:T(8,128)(2,1)}, bf16[2,128,512]{2,1,0:T(8,128)(2,1)S(1)}, u32[]{:S(2)}, u32[]{:S(2)}) collective-permute-start(bf16[2,128,512]{2,1,0:T(8,128)(2,1)} %get-tuple-element.39), channel_id=1, source_target_pairs={{0,2},{1,3},{2,0},{3,1},{4,6},{5,7},{6,4},{7,5},{8,10},{9,11},{10,... | collective-permute-start | bytes 786440 | tf_op jit(solution)/shard_map/ppermute | solution.py:74
  11.6 39.7 %collective-permute-start.4 = (bf16[2,128,512]{2,1,0:T(8,128)(2,1)}, bf16[2,128,512]{2,1,0:T(8,128)(2,1)S(1)}, u32[]{:S(2)}, u32[]{:S(2)}) collective-permute-start(bf16[2,128,512]{2,1,0:T(8,128)(2,1)} %get-tuple-element.43), channel_id=1, source_target_pairs={{0,5},{1,4},{2,7},{3,6},{4,1},{5,0},{6,3},{7,2},{8,13},{9,12},{10,... | collective-permute-start | bytes 786440 | tf_op jit(solution)/shard_map/ppermute | solution.py:74
  17.5 19.6 %copy-start.8 = (bf16[2,128,512]{2,1,0:T(8,128)(2,1)S(1)}, bf16[2,128,512]{2,1,0:T(8,128)(2,1)}, u32[]{:S(2)}) copy-start(bf16[2,128,512]{2,1,0:T(8,128)(2,1)} %get-tuple-element.45) | copy-start | bytes 786436
  17.5 19.7 %copy-start.7 = (bf16[2,128,512]{2,1,0:T(8,128)(2,1)S(1)}, bf16[2,128,512]{2,1,0:T(8,128)(2,1)}, u32[]{:S(2)}) copy-start(bf16[2,128,512]{2,1,0:T(8,128)(2,1)} %get-tuple-element.47) | copy-start | bytes 786436
  37.1 18.8 %collective-permute-start.5 = (bf16[2,128,512]{2,1,0:T(8,128)(2,1)S(1)}, bf16[2,128,512]{2,1,0:T(8,128)(2,1)S(1)}, u32[]{:S(2)}, u32[]{:S(2)}) collective-permute-start(bf16[2,128,512]{2,1,0:T(8,128)(2,1)S(1)} %copy-done.8), channel_id=1, source_target_pairs={{0,4},{1,5},{2,6},{3,7},{4,0},{5,1},{6,2},{7,3},{8,12},{9,13},{10,... | collective-permute-start | bytes 786440 | tf_op jit(solution)/shard_map/ppermute | solution.py:74
  37.2 18.7 %collective-permute-start.6 = (bf16[2,128,512]{2,1,0:T(8,128)(2,1)S(1)}, bf16[2,128,512]{2,1,0:T(8,128)(2,1)S(1)}, u32[]{:S(2)}, u32[]{:S(2)}) collective-permute-start(bf16[2,128,512]{2,1,0:T(8,128)(2,1)S(1)} %copy-done.7), channel_id=1, source_target_pairs={{0,3},{1,2},{2,1},{3,0},{4,7},{5,6},{6,5},{7,4},{8,11},{9,10},{10,... | collective-permute-start | bytes 786440 | tf_op jit(solution)/shard_map/ppermute | solution.py:74
  56.0 31.5 %all-to-all-start = ((bf16[8,128,512]{2,1,0:T(8,128)(2,1)}), bf16[8,128,512]{2,1,0:T(8,128)(2,1)S(1)}, u32[]{:S(2)}, u32[]{:S(2)}) async-start(bf16[8,128,512]{2,1,0:T(8,128)(2,1)} %get-tuple-element.57), calls=%async_computation | async-start | bytes 2097152 | tf_op jit(solution)/shard_map/all_to_all | solution.py:662
  66.2 15.7 %collective-permute-start.7 = (bf16[256,512]{1,0:T(8,128)(2,1)}, bf16[256,512]{1,0:T(8,128)(2,1)S(1)}, u32[]{:S(2)}, u32[]{:S(2)}) collective-permute-start(bf16[256,512]{1,0:T(8,128)(2,1)} %get-tuple-element.52), channel_id=1, source_target_pairs={{0,8},{8,16},{16,24},{24,0},{1,9},{9,17},{17,25},{25,1},{2,10},{10... | collective-permute-start | bytes 786440 | tf_op jit(solution)/shard_map/ppermute | solution.py:668
  66.3 15.7 %collective-permute-start.8 = (bf16[256,512]{1,0:T(8,128)(2,1)}, bf16[256,512]{1,0:T(8,128)(2,1)S(1)}, u32[]{:S(2)}, u32[]{:S(2)}) collective-permute-start(bf16[256,512]{1,0:T(8,128)(2,1)} %get-tuple-element.54), channel_id=1, source_target_pairs={{0,16},{8,24},{16,0},{24,8},{1,17},{9,25},{17,1},{25,9},{2,18},{10... | collective-permute-start | bytes 786440 | tf_op jit(solution)/shard_map/ppermute | solution.py:668
  67.9 14.1 %collective-permute-start.9 = (bf16[256,512]{1,0:T(8,128)(2,1)}, bf16[256,512]{1,0:T(8,128)(2,1)S(1)}, u32[]{:S(2)}, u32[]{:S(2)}) collective-permute-start(bf16[256,512]{1,0:T(8,128)(2,1)} %get-tuple-element.55), channel_id=1, source_target_pairs={{0,24},{8,0},{16,8},{24,16},{1,25},{9,1},{17,9},{25,17},{2,26},{10... | collective-permute-start | bytes 786440 | tf_op jit(solution)/shard_map/ppermute | solution.py:668
  69.3 12.8 %copy-start.6 = (f32[256,512]{1,0:T(8,128)S(1)}, f32[256,512]{1,0:T(8,128)}, u32[]{:S(2)}) copy-start(f32[256,512]{1,0:T(8,128)} %get-tuple-element.51) | copy-start | bytes 1572868
  82.2 5.1 %collective-permute-start.10 = (bf16[128,512]{1,0:T(8,128)(2,1)S(1)}, bf16[128,512]{1,0:T(8,128)(2,1)S(1)}, u32[]{:S(2)}, u32[]{:S(2)}) collective-permute-start(bf16[128,512]{1,0:T(8,128)(2,1)S(1)} %fusion), channel_id=1, source_target_pairs={{0,1},{1,0},{2,3},{3,2},{4,5},{5,4},{6,7},{7,6},{8,9},{9,8},{10,11... | collective-permute-start | bytes 393224 | tf_op jit(solution)/shard_map/ppermute | solution.py:571
  87.5 5.0 %collective-permute-start.11 = (bf16[128,512]{1,0:T(8,128)(2,1)S(1)}, bf16[128,512]{1,0:T(8,128)(2,1)S(1)}, u32[]{:S(2)}, u32[]{:S(2)}) collective-permute-start(bf16[128,512]{1,0:T(8,128)(2,1)S(1)} %bitcast_add_fusion), channel_id=1, source_target_pairs={{0,2},{1,3},{2,0},{3,1},{4,6},{5,7},{6,4},{7,5},{8,10},{9,11},{10,... | collective-permute-start | bytes 393224 | tf_op jit(solution)/shard_map/ppermute | solution.py:585
  92.5 7.3 %collective-permute-start.12 = (bf16[128,512]{1,0:T(8,128)(2,1)S(1)}, bf16[128,512]{1,0:T(8,128)(2,1)S(1)}, u32[]{:S(2)}, u32[]{:S(2)}) collective-permute-start(bf16[128,512]{1,0:T(8,128)(2,1)S(1)} %add_convert_fusion.1), channel_id=1, source_target_pairs={{0,4},{1,5},{2,6},{3,7},{4,0},{5,1},{6,2},{7,3},{8,12},{9,13},{10,... | collective-permute-start | bytes 393224 | tf_op jit(solution)/shard_map/ppermute | solution.py:585
  99.9 7.3 %collective-permute-start.13 = (bf16[128,512]{1,0:T(8,128)(2,1)S(1)}, bf16[128,512]{1,0:T(8,128)(2,1)S(1)}, u32[]{:S(2)}, u32[]{:S(2)}) collective-permute-start(bf16[128,512]{1,0:T(8,128)(2,1)S(1)} %add_convert_fusion), channel_id=1, source_target_pairs={{0,1},{1,0},{2,3},{3,2},{4,5},{5,4},{6,7},{7,6},{8,9},{9,8},{10,11... | collective-permute-start | bytes 393224 | tf_op jit(solution)/shard_map/ppermute | solution.py:597
  102.2 25.6 %all-to-all-start.1 = ((bf16[8,128,512]{2,1,0:T(8,128)(2,1)}), bf16[8,128,512]{2,1,0:T(8,128)(2,1)S(1)}, u32[]{:S(2)}, u32[]{:S(2)}) async-start(bf16[8,128,512]{2,1,0:T(8,128)(2,1)} %get-tuple-element.59), calls=%async_computation.1 | async-start | bytes 2097152 | tf_op jit(solution)/shard_map/all_to_all | solution.py:662
  107.3 13.7 %collective-permute-start.14 = (bf16[2,128,512]{2,1,0:T(8,128)(2,1)S(1)}, bf16[2,128,512]{2,1,0:T(8,128)(2,1)S(1)}, u32[]{:S(2)}, u32[]{:S(2)}) collective-permute-start(bf16[2,128,512]{2,1,0:T(8,128)(2,1)S(1)} %get-tuple-element.65), channel_id=1, source_target_pairs={{0,16},{8,24},{16,0},{24,8},{1,17},{9,25},{17,1},{25,9},{2,18},{10... | collective-permute-start | bytes 786440 | tf_op jit(solution)/shard_map/ppermute | solution.py:597
  121.1 2.0 %collective-permute-start.15 = (bf16[2,2,128,512]{3,2,1,0:T(8,128)(2,1)S(1)}, bf16[2,2,128,512]{3,2,1,0:T(8,128)(2,1)S(1)}, u32[]{:S(2)}, u32[]{:S(2)}) collective-permute-start(bf16[2,2,128,512]{3,2,1,0:T(8,128)(2,1)S(1)} %pad_maximum_fusion.1), channel_id=1, source_target_pairs={{0,8},{8,0},{16,24},{24,16},{1,9},{9,1},{17,25},{25,17},{2,10},{10... | collective-permute-start | bytes 1572872 | tf_op jit(solution)/shard_map/ppermute | solution.py:597
  (3 other events, 27.4 us)
